TPU v7x, 32 devices: a whole 2x2x4 slice. The times are simulated.
32 devices in a mesh: fsdp: 16 (over z, x, core), tp: 2 (over y).
Axes of the slice: x: 2, y: 2, z: 4, core: 2. Of those that a mesh axis runs over, the one named last changes fastest.
Arguments:
- tokens: bfloat16 [2, 2048, 1792], P(None, ('fsdp', 'tp')), may hold values from -6 to 6
- doc_starts: int32 [2, 2048], P(None, 'fsdp'), may hold values from 0 to 1, as said below
- w_qkv: bfloat16 [3, 1792, 1792], P(None, 'fsdp', 'tp'), may hold values from -0.125 to 0.125
- w_out: bfloat16 [1792, 1792], P('tp', 'fsdp'), may hold values from -0.375 to 0.375
- w_gate_up: bfloat16 [2, 1792, 4864], P(None, 'fsdp', 'tp'), may hold values from -0.125 to 0.125
- w_down: bfloat16 [4864, 1792], P('tp', 'fsdp'), may hold values from -0.078125 to 0.078125
- gains: bfloat16 [2, 1792], P(None, 'fsdp'), may hold values from 0.5 to 1.5
- cotangent: bfloat16 [2, 2048, 1792], P(None, ('fsdp', 'tp')), may hold values from -6 to 6
Outputs:
- output: bfloat16 [2, 2048, 1792], P(None, ('fsdp', 'tp'))
- input_grad: float32 [2, 2048, 1792], P(None, ('fsdp', 'tp'))
- grad_qkv: float32 [3, 1792, 1792], P(None, 'fsdp', 'tp')
- grad_out: float32 [1792, 1792], P('tp', 'fsdp')
- grad_gate_up: float32 [2, 1792, 4864], P(None, 'fsdp', 'tp')
- grad_down: float32 [4864, 1792], P('tp', 'fsdp')
- grad_gains: float32 [2, 1792], P(None, 'fsdp')
Inputs may be any that keep to these rules, and one draw needn't show every extreme that they name: `doc_starts`: each micro-batch's first position starts a document. In one micro-batch drawn from the seed a single document starts at position 64 and runs to position 1984 or beyond.
All inputs are finite; a program needn't handle non-finite values.
Results may differ from a plain program's by a relative error of at most 0.015.
Values may be sent and summed in bfloat16 or wider, within the bound.
A program may use at most 320 MiB of HBM per device.

v0:
```python
import jax
import jax.numpy as jnp
from jax import lax
from jax.sharding import PartitionSpec as P

DH = 112
WINDOW = 64


EPSILON = 1e-06


def passed_along(block, axis, distance):
    devices = range(lax.axis_size(axis))
    route = [(i - distance, i) for i in devices if i - distance in devices]
    return lax.ppermute(block, axis, route)


def normalize(rows, gain):
    scale = lax.rsqrt(jnp.mean(rows * rows, axis=-1, keepdims=True) + EPSILON)
    unit = rows * scale
    return (unit * gain, unit, scale)


def normalize_back(grad, unit, scale, gain):
    d_unit = grad * gain
    inner = jnp.mean(d_unit * unit, axis=-1, keepdims=True)
    return (scale * (d_unit - unit * inner), jnp.sum(grad * unit, axis=0))


def fetch_weights(weights):
    return (
        lax.all_gather(weights[0], "fsdp", axis=1, tiled=True),
        lax.all_gather(weights[1], "fsdp", axis=1, tiled=True),
        lax.all_gather(weights[2], "fsdp", axis=1, tiled=True),
        lax.all_gather(weights[3], "fsdp", axis=1, tiled=True),
        lax.all_gather(weights[4], "fsdp", axis=1, tiled=True),
    )


def owner_sums(grads):
    grad_qkv, grad_outproj, grad_gate_up, grad_down, grad_gain = grads
    gate_share, out_share = (
        lax.psum_scatter(grad_gate_up, "fsdp", scatter_dimension=1, tiled=True),
        lax.psum_scatter(grad_outproj, "fsdp", scatter_dimension=1, tiled=True),
    )
    qkv_share, down_share, gain_share = (
        lax.psum_scatter(grad_qkv, "fsdp", scatter_dimension=1, tiled=True),
        lax.psum_scatter(grad_down, "fsdp", scatter_dimension=1, tiled=True),
        lax.psum_scatter(grad_gain, "fsdp", scatter_dimension=1, tiled=True),
    )
    return (qkv_share, out_share, gate_share, down_share, gain_share)


def masked_scores(queries, keys_all, allowed):
    scores = jnp.einsum(
        "ihd,jhd->hij", queries, keys_all, preferred_element_type=jnp.float32
    ) * DH ** (-0.5)
    return jnp.where(allowed[None], scores, -1e30)


def body(tokens, doc_starts, w_qkv, w_out, w_gate_up, w_down, gains, cotangent):
    batches = tokens.shape[0]
    head_cols = w_qkv.shape[2]
    heads_local = head_cols // DH
    local = (w_qkv, w_out, w_gate_up, w_down, gains)
    outputs = []
    input_grads = []
    totals = None
    for batch in range(batches):
        qkv_full, out_full, gate_full, down_full, gain_full = fetch_weights(local)
        gain_rows = gain_full.astype(jnp.float32)
        rows_in = tokens[batch].astype(jnp.float32)
        normed_one, unit_one, scale_one = normalize(rows_in, gain_rows[0])
        normed_all = lax.all_gather(normed_one.astype(jnp.bfloat16), "tp", axis=0, tiled=True)
        projected = jnp.einsum(
            "td,sdh->sth", normed_all, qkv_full, preferred_element_type=jnp.float32
        ).astype(jnp.bfloat16)
        queries, keys_now, values_now = (projected[0], projected[1], projected[2])
        seq_rows = keys_now.shape[0]
        starts_now = doc_starts[batch].astype(jnp.float32)
        rim_keys, rim_values, rim_starts = passed_along(
            (
                keys_now[seq_rows - WINDOW :],
                values_now[seq_rows - WINDOW :],
                starts_now[seq_rows - WINDOW :].astype(jnp.bfloat16),
            ),
            "fsdp",
            1,
        )
        keys_all = jnp.concatenate([rim_keys, keys_now], axis=0).reshape(
            seq_rows + WINDOW, heads_local, DH
        )
        values_all = jnp.concatenate([rim_values, values_now], axis=0).reshape(
            seq_rows + WINDOW, heads_local, DH
        )
        counts = jnp.cumsum(jnp.concatenate([rim_starts.astype(jnp.float32), starts_now]))
        offset = jnp.arange(seq_rows)[:, None] + WINDOW - jnp.arange(seq_rows + WINDOW)[None, :]
        allowed = (offset >= 0) & (offset < WINDOW) & (counts[WINDOW:, None] == counts[None, :])
        query_heads = queries.reshape(seq_rows, heads_local, DH)
        scores = masked_scores(query_heads, keys_all, allowed)
        top = jnp.max(scores, axis=-1, keepdims=True)
        weights_exp = jnp.exp(scores - top)
        total = jnp.sum(weights_exp, axis=-1, keepdims=True)
        probs = weights_exp / total
        log_total = top + jnp.log(total)
        heads_out = (
            jnp.einsum(
                "hij,jhd->ihd",
                probs.astype(jnp.bfloat16),
                values_all,
                preferred_element_type=jnp.float32,
            )
            .astype(jnp.bfloat16)
            .reshape(seq_rows, head_cols)
        )
        attn_rows = lax.psum_scatter(
            jnp.dot(heads_out, out_full, preferred_element_type=jnp.float32).astype(jnp.bfloat16),
            "tp",
            scatter_dimension=0,
            tiled=True,
        ).astype(jnp.float32)
        resid = rows_in + attn_rows
        normed_two, unit_two, scale_two = normalize(resid, gain_rows[1])
        mixed_all = lax.all_gather(normed_two.astype(jnp.bfloat16), "tp", axis=0, tiled=True)
        gate_up = jnp.einsum(
            "td,sdf->stf", mixed_all, gate_full, preferred_element_type=jnp.float32
        )
        gate, upward = (gate_up[0], gate_up[1])
        sigmoid_gate = jax.nn.sigmoid(gate)
        silu_gate = gate * sigmoid_gate
        hidden = (silu_gate * upward).astype(jnp.bfloat16)
        mlp_out = lax.psum_scatter(
            jnp.dot(hidden, down_full, preferred_element_type=jnp.float32).astype(jnp.bfloat16),
            "tp",
            scatter_dimension=0,
            tiled=True,
        ).astype(jnp.float32)
        outputs.append((resid + mlp_out).astype(jnp.bfloat16))
        qkv_full, out_full, gate_full, down_full, spare_gains = fetch_weights(local)
        grad_rows = cotangent[batch].astype(jnp.float32)
        grad_mlp = lax.all_gather(cotangent[batch], "tp", axis=0, tiled=True)
        grad_down = jnp.einsum("tf,td->fd", hidden, grad_mlp, preferred_element_type=jnp.float32)
        d_hidden = jnp.einsum("td,fd->tf", grad_mlp, down_full, preferred_element_type=jnp.float32)
        d_gate = (d_hidden * upward * sigmoid_gate * (1.0 + gate * (1.0 - sigmoid_gate))).astype(
            jnp.bfloat16
        )
        d_up = (d_hidden * silu_gate).astype(jnp.bfloat16)
        d_gate_up = jnp.stack([d_gate, d_up])
        grad_gate_up = jnp.einsum(
            "td,stf->sdf", mixed_all, d_gate_up, preferred_element_type=jnp.float32
        )
        d_normed_two = lax.psum_scatter(
            jnp.einsum(
                "stf,sdf->td", d_gate_up, gate_full, preferred_element_type=jnp.float32
            ).astype(jnp.bfloat16),
            "tp",
            scatter_dimension=0,
            tiled=True,
        ).astype(jnp.float32)
        resid_part, gain_two_grad = normalize_back(d_normed_two, unit_two, scale_two, gain_rows[1])
        d_resid = grad_rows + resid_part
        grad_attn = lax.all_gather(d_resid.astype(jnp.bfloat16), "tp", axis=0, tiled=True)
        grad_outproj = jnp.einsum(
            "th,td->hd", heads_out, grad_attn, preferred_element_type=jnp.float32
        )
        d_heads = jnp.einsum(
            "td,hd->th", grad_attn, out_full, preferred_element_type=jnp.float32
        ).astype(jnp.bfloat16)
        d_heads = d_heads.reshape(seq_rows, heads_local, DH)
        scores = masked_scores(query_heads, keys_all, allowed)
        probs = jnp.exp(scores - log_total)
        d_values_all = jnp.einsum(
            "hij,ihd->jhd", probs.astype(jnp.bfloat16), d_heads, preferred_element_type=jnp.float32
        )
        d_probs = jnp.einsum(
            "ihd,jhd->hij", d_heads, values_all, preferred_element_type=jnp.float32
        )
        d_scores = (probs * (d_probs - jnp.sum(probs * d_probs, axis=-1, keepdims=True))).astype(
            jnp.bfloat16
        )
        d_queries = (
            (
                jnp.einsum("hij,jhd->ihd", d_scores, keys_all, preferred_element_type=jnp.float32)
                * DH ** (-0.5)
            )
            .astype(jnp.bfloat16)
            .reshape(seq_rows, head_cols)
        )
        d_keys_all = (
            jnp.einsum("hij,ihd->jhd", d_scores, query_heads, preferred_element_type=jnp.float32)
            * DH ** (-0.5)
        ).reshape(seq_rows + WINDOW, head_cols)
        d_values_all = d_values_all.reshape(seq_rows + WINDOW, head_cols)
        back_keys, back_values = (
            passed_along(d_keys_all[:WINDOW].astype(jnp.bfloat16), "fsdp", -1).astype(jnp.float32),
            passed_along(d_values_all[:WINDOW].astype(jnp.bfloat16), "fsdp", -1).astype(
                jnp.float32
            ),
        )
        d_keys = d_keys_all[WINDOW:]
        d_values = d_values_all[WINDOW:]
        d_keys = jnp.concatenate(
            [d_keys[: seq_rows - WINDOW], d_keys[seq_rows - WINDOW :] + back_keys], axis=0
        )
        d_values = jnp.concatenate(
            [d_values[: seq_rows - WINDOW], d_values[seq_rows - WINDOW :] + back_values], axis=0
        )
        d_projected = jnp.stack(
            [d_queries, d_keys.astype(jnp.bfloat16), d_values.astype(jnp.bfloat16)]
        )
        grad_qkv = jnp.einsum(
            "td,sth->sdh", normed_all, d_projected, preferred_element_type=jnp.float32
        )
        d_normed_one = lax.psum_scatter(
            jnp.einsum(
                "sth,sdh->td", d_projected, qkv_full, preferred_element_type=jnp.float32
            ).astype(jnp.bfloat16),
            "tp",
            scatter_dimension=0,
            tiled=True,
        ).astype(jnp.float32)
        input_part, gain_one_grad = normalize_back(d_normed_one, unit_one, scale_one, gain_rows[0])
        input_grads.append(d_resid + input_part)
        grads = (
            grad_qkv,
            grad_outproj,
            grad_gate_up,
            grad_down,
            jnp.stack([gain_one_grad, gain_two_grad]),
        )
        shares = owner_sums(grads)
        totals = shares if totals is None else jax.tree.map(jnp.add, totals, shares)
    gains_total = lax.psum(totals[4], "tp")
    return (
        jnp.stack(outputs),
        jnp.stack(input_grads),
        totals[0],
        totals[1],
        totals[2],
        totals[3],
        gains_total,
    )


def solution(mesh):
    in_specs = (
        P(None, ("fsdp", "tp"), None),
        P(None, "fsdp"),
        P(None, "fsdp", "tp"),
        P("tp", "fsdp"),
        P(None, "fsdp", "tp"),
        P("tp", "fsdp"),
        P(None, "fsdp"),
        P(None, ("fsdp", "tp"), None),
    )
    out_specs = (
        P(None, ("fsdp", "tp"), None),
        P(None, ("fsdp", "tp"), None),
        P(None, "fsdp", "tp"),
        P("tp", "fsdp"),
        P(None, "fsdp", "tp"),
        P("tp", "fsdp"),
        P(None, "fsdp"),
    )
    return jax.shard_map(body, mesh=mesh, in_specs=in_specs, out_specs=out_specs, check_vma=False)
```

profile of v0, /device:TPU:0, one launch (start us, length us, event | category | flops | bytes accessed | tf_op | source)
XLA Modules:
  0.0 1689.6 jit_solution(18329337177922518703)
XLA Ops:
  9.5 2.3 collective-permute-start.4
  12.0 4.5 collective-permute-start.1
  16.5 20.3 %all-gather.2 = bf16[16,112,2]{1,2,0:T(2,128)(2,1)S(1)} all-gather(bf16[1,112,2]{1,2,0:T(2,128)(2,1)} %bitcast.308), channel_id=1, replica_groups=mesh['fsdp'=16,'tp'=2] {'fsdp'}, dimensions={0}, use_global_device_ids=true | all-gather | bytes 7616 | tf_op jit(solution)/shard_map/all_gather | solution.py:37
  38.4 8.5 all_gather.53
  46.9 7.7 all_gather.59
  56.3 39.4 %all-gather.8.cloned.1.call-done = bf16[3,1792,896]{2,1,0:T(8,128)(2,1)} async-done(((bf16[3,112,896]{2,1,0:T(8,128)(2,1)}), bf16[3,1792,896]{2,1,0:T(8,128)(2,1)}) %all-gather.8.cloned.1.call-update) | async-done | bytes 9633808 | tf_op jit(solution)/shard_map/all_gather | solution.py:33
  95.7 5.4 fusion.9
  101.1 2.3 collective-permute-start.3
  103.4 2.4 collective-permute-start.5
  105.8 1.5 fusion.8
  107.4 2.2 collective-permute-start
  109.5 3.3 collective-permute-start.2
  118.0 24.5 %all-gather.10.cloned.1.call-done = bf16[896,1792]{0,1:T(8,128)(2,1)} async-done(((bf16[896,112]{0,1:T(8,128)(2,1)}), bf16[896,1792]{0,1:T(8,128)(2,1)}) %all-gather.10.cloned.1.call-update) | async-done | bytes 3211280 | tf_op jit(solution)/shard_map/all_gather | solution.py:34
  142.5 3.7 convolution_convert_fusion.3
  148.9 1.8 convolution_convert_fusion.1
  153.1 10.0 all-gather.1
  163.1 8.2 all-gather
  171.2 8.2 reduce-scatter.21.cloned.1.call-done
  179.4 1.5 multiply_reduce_fusion.3
  182.4 8.1 all_gather.56
  190.6 7.4 all_gather.60
  198.0 75.0 %all-gather.12.cloned.1.call-done = bf16[2,1792,2432]{2,1,0:T(8,128)(2,1)} async-done(((bf16[2,112,2432]{2,1,0:T(8,128)(2,1)}), bf16[2,1792,2432]{2,1,0:T(8,128)(2,1)}) %all-gather.12.cloned.1.call-update) | async-done | bytes 17432592 | tf_op jit(solution)/shard_map/all_gather | solution.py:35
  273.0 10.0 convolution_bitcast_fusion
  283.0 69.0 %all-gather.14.cloned.1.call-done = bf16[2432,1792]{0,1:T(8,128)(2,1)} async-done(((bf16[2432,112]{0,1:T(8,128)(2,1)}), bf16[2432,1792]{0,1:T(8,128)(2,1)}) %all-gather.14.cloned.1.call-update) | async-done | bytes 8716304 | tf_op jit(solution)/shard_map/all_gather | solution.py:36
  352.0 7.2 fusion.28
  359.2 12.8 fusion.2
  372.5 8.8 convolution_bitcast_fusion.1
  381.3 6.6 fusion.27
  387.9 12.8 fusion
  400.7 7.0 convolution_convert_fusion
  407.8 5.0 reduce-scatter.25.cloned.1.call-done
  412.9 2.3 fusion.49
  415.2 14.4 reduce-scatter.23.cloned.1.call-done
  429.6 2.5 fusion.106
  432.1 8.0 all_gather.62
  443.4 3.1 multiply_reduce_fusion.1
  447.8 7.3 all_gather.64
  464.9 1.8 copy.136
  466.7 1.6 fusion.112
  469.1 1.7 concatenate.115
  470.8 1.6 copy.135
  472.5 1.7 convert_element_type.310
  489.0 7.3 fusion.3
  497.5 7.3 fusion.1
  504.9 7.0 convolution_convert_fusion.2
  512.3 13.8 fusion.14
  526.2 5.5 reduce-scatter.27.cloned.1.call-done
  531.7 2.0 fusion.53
  535.2 22.3 %add_bitcast_fusion = f32[2,1792,2432]{1,2,0:T(8,128)} fusion(f32[2,2432,1792]{2,1,0:T(8,128)} %fusion.14, bf16[1,128,2432]{2,1,0:T(8,128)(2,1)S(1)} %copy-done.27, bf16[1,128,2432]{2,1,0:T(8,128)(2,1)S(1)} %copy-done.26, bf16[128,1792]{1,0:T(8,128)(2,1)S(1)} %copy-done.12), kind=kOutput, calls=%fused_computation | convolution fusion | flops 2240708608 | bytes 71434240 | tf_op jit(solution)/shard_map/td,stf->sdf/dot_general | solution.py:150
  557.5 53.2 %copy.149 = f32[2,1792,2432]{2,0,1:T(2,128)} copy(f32[2,1792,2432]{1,2,0:T(8,128)} %add_bitcast_fusion) | data formatting | bytes 69730304 | tf_op jit(solution)/shard_map/add | solution.py:233
  611.9 10.5 fusion.72
  622.4 16.2 add_bitcast_fusion.1
  638.6 31.6 %copy.156 = f32[3,1792,896]{2,0,1:T(4,128)} copy(f32[3,1792,896]{1,2,0:T(8,128)} %add_bitcast_fusion.1) | data formatting | bytes 38535168
  670.2 18.3 %copy.161 = f32[224,8,3,896]{3,1,2,0:T(8,128)} copy(f32[224,8,3,896]{3,2,1,0:T(4,128)} %bitcast.282) | data formatting | bytes 38535168
  690.7 3.8 convolution_add_fusion.1
  694.5 3.6 fusion.62
  698.1 9.6 convolution_add_fusion
  714.4 5.5 psum.7
  719.9 481.1 %all-reduce.5.cloned.1.call-done = f32[2,1792,2432]{2,0,1:T(2,128)} async-done(((f32[2,1792,2432]{2,0,1:T(2,128)}), f32[2,1792,2432]{2,0,1:T(2,128)}) %all-reduce.5.cloned.1.call-update) | async-done | bytes 34865168
  1201.0 1.8 constant_dynamic-slice_fusion
  1204.3 199.4 %reduce-scatter.37.cloned.1.call-done = f32[112,2688]{1,0:T(8,128)} async-done(((f32[1792,2688]{1,0:T(8,128)}), f32[112,2688]{1,0:T(8,128)}) %reduce-scatter.37.cloned.1.call-update) | async-done | bytes 1204240
  1403.8 1.6 reshape.432
  1406.5 87.6 %reduce-scatter.33.cloned.1.call-done = f32[896,112]{0,1:T(8,128)} async-done(((f32[896,1792]{0,1:T(8,128)}), f32[896,112]{0,1:T(8,128)}) %reduce-scatter.33.cloned.1.call-update) | async-done | bytes 401424 | tf_op jit(solution)/shard_map/reduce_scatter | solution.py:45
  1494.1 188.6 %reduce-scatter.35.cloned.1.call-done = f32[2432,112]{0,1:T(8,128)} async-done(((f32[2432,1792]{0,1:T(8,128)}), f32[2432,112]{0,1:T(8,128)}) %reduce-scatter.35.cloned.1.call-update) | async-done | bytes 1089552 | tf_op jit(solution)/shard_map/reduce_scatter | solution.py:49
  (375 shorter events, 61.7 us)
Async XLA Ops:
  7.2 31.1 %copy-start.2 = (bf16[2,64,1792]{2,1,0:T(8,128)(2,1)S(1)}, bf16[2,64,1792]{2,1,0:T(8,128)(2,1)}, u32[]{:S(2)}) copy-start(bf16[2,64,1792]{2,1,0:T(8,128)(2,1)} %param.8) | copy-start | bytes 1376260
  7.2 88.5 %all-gather.8.cloned.1.call-start = ((), (), s32[]{:S(2)}) async-start(), calls=%async_computation.12 | async-start | bytes 10235904 | tf_op jit(solution)/shard_map/all_gather | solution.py:33
  7.9 134.6 %all-gather.10.cloned.1.call-start = ((), (), s32[]{:S(2)}) async-start(), calls=%async_computation.13 | async-start | bytes 3411968 | tf_op jit(solution)/shard_map/all_gather | solution.py:34
  8.7 162.6 %reduce-scatter.17.cloned.1.call-start = ((), (), s32[]{:S(2)}) async-start(), calls=%async_computation.14 | async-start | bytes 688128 | tf_op jit(solution)/shard_map/reduce_scatter | solution.py:117
  9.5 45.0 %collective-permute-start.4 = (bf16[64]{0:T(256)(128)(2,1)S(1)}, bf16[64]{0:T(256)(128)(2,1)S(1)}, u32[]{:S(2)}, u32[]{:S(2)}) collective-permute-start(bf16[64]{0:T(256)(128)(2,1)S(1)} %slice_bitcast_fusion.8), channel_id=1, source_target_pairs={{0,2},{2,4},{4,6},{6,8},{8,10},{10,12},{12,14},{14,16},{16,18},{18... | collective-permute-start | bytes 392 | tf_op jit(solution)/shard_map/ppermute | solution.py:16
  12.0 43.4 %collective-permute-start.1 = (bf16[64]{0:T(256)(128)(2,1)S(1)}, bf16[64]{0:T(256)(128)(2,1)S(1)}, u32[]{:S(2)}, u32[]{:S(2)}) collective-permute-start(bf16[64]{0:T(256)(128)(2,1)S(1)} %slice_bitcast_fusion.9), channel_id=1, source_target_pairs={{0,2},{2,4},{4,6},{6,8},{8,10},{10,12},{12,14},{14,16},{16,18},{18... | collective-permute-start | bytes 392 | tf_op jit(solution)/shard_map/ppermute | solution.py:16
  36.9 392.7 %copy-start.70 = (f32[1792]{0:T(1024)}, f32[1792]{0:T(1024)S(1)}, u32[]{:S(2)}) copy-start(f32[1792]{0:T(1024)S(1)} %get-tuple-element.51) | copy-start | bytes 21508
  38.2 18.0 %copy-start.89 = (f32[64]{0:T(128)}, f32[64]{0:T(128)S(1)}, u32[]{:S(2)}) copy-start(f32[64]{0:T(128)S(1)} %add_rsqrt_fusion.3) | copy-start | bytes 772
  38.2 16.4 copy-start.87
  46.9 58.9 %copy-start.18 = (bf16[128,1792]{1,0:T(8,128)(2,1)}, bf16[128,1792]{1,0:T(8,128)(2,1)S(1)}, u32[]{:S(2)}) copy-start(bf16[128,1792]{1,0:T(8,128)(2,1)S(1)} %all_gather.53) | copy-start | bytes 1376260
  54.6 46.5 %copy-start.15 = (bf16[128,1792]{1,0:T(8,128)(2,1)}, bf16[128,1792]{1,0:T(8,128)(2,1)S(1)}, u32[]{:S(2)}) copy-start(bf16[128,1792]{1,0:T(8,128)(2,1)S(1)} %all_gather.59) | copy-start | bytes 1376260
  95.7 10.1 copy-start.1
  101.1 13.7 collective-permute-start.3
  103.4 12.3 collective-permute-start.5
  107.4 8.5 collective-permute-start
  109.5 6.6 collective-permute-start.2
  113.3 33.4 %copy-start.35 = (bf16[128,8,112]{2,0,1:T(8,128)(2,1)}, bf16[128,8,112]{2,0,1:T(8,128)(2,1)S(1)}, u32[]{:S(2)}) copy-start(bf16[128,8,112]{2,0,1:T(8,128)(2,1)S(1)} %copy.124) | copy-start | bytes 688132
  113.7 32.6 %copy-start.74 = (bf16[128,8,112]{2,0,1:T(8,128)(2,1)}, bf16[128,8,112]{2,0,1:T(8,128)(2,1)S(1)}, u32[]{:S(2)}) copy-start(bf16[128,8,112]{2,0,1:T(8,128)(2,1)S(1)} %copy.128) | copy-start | bytes 688132
  113.9 32.4 %copy-start.45 = (bf16[1,128,896]{1,2,0:T(8,128)(2,1)}, bf16[1,128,896]{1,2,0:T(8,128)(2,1)S(1)}, u32[]{:S(2)}) copy-start(bf16[1,128,896]{1,2,0:T(8,128)(2,1)S(1)} %copy.125) | copy-start | bytes 688132
  115.9 30.4 %copy-start.76 = (bf16[64,8,112]{2,0,1:T(8,128)(2,1)}, bf16[64,8,112]{2,0,1:T(8,128)(2,1)S(1)}, u32[]{:S(2)}) copy-start(bf16[64,8,112]{2,0,1:T(8,128)(2,1)S(1)} %copy.127) | copy-start | bytes 344068
  118.0 28.2 %copy-start.33 = (bf16[8,112,128]{2,1,0:T(8,128)(2,1)}, bf16[8,112,128]{2,1,0:T(8,128)(2,1)S(1)}, u32[]{:S(2)}) copy-start(bf16[8,112,128]{2,1,0:T(8,128)(2,1)S(1)} %convolution_convert_fusion.9) | copy-start | bytes 688132
  146.2 33.2 %reduce-scatter.21.cloned.1.call-start = ((), (), s32[]{:S(2)}) async-start(), calls=%async_computation.18 | async-start | bytes 688128 | tf_op jit(solution)/shard_map/reduce_scatter | solution.py:117
  150.8 122.2 %all-gather.12.cloned.1.call-start = ((), (), s32[]{:S(2)}) async-start(), calls=%async_computation.15 | async-start | bytes 18522112 | tf_op jit(solution)/shard_map/all_gather | solution.py:35
  151.4 200.6 %all-gather.14.cloned.1.call-start = ((), (), s32[]{:S(2)}) async-start(), calls=%async_computation.16 | async-start | bytes 9261056 | tf_op jit(solution)/shard_map/all_gather | solution.py:36
  151.9 255.9 %reduce-scatter.29.cloned.1.call-start = ((), (), s32[]{:S(2)}) async-start(), calls=%async_computation.22 | async-start | bytes 688128 | tf_op jit(solution)/shard_map/reduce_scatter | solution.py:153
  180.9 248.6 %copy-start.83 = (f32[64]{0:T(128)}, f32[64]{0:T(128)S(1)}, u32[]{:S(2)}) copy-start(f32[64]{0:T(128)S(1)} %get-tuple-element.110) | copy-start | bytes 772
  181.0 248.6 %copy-start.85 = (f32[64]{0:T(128)}, f32[64]{0:T(128)S(1)}, u32[]{:S(2)}) copy-start(f32[64]{0:T(128)S(1)} %get-tuple-element.111) | copy-start | bytes 772
  372.0 40.9 %reduce-scatter.25.cloned.1.call-start = ((), (), s32[]{:S(2)}) async-start(), calls=%async_computation.20 | async-start | bytes 688128 | tf_op jit(solution)/shard_map/reduce_scatter | solution.py:153
  372.5 8.8 copy-start.32
  400.7 28.9 %reduce-scatter.23.cloned.1.call-start = ((), (), s32[]{:S(2)}) async-start(), calls=%async_computation.19 | async-start | bytes 688128 | tf_op jit(solution)/shard_map/reduce_scatter | solution.py:133
  400.7 12.1 copy-start.9
  407.7 118.5 %reduce-scatter.31.cloned.1.call-start = ((), (), s32[]{:S(2)}) async-start(), calls=%async_computation.23 | async-start | bytes 688128 | tf_op jit(solution)/shard_map/reduce_scatter | solution.py:215
  415.2 16.9 %copy-start.93 = (f32[64]{0:T(128)}, f32[64]{0:T(128)S(1)}, u32[]{:S(2)}) copy-start(f32[64]{0:T(128)S(1)} %broadcast_multiply_fusion.3) | copy-start | bytes 772
  415.2 16.9 %copy-start.91 = (f32[64]{0:T(128)}, f32[64]{0:T(128)S(1)}, u32[]{:S(2)}) copy-start(f32[64]{0:T(128)S(1)} %broadcast_multiply_fusion.1) | copy-start | bytes 772
  474.2 22.2 %collective-permute-start.7 = (bf16[64,896]{1,0:T(8,128)(2,1)}, bf16[64,896]{1,0:T(8,128)(2,1)}, u32[]{:S(2)}, u32[]{:S(2)}) collective-permute-start(bf16[64,896]{1,0:T(8,128)(2,1)} %convert_element_type.310), channel_id=1, source_target_pairs={{2,0},{4,2},{6,4},{8,6},{10,8},{12,10},{14,12},{16,14},{18,16},{20... | collective-permute-start | bytes 344072 | tf_op jit(solution)/shard_map/ppermute | solution.py:16
  477.0 11.0 collective-permute-start.9
  484.2 4.7 collective-permute-start.8
  486.1 11.3 copy-start.68
  486.4 11.0 collective-permute-start.6
  496.3 35.4 %reduce-scatter.27.cloned.1.call-start = ((), (), s32[]{:S(2)}) async-start(), calls=%async_computation.21 | async-start | bytes 688128 | tf_op jit(solution)/shard_map/reduce_scatter | solution.py:215
  497.4 7.4 copy-start.58
  497.5 7.4 copy-start.24
  504.8 204.9 %reduce-scatter.19.cloned.1.call-start = ((), (), s32[]{:S(2)}) async-start(), calls=%async_computation.17 | async-start | bytes 688128 | tf_op jit(solution)/shard_map/reduce_scatter | solution.py:133
  504.9 7.4 copy-start.13
  504.9 7.4 copy-start.28
  504.9 7.4 copy-start.29
  511.9 14.2 copy-start.81
  511.9 14.2 copy-start.80
  511.9 19.8 %copy-start.3 = (bf16[2,64,1792]{2,1,0:T(8,128)(2,1)S(1)}, bf16[2,64,1792]{2,1,0:T(8,128)(2,1)}, u32[]{:S(2)}) copy-start(bf16[2,64,1792]{2,1,0:T(8,128)(2,1)} %param.8) | copy-start | bytes 1376260
  512.0 19.8 %copy-start.88 = (f32[64]{0:T(128)S(1)}, f32[64]{0:T(128)}, u32[]{:S(2)}) copy-start(f32[64]{0:T(128)} %copy-done.87) | copy-start | bytes 772
  512.0 19.8 %copy-start.90 = (f32[64]{0:T(128)S(1)}, f32[64]{0:T(128)}, u32[]{:S(2)}) copy-start(f32[64]{0:T(128)} %copy-done.89) | copy-start | bytes 772
  512.0 201.6 %reduce-scatter.39.cloned.1.call-start = ((), (), s32[]{:S(2)}) async-start(), calls=%async_computation.27 | async-start | bytes 974848
  526.1 9.0 copy-start.12
  526.2 9.0 copy-start.26
  526.2 9.0 copy-start.27
  535.1 665.9 %all-reduce.5.cloned.1.call-start = ((), (), s32[]{:S(2)}) async-start(), calls=%async_computation.28 | async-start | bytes 69730304
  610.7 11.6 copy-start.16
  610.8 11.6 copy-start.55
  610.8 11.6 copy-start.57
  610.8 11.6 copy-start.65
  610.8 11.6 copy-start.67
  610.8 793.0 %reduce-scatter.37.cloned.1.call-start = ((), (), s32[]{:S(2)}) async-start(), calls=%async_computation.26 | async-start | bytes 20471808
  688.6 805.5 %reduce-scatter.33.cloned.1.call-start = ((), (), s32[]{:S(2)}) async-start(), calls=%async_computation.24 | async-start | bytes 6823936 | tf_op jit(solution)/shard_map/reduce_scatter | solution.py:45
  694.5 988.2 %reduce-scatter.35.cloned.1.call-start = ((), (), s32[]{:S(2)}) async-start(), calls=%async_computation.25 | async-start | bytes 18522112 | tf_op jit(solution)/shard_map/reduce_scatter | solution.py:49
  (61 other events, 131.4 us)
Sparse Core Ops, SparseCore 0:
  10.2 85.4 all-gather.7
  97.8 44.6 all-gather.9
  146.3 14.1 reduce-scatter.16
  163.3 16.0 reduce-scatter.20
  180.8 92.1 all-gather.11
  275.0 76.9 all-gather.13
  372.1 12.0 reduce-scatter.28
  400.8 12.0 reduce-scatter.24
  415.7 13.8 reduce-scatter.22
  496.5 18.5 reduce-scatter.30
  517.9 13.8 reduce-scatter.26
  534.5 13.8 reduce-scatter.18
  552.5 56.9 reduce-scatter.38
  614.1 586.9 all-reduce.4
  1205.6 198.1 reduce-scatter.36
  1408.7 85.3 reduce-scatter.32
  1499.2 183.3 reduce-scatter.34
where the time goes:
time: 1700 us; the launch traced here: 1690 us
  waiting for transfers between devices  1200 us (71%)
  matrix products  194 us (11%)
  local copies, waits for them, and re-layouts  144 us (8%)
  blocking collectives  91 us (5%)
  starting transfers between devices  23.7 us (1%)
  other arithmetic  19.5 us (1%)
    unnamed x20, waiting for transfers between devices  683 us
    reduce_scatter x1, waiting for transfers between devices, owner_sums(): lax.psum_scatter(grad_down, 'fsdp', scatter_dimension=1, tiled=True)  189 us
    reduce_scatter x1, waiting for transfers between devices, owner_sums(): lax.psum_scatter(grad_outproj, 'fsdp', scatter_dimension=1, tiled=True)  87.6 us
    all_gather x1, waiting for transfers between devices, fetch_weights(): lax.all_gather(weights[2], 'fsdp', axis=1, tiled=True)  75 us
    all_gather x1, waiting for transfers between devices, fetch_weights(): lax.all_gather(weights[3], 'fsdp', axis=1, tiled=True)  69 us
    unnamed x205, local copies, waits for them, and re-layouts  65.9 us
    add x1, local copies, waits for them, and re-layouts, body(): totals = shares if totals is None else jax.tree.map(jnp.add, totals, shares)  53.2 us
    all_gather x1, waiting for transfers between devices, fetch_weights(): lax.all_gather(weights[0], 'fsdp', axis=1, tiled=True)  39.4 us
  transfers between devices with their start and end apart: 27, of which 12 were waited for; matrix products, arithmetic and copies ran while one was open for 18% of the time, Pallas kernels for 0%

commit v1 on v0

v1 whole, which is shorter than its diff:
```python
import functools

import jax
import jax.numpy as jnp
from jax import lax
from jax.experimental import pallas as pl
from jax.experimental.pallas import tpu as pltpu
from jax.sharding import PartitionSpec as P

DH = 112
HP = 128
WINDOW = 64
EPSILON = 1e-06
SUB = 4
BF = jnp.bfloat16
F32 = jnp.float32
NN = (((1,), (0,)), ((), ()))
NT = (((1,), (1,)), ((), ()))
TN = (((0,), (0,)), ((), ()))


def dot(a, b, dims):
    return lax.dot_general(a, b, dims, preferred_element_type=F32)


def flat(value):
    return value.reshape(-1, value.shape[-1])


def half_of(cols):
    return (cols // 256) * 128


class Kernel:
    def __init__(self, cfg, refs):
        self.cfg = cfg
        self.__dict__.update(refs)
        f = lax.axis_index("fsdp")
        self.y = lax.axis_index("tp")
        self.r = f // SUB
        self.s = f % SUB
        core = self.s % 2
        self.sib = self.s + 1 - 2 * core
        self.xn = (self.s + 2) % SUB
        self.diag = (self.sib + 2) % SUB
        self.yn = 1 - self.y
        self.up = (self.r + 1) % cfg["R"]
        self.down = (self.r + cfg["R"] - 1) % cfg["R"]
        self.count = 0
        self.local_count = 0
        self.sends = []
        self.gathered = []

    def dev(self, r, s, y):
        return {"fsdp": r * SUB + s, "tp": y}

    def barrier(self):
        sem = pltpu.get_barrier_semaphore()
        partners = [self.dev(self.r, s, self.y) for s in (self.sib, self.xn, self.diag)]
        partners += [self.dev(self.r, self.s, self.yn)]
        partners += [self.dev(r, self.s, self.y) for r in (self.up, self.down)]
        for partner in partners:
            pl.semaphore_signal(sem, inc=1, device_id=partner, device_id_type=pl.DeviceIdType.MESH)
        pl.semaphore_wait(sem, len(partners))

    def remote(self, src, dst, device):
        k = self.count
        self.count += 1
        copy = pltpu.make_async_remote_copy(
            src_ref=src,
            dst_ref=dst,
            send_sem=self.send_sems.at[k],
            recv_sem=self.recv_sems.at[k],
            device_id=device,
            device_id_type=pl.DeviceIdType.MESH,
        )
        copy.start()
        self.sends.append(copy)
        return copy

    def to_sib(self, src, dst):
        return self.remote(src, dst, self.dev(self.r, self.sib, self.y))

    def to_x(self, src, dst):
        return self.remote(src, dst, self.dev(self.r, self.xn, self.y))

    def to_y(self, src, dst):
        return self.remote(src, dst, self.dev(self.r, self.s, self.yn))

    def to_up(self, src, dst):
        return self.remote(src, dst, self.dev(self.up, self.s, self.y))

    def to_down(self, src, dst):
        return self.remote(src, dst, self.dev(self.down, self.s, self.y))

    def local(self, src, dst):
        k = self.local_count
        self.local_count += 1
        copy = pltpu.make_async_copy(src, dst, self.local_sems.at[k])
        copy.start()
        return copy


    def block(self, ref, b, cols=slice(None)):
        rows = self.cfg["BR"]
        return ref.at[pl.ds(pl.multiple_of(b * rows, 16), rows), cols]

    def share_rows(self, ref, s):
        db = self.cfg["DB"]
        return ref.at[pl.ds(pl.multiple_of(self.r * self.cfg["BR"] + s * db, 16), db), :]

    def columns_out(self, shares, full):
        if self.cfg["exchanged"]:
            copies = [self.local(shares, self.block(full, self.r))]
            return lambda: [c.wait() for c in copies]
        mine = self.share_rows(full, self.s)
        copies = [
            self.remote(shares.at[s], mine, self.dev(self.r, s, self.y))
            for s in (self.xn, self.diag, self.sib)
        ]
        own = self.local(shares.at[self.s], mine)

        def wait():
            for c in copies:
                c.wait_recv()
            own.wait()

        return wait

    def columns_back(self, full, result):
        if self.cfg["exchanged"]:
            own = self.local(self.block(full, self.r), result)
            return own.wait
        copies = [
            self.remote(self.share_rows(full, s), result.at[self.s], self.dev(self.r, s, self.y))
            for s in (self.xn, self.diag, self.sib)
        ]
        own = self.local(self.share_rows(full, self.s), result.at[self.s])

        def wait():
            for c in copies:
                c.wait_recv()
            own.wait()

        return wait

    def ring_gather(self, full, step):
        ring, cols = self.cfg["R"], full.shape[1]
        low, high = slice(None), slice(None)
        if step == ring // 2:
            low, high = slice(0, half_of(cols)), slice(half_of(cols), cols)
        ahead = (self.r + ring - step + 1) % ring
        back = (self.r + step - 1) % ring
        a = self.block(full, ahead, low)
        b = self.block(full, back, high)
        pair = (self.to_up(a, a), self.to_down(b, b))
        self.gathered += pair

        def wait():
            for c in pair:
                c.wait_recv()

        return wait

    def ring_gather_rest(self, full, wait):
        for step in range(2, self.cfg["R"] // 2 + 1):
            wait()
            wait = self.ring_gather(full, step)
        return wait

    def ring_scatter(self, grad, slots, step):
        ring, cols = self.cfg["R"], grad.shape[1]
        first_up, first_down, rest_up, rest_down = slots
        low, high = slice(None), slice(None)
        if step == 1:
            low, high = slice(0, half_of(cols)), slice(half_of(cols), cols)
            to_up, to_down = first_up, first_down
        else:
            to_up, to_down = rest_up.at[step - 2], rest_down.at[step - 2]
        width = cols
        if step == 1:
            to_up = to_up.at[:, : half_of(cols)]
            to_down = to_down.at[:, : cols - half_of(cols)]
        else:
            to_up, to_down = to_up.at[:, :width], to_down.at[:, :width]
        distance = ring // 2 - step + 1
        ahead = (self.r + distance) % ring
        back = (self.r + ring - distance) % ring
        pair = (
            self.to_up(self.block(grad, ahead, low), to_up),
            self.to_down(self.block(grad, back, high), to_down),
        )

        def add():
            for c in pair:
                c.wait_recv()
            near = ring // 2 - step
            targets = [((self.r + near) % ring, low, to_up), ((self.r + ring - near) % ring, high, to_down)]
            tile = next(t for t in (112, 64, 16) if self.cfg["BR"] % t == 0)
            for i in range(self.cfg["BR"] // tile):
                if near == 0:
                    rows = pl.ds(pl.multiple_of(self.r * self.cfg["BR"] + i * tile, 16), tile)
                    part = slice(i * tile, (i + 1) * tile)
                    total = grad[rows, :].astype(F32) + to_up[part, :].astype(F32) + to_down[part, :].astype(F32)
                    grad[rows, :] = total.astype(BF)
                else:
                    for b, span, ref in targets:
                        rows = pl.ds(pl.multiple_of(b * self.cfg["BR"] + i * tile, 16), tile)
                        part = slice(i * tile, (i + 1) * tile)
                        total = grad[rows, span].astype(F32) + ref[part, :].astype(F32)
                        grad[rows, span] = total.astype(BF)

        return pair, add


    def gather_start(self, buf):
        own = buf.at[self.s, self.y]
        return {"x": self.to_x(own, own), "y": self.to_y(own, own), "own": self.to_sib(own, own), "buf": buf}

    def gather_relay(self, g):
        buf, cut = g["buf"], self.cfg["cut"]
        g["x"].wait_recv()
        part = buf.at[self.xn, self.y, :, slice(0, cut)]
        g["d0"] = self.to_y(part, part)
        whole = buf.at[self.xn, self.y]
        g["fx"] = self.to_sib(whole, whole)
        g["y"].wait_recv()
        part = buf.at[self.s, self.yn, :, slice(cut, self.cfg["D"])]
        g["d1"] = self.to_x(part, part)
        whole = buf.at[self.s, self.yn]
        g["fy"] = self.to_sib(whole, whole)

    def gather_finish(self, g):
        buf, cut = g["buf"], self.cfg["cut"]
        g["d0"].wait_recv()
        part = buf.at[self.xn, self.yn, :, slice(0, cut)]
        f0 = self.to_sib(part, part)
        g["d1"].wait_recv()
        part = buf.at[self.xn, self.yn, :, slice(cut, self.cfg["D"])]
        f1 = self.to_sib(part, part)
        for c in (g["own"], g["fx"], g["fy"], f0, f1):
            c.wait_recv()
        g["copies"] = [g[n] for n in ("own", "x", "y", "d0", "d1", "fx", "fy")] + [f0, f1]

    def scatter_pair(self, st, partial):
        sc, rc = st["sc"], st["rc"]
        copies = []
        for k, pair in enumerate(((self.sib + 2) % SUB, self.sib)):
            sc[k] = partial(pair).astype(BF).reshape(sc.shape[1:])
            copies.append(self.to_sib(sc.at[k], rc.at[k]))
        return {"pair": copies, "st": st}

    def scatter_send(self, g, partial):
        st, cut, d = g["st"], self.cfg["cut"], self.cfg["D"]
        so, rc = st["so"], st["rc"]
        lo, hi = slice(0, cut), slice(cut, d)
        value = partial(self.xn)
        g["pair"][0].wait_recv()
        so[0] = (value + flat(rc[0].astype(F32))).astype(BF).reshape(so.shape[1:])
        g["d0"] = self.to_x(so.at[0, self.yn, :, lo], st["rd0"])
        g["d1"] = self.to_y(so.at[0, self.yn, :, hi], st["rd1"])
        g["x0"] = self.to_x(so.at[0, self.y, :, lo], st["rx"].at[:, lo])
        value = partial(self.s)
        g["pair"][1].wait_recv()
        so[1] = (value + flat(rc[1].astype(F32))).astype(BF).reshape(so.shape[1:])
        g["y1"] = self.to_y(so.at[1, self.yn, :, hi], st["ry"].at[:, hi])

    def scatter_relay(self, g):
        st, cut, d = g["st"], self.cfg["cut"], self.cfg["D"]
        so = st["so"]
        lo, hi = slice(0, cut), slice(cut, d)
        g["d1"].wait_recv()
        so[0, self.y, :, hi] = (so[0, self.y, :, hi].astype(F32) + st["rd1"][...].astype(F32)).astype(BF)
        g["x1"] = self.to_x(so.at[0, self.y, :, hi], st["rx"].at[:, hi])
        g["d0"].wait_recv()
        so[1, self.yn, :, lo] = (so[1, self.yn, :, lo].astype(F32) + st["rd0"][...].astype(F32)).astype(BF)
        g["y0"] = self.to_y(so.at[1, self.yn, :, lo], st["ry"].at[:, lo])

    def scatter_finish(self, g):
        st = g["st"]
        for name in ("x0", "x1", "y0", "y1"):
            g[name].wait_recv()
        total = st["so"][1, self.y].astype(F32) + st["rx"][...].astype(F32) + st["ry"][...].astype(F32)
        self.settle(g["pair"] + [g[n] for n in ("d0", "d1", "x0", "x1", "y0", "y1")])
        return total


    def project(self, w):
        def step(i, _):
            rows = flat(self.u1[i])
            out = dot(rows, w[...], NN).astype(BF)
            self.qkv[pl.ds(1 + 2 * i, 2)] = out.reshape(2, 2 * WINDOW, out.shape[1])
            return 0

        lax.fori_loop(0, SUB, step, 0)

    def masks(self, quad):
        before, own = self.starts[quad], self.starts[quad + 1]
        lane = lax.broadcasted_iota(jnp.int32, before.shape, 1)
        even = jnp.where(lane < WINDOW, pltpu.roll(before, WINDOW, 1), pltpu.roll(own, WINDOW, 1))
        shape = (WINDOW, 2 * WINDOW)
        i = lax.broadcasted_iota(jnp.int32, shape, 0)
        j = lax.broadcasted_iota(jnp.int32, shape, 1)
        square = (2 * WINDOW, 2 * WINDOW)
        later = lax.broadcasted_iota(jnp.int32, square, 0) > lax.broadcasted_iota(jnp.int32, square, 1)
        later = later.astype(F32).astype(BF)
        band = (j <= i + WINDOW) & (j > i)
        result = []
        for rows in (even, own):
            per_batch = []
            for batch in range(2):
                line = jnp.broadcast_to(rows[batch : batch + 1, :], shape)
                line = jnp.where(j <= i + WINDOW, line, 0.0).astype(BF)
                between = dot(line, later, NN)
                per_batch.append(band & (between < 0.5))
            result.append(per_batch)
        return result

    def tile(self, index, batch, part, head):
        cols = slice(part * 2 * HP + head * HP, part * 2 * HP + (head + 1) * HP)
        return self.qkv[index, batch * WINDOW : (batch + 1) * WINDOW, cols]

    def attend(self):
        def step(n, _):
            quad = SUB - 1 - n
            allowed = self.masks(quad)
            for half in range(2):
                p = 2 * quad + half
                for batch in range(2):
                    for head in range(2):
                        q = self.tile(p + 1, batch, 0, head)
                        k = jnp.concatenate([self.tile(p, batch, 1, head), self.tile(p + 1, batch, 1, head)], axis=0)
                        v = jnp.concatenate([self.tile(p, batch, 2, head), self.tile(p + 1, batch, 2, head)], axis=0)
                        scores = dot(q, k, NT) * DH ** (-0.5)
                        scores = jnp.where(allowed[half][batch], scores, -1e30)
                        top = jnp.max(scores, axis=-1, keepdims=True)
                        weights = jnp.exp(scores - top)
                        probs = weights / jnp.sum(weights, axis=-1, keepdims=True)
                        self.probs[p, 2 * batch + head] = probs
                        out = dot(probs.astype(BF), v, NN).astype(BF)
                        self.heads[quad, half, batch * WINDOW : (batch + 1) * WINDOW, head * HP : (head + 1) * HP] = out
            return 0

        lax.fori_loop(0, SUB, step, 0)

    def attend_back_quad(self, quad):
        for half in range(2):
            p = 2 * quad + half
            for batch in range(2):
                rows = slice(batch * WINDOW, (batch + 1) * WINDOW)
                for head in range(2):
                    cols = slice(head * HP, (head + 1) * HP)
                    q = self.tile(p + 1, batch, 0, head)
                    k = jnp.concatenate([self.tile(p, batch, 1, head), self.tile(p + 1, batch, 1, head)], axis=0)
                    v = jnp.concatenate([self.tile(p, batch, 2, head), self.tile(p + 1, batch, 2, head)], axis=0)
                    probs = self.probs[p, 2 * batch + head]
                    d_out = self.d_heads[quad, half, rows, cols]
                    d_probs = dot(d_out, v, NT)
                    inner = jnp.sum(probs * d_probs, axis=-1, keepdims=True)
                    d_scores = (probs * (d_probs - inner)).astype(BF)
                    d_q = dot(d_scores, k, NN) * DH ** (-0.5)
                    d_k = dot(d_scores, q, TN) * DH ** (-0.5)
                    d_v = dot(probs.astype(BF), d_out, TN)
                    self.qkv[p + 1, rows, head * HP : (head + 1) * HP] = d_q.astype(BF)
                    for part, grad in ((1, d_k), (2, d_v)):
                        slot = slice((part - 1) * 2 * HP + head * HP, (part - 1) * 2 * HP + (head + 1) * HP)
                        place = slice(part * 2 * HP + head * HP, part * 2 * HP + (head + 1) * HP)
                        done = self.carry[rows, slot] + grad[:WINDOW]
                        self.qkv[p, rows, place] = done.astype(BF)
                        self.carry[rows, slot] = grad[WINDOW:]

    def grad_into(self, target, left, right):
        width = 256

        def step(m, _):
            cols = pl.ds(pl.multiple_of(m * width, width), width)
            a = flat(left[:, :, :, cols])
            target[cols, :] = dot(a, right(), TN).astype(BF)
            return 0

        lax.fori_loop(0, self.cfg["D"] // width, step, 0)

    def feed_forward(self):
        ff = self.w_dn.shape[1]

        def step(i, _):
            rows = flat(self.u2[i])
            gate = dot(rows, self.w_gu[:, :ff], NN)
            upward = dot(rows, self.w_gu[:, ff:], NN)
            d_hidden = dot(flat(self.g[i]), self.w_dn[...], NN)
            sig = jax.nn.sigmoid(gate)
            silu = gate * sig
            shape = (2, 2 * WINDOW, ff)
            self.hidden[i] = (silu * upward).astype(BF).reshape(shape)
            d_gate = d_hidden * upward * sig * (1.0 + gate * (1.0 - sig))
            self.d_gu[i, :, :, :ff] = d_gate.astype(BF).reshape(shape)
            self.d_gu[i, :, :, ff:] = (d_hidden * silu).astype(BF).reshape(shape)
            return 0

        lax.fori_loop(0, SUB, step, 0)

    def run(self):
        cfg = self.cfg
        me = (self.s, self.y)
        norm = lambda v: lax.rsqrt(jnp.mean(v * v, axis=-1, keepdims=True) + EPSILON)
        steps = cfg["R"] // 2

        self.barrier()
        qkv_here = self.columns_out(self.sh_qkv, self.w_qkv)
        start_copies = [
            self.remote(self.starts_in, self.starts.at[self.s + 1], self.dev(self.r, s, self.y))
            for s in (self.sib, self.xn, self.diag)
        ]
        self.starts[self.s + 1] = self.starts_in[...]

        x = self.x[...].astype(F32)
        self.u1[me] = (x * norm(x)).astype(BF)
        gather_one = self.gather_start(self.u1)
        out_here = self.columns_out(self.sh_out, self.w_out)
        qkv_here()
        ring_qkv = self.ring_gather(self.w_qkv, 1)
        gu_here = self.columns_out(self.sh_gu, self.w_gu)
        for c in start_copies:
            c.wait_recv()
        rim_starts = self.to_up(self.starts.at[SUB], self.starts.at[0])
        self.gather_relay(gather_one)
        out_here()
        ring_qkv = self.ring_gather_rest(self.w_qkv, ring_qkv)
        ring_out = self.ring_gather(self.w_out, 1)
        gu_here()
        ring_gu = self.ring_gather(self.w_gu, 1)
        self.gather_finish(gather_one)
        self.g[me] = self.g_in[...]
        gather_g = self.gather_start(self.g)
        dn_here = self.columns_out(self.sh_dn, self.w_dn)
        ring_qkv()

        self.project(self.w_qkv)
        rims = [
            self.to_up(self.qkv.at[2 * SUB, :, part], self.qkv.at[0, :, part])
            for part in (slice(2 * HP, 4 * HP), slice(4 * HP, 6 * HP))
        ]
        ring_out = self.ring_gather_rest(self.w_out, ring_out)
        self.gather_relay(gather_g)
        rim_starts.wait_recv()
        for c in rims:
            c.wait_recv()
        self.attend()
        self.gather_finish(gather_g)
        dn_here()
        ring_out()

        partial = lambda pair: dot(flat(self.heads[pair]), self.w_out[...], NT)
        stage = {n: getattr(self, n) for n in ("sc", "rc", "so", "rd0", "rd1", "rx", "ry")}
        scatter = self.scatter_pair(stage, partial)
        self.scatter_send(scatter, partial)
        self.scatter_relay(scatter)
        ring_gu = self.ring_gather_rest(self.w_gu, ring_gu)
        ring_dn = self.ring_gather(self.w_dn, 1)
        self.resid[...] = self.x[...].astype(F32) + self.scatter_finish(scatter)
        resid = self.resid[...]
        self.u2[me] = (resid * norm(resid)).astype(BF)
        gather_two = self.gather_start(self.u2)
        self.gather_relay(gather_two)
        self.gather_finish(gather_two)
        ring_gu()
        ring_dn = self.ring_gather_rest(self.w_dn, ring_dn)
        ring_dn()

        self.feed_forward()
        partial = lambda pair: dot(flat(self.d_gu[pair]), self.w_gu[...], NT)
        scatter = self.scatter_pair(stage, partial)
        self.scatter_send(scatter, partial)
        self.grad_into(self.g_dn, self.g, lambda: flat(self.hidden[...]))
        dn_add = self.ring_scatter(self.g_dn, self.slots_dn, 1)[1]
        self.scatter_relay(scatter)
        self.settle(self.gathered)
        self.grad_into(self.w_gu, self.u2, lambda: flat(self.d_gu[...]))
        gu_add = self.ring_scatter(self.w_gu, self.slots_gu, 1)[1]
        d_unit = self.scatter_finish(scatter)
        resid = self.resid[...]
        scale = norm(resid)
        unit = resid * scale
        inner = jnp.mean(d_unit * unit, axis=-1, keepdims=True)
        self.d_resid[...] = self.g_in[...].astype(F32) + scale * (d_unit - unit * inner)
        self.d_r[me] = self.d_resid[...].astype(BF)
        self.settle(gather_g["copies"] + gather_two["copies"] + rims)
        gather_d = self.gather_start(self.d_r)
        dn_add = self.ring_scatter_rest(self.g_dn, self.slots_dn, dn_add)
        self.gather_relay(gather_d)
        gu_add = self.ring_scatter_rest(self.w_gu, self.slots_gu, gu_add)
        self.gather_finish(gather_d)

        def heads_back(i, _):
            value = dot(flat(self.d_r[i]), self.w_out[...], NN).astype(BF)
            self.d_heads[i] = value.reshape(2, 2 * WINDOW, 2 * HP)
            return 0

        lax.fori_loop(0, SUB, heads_back, 0)

        view = {
            "sc": self.u2.at[0:2],
            "so": self.u2.at[2:4],
            "rc": self.g.at[0:2],
            "rd0": self.g.at[2, 0, :, slice(0, cfg["cut"])],
            "rd1": self.g.at[2, 0, :, slice(cfg["cut"], cfg["D"])],
            "rx": self.g.at[2, 1],
            "ry": self.g.at[3, 0],
        }
        partial = lambda pair: dot(flat(self.hidden[pair]), self.w_dn[...], NT)
        mlp = self.scatter_pair(view, partial)
        self.scatter_send(mlp, partial)

        self.carry[...] = jnp.zeros_like(self.carry)
        self.attend_back_quad(0)
        rim_back = [
            self.to_down(self.qkv.at[0, :, part], self.rim.at[:, slice(k * 2 * HP, (k + 1) * 2 * HP)])
            for k, part in enumerate((slice(2 * HP, 4 * HP), slice(4 * HP, 6 * HP)))
        ]
        self.scatter_relay(mlp)

        def back(quad, _):
            self.attend_back_quad(quad)
            return 0

        lax.fori_loop(1, SUB, back, 0)
        for c in rim_back:
            c.wait_recv()
        done = self.carry[...] + self.rim[...].astype(F32)
        self.qkv[2 * SUB, :, 2 * HP :] = done.astype(BF)

        d_qkv = lambda: flat(self.qkv[1:])
        self.grad_into(self.g_qkv, self.u1, d_qkv)
        dn_add()
        dn_back = self.columns_back(self.g_dn, self.o_dn)
        gu_add()
        gu_back = self.columns_back(self.w_gu, self.o_gu)
        qkv_add = self.ring_scatter(self.g_qkv, self.slots_qkv, 1)[1]
        partial = lambda pair: dot(flat(self.qkv[pl.ds(1 + 2 * pair, 2)]), self.w_qkv[...], NT)
        scatter = self.scatter_pair(stage, partial)
        self.scatter_send(scatter, partial)
        self.grad_into(self.w_out, self.d_r, lambda: flat(self.heads[...]))
        qkv_add = self.ring_scatter_rest(self.g_qkv, self.slots_qkv, qkv_add)
        out_add = self.ring_scatter(self.w_out, self.slots_out, 1)[1]
        self.scatter_relay(scatter)
        self.out[...] = (self.resid[...] + self.scatter_finish(mlp)).astype(BF)
        out_add = self.ring_scatter_rest(self.w_out, self.slots_out, out_add)
        d_unit = self.scatter_finish(scatter)
        x = self.x[...].astype(F32)
        scale = norm(x)
        unit = x * scale
        inner = jnp.mean(d_unit * unit, axis=-1, keepdims=True)
        self.in_grad[...] = self.d_resid[...] + scale * (d_unit - unit * inner)
        qkv_add()
        qkv_back = self.columns_back(self.g_qkv, self.o_qkv)
        out_add()
        out_back = self.columns_back(self.w_out, self.o_out)
        for wait in (dn_back, gu_back, qkv_back, out_back):
            wait()
        self.settle()

    def ring_scatter_rest(self, grad, slots, add):
        for step in range(2, self.cfg["R"] // 2 + 1):
            add()
            add = self.ring_scatter(grad, slots, step)[1]
        return add

    def settle(self, copies=None):
        for c in self.sends:
            if copies is None or any(c is other for other in copies):
                c.wait_send()
        if copies is None:
            self.sends = []
        else:
            self.sends = [c for c in self.sends if not any(c is other for other in copies)]


def fused(cfg, cols, shares, starts, x, g):
    n_qkv, n_out, n_gu, n_dn = cols
    d, ring, br, db = cfg["D"], cfg["R"], cfg["BR"], cfg["DB"]
    rows = 2 * WINDOW
    cut = cfg["cut"]
    steps = ring // 2
    anywhere = pl.BlockSpec(memory_space=pl.ANY)
    vmem = pl.BlockSpec(memory_space=pltpu.VMEM)
    result = (br,) if cfg["exchanged"] else (SUB, db)
    outs = [
        ("out", (rows, d), BF, vmem),
        ("in_grad", (rows, d), F32, vmem),
        ("o_qkv", result + (n_qkv,), BF, anywhere),
        ("o_out", result + (n_out,), BF, anywhere),
        ("o_gu", result + (n_gu,), BF, anywhere),
        ("o_dn", result + (n_dn,), BF, anywhere),
    ]
    ins = [
        ("sh_qkv", anywhere),
        ("sh_out", anywhere),
        ("sh_gu", anywhere),
        ("sh_dn", anywhere),
        ("starts_in", vmem),
        ("x", vmem),
        ("g_in", vmem),
    ]
    plane = (SUB, 2, rows)
    wide = max(n_gu, n_qkv)
    scratch = [
        ("w_qkv", (d, n_qkv), BF),
        ("w_out", (d, n_out), BF),
        ("w_gu", (d, n_gu), BF),
        ("w_dn", (d, n_dn), BF),
        ("g_qkv", (d, n_qkv), BF),
        ("g_dn", (d, n_dn), BF),
        ("u1", plane + (d,), BF),
        ("u2", plane + (d,), BF),
        ("g", plane + (d,), BF),
        ("d_r", plane + (d,), BF),
        ("starts", (SUB + 1, 8, rows), F32),
        ("qkv", (2 * SUB + 1, rows, n_qkv), BF),
        ("probs", (2 * SUB, 4, WINDOW, 2 * WINDOW), F32),
        ("heads", plane + (n_out,), BF),
        ("d_heads", plane + (n_out,), BF),
        ("hidden", plane + (n_dn,), BF),
        ("d_gu", plane + (n_gu,), BF),
        ("carry", (rows, 4 * HP), F32),
        ("rim", (rows, 4 * HP), BF),
        ("resid", (rows, d), F32),
        ("d_resid", (rows, d), F32),
        ("sc", (2, 2, rows, d), BF),
        ("rc", (2, 2, rows, d), BF),
        ("so", (2, 2, rows, d), BF),
        ("rd0", (rows, cut), BF),
        ("rd1", (rows, d - cut), BF),
        ("rx", (rows, d), BF),
        ("ry", (rows, d), BF),
    ]
    for name, width in (("wide", wide), ("dn", n_dn), ("out", n_out)):
        high = width - half_of(width)
        scratch += [
            ("first_up_" + name, (br, high), BF),
            ("first_down_" + name, (br, high), BF),
            ("rest_up_" + name, (steps - 1, br, width), BF),
            ("rest_down_" + name, (steps - 1, br, width), BF),
        ]
    number = 110 + 4 * (6 + 4 * ring)
    names = [n for n, _ in ins] + [n for n, *_ in outs] + [n for n, *_ in scratch]
    names += ["send_sems", "recv_sems", "local_sems"]

    def kernel(*refs):
        table = dict(zip(names, refs, strict=True))
        for name, key in (("qkv", "wide"), ("gu", "wide"), ("dn", "dn"), ("out", "out")):
            table["slots_" + name] = tuple(
                table[part + key] for part in ("first_up_", "first_down_", "rest_up_", "rest_down_")
            )
        Kernel(cfg, table).run()

    results = pl.pallas_call(
        kernel,
        out_shape=[jax.ShapeDtypeStruct(shape, kind) for _, shape, kind, _ in outs],
        in_specs=[spec for _, spec in ins],
        out_specs=[spec for *_, spec in outs],
        scratch_shapes=[pltpu.VMEM(shape, kind) for _, shape, kind in scratch]
        + [
            pltpu.SemaphoreType.DMA((number,)),
            pltpu.SemaphoreType.DMA((number,)),
            pltpu.SemaphoreType.DMA((8,)),
        ],
        compiler_params=pltpu.CompilerParams(
            collective_id=0, has_side_effects=True, vmem_limit_bytes=63 * 2**20
        ),
    )(*shares, starts, x, g)
    return results


def padded(value, size):
    pads = [(0, 0)] * (value.ndim - 1) + [(0, size - value.shape[-1])]
    return jnp.pad(value, pads)


def body(ring, tokens, doc_starts, w_qkv, w_out, w_gate_up, w_down, gains, cotangent):
    batches, rows, d = tokens.shape
    db = w_qkv.shape[1]
    ff = w_gate_up.shape[2] // SUB
    ffp = -(-ff // HP) * HP
    heads = w_qkv.shape[2] // (SUB * DH)
    gain = gains.astype(F32)

    exchanged = db % 16 != 0
    groups = [[r * SUB + s for s in range(SUB)] for r in range(ring)]
    cfg = {
        "D": d,
        "R": ring,
        "DB": db,
        "BR": SUB * db,
        "cut": d // 256 * 128,
        "exchanged": exchanged,
    }

    sh_qkv = (w_qkv.astype(F32) * gain[0][None, :, None]).astype(BF).reshape(3, db, SUB, heads, DH)
    sh_qkv = padded(sh_qkv, HP).transpose(2, 1, 0, 3, 4).reshape(SUB, db, 3 * heads * HP)
    sh_out = w_out.T.reshape(db, SUB, heads, DH)
    sh_out = padded(sh_out, HP).transpose(1, 0, 2, 3).reshape(SUB, db, heads * HP)
    sh_gu = (w_gate_up.astype(F32) * gain[1][None, :, None]).astype(BF).reshape(2, db, SUB, ff)
    sh_gu = padded(sh_gu, ffp).transpose(2, 1, 0, 3).reshape(SUB, db, 2 * ffp)
    sh_dn = padded(w_down.T.reshape(db, SUB, ff), ffp).transpose(1, 0, 2)
    shares = [sh_qkv, sh_out, sh_gu, sh_dn]
    cols = [v.shape[2] for v in shares]

    def swapped(v):
        return lax.all_to_all(v, "fsdp", 0, 0, axis_index_groups=groups, tiled=True)

    if exchanged:
        shares = [swapped(v).reshape(SUB * db, v.shape[2]) for v in shares]
    starts = jnp.pad(doc_starts.astype(F32), ((0, 8 - batches), (0, 0)))
    out, in_grad, *grads = fused(
        cfg, cols, shares, starts, tokens.reshape(batches * rows, d), cotangent.reshape(batches * rows, d)
    )
    if exchanged:
        grads = [swapped(v.reshape(SUB, db, v.shape[1])) for v in grads]
    g_qkv, g_out, g_gu, g_dn = [v.astype(F32) for v in grads]
    g_qkv = g_qkv.reshape(SUB, db, 3, heads, HP)[..., :DH].transpose(2, 1, 0, 3, 4).reshape(w_qkv.shape)
    g_out = g_out.reshape(SUB, db, heads, HP)[..., :DH].transpose(0, 2, 3, 1).reshape(w_out.shape)
    g_gu = g_gu.reshape(SUB, db, 2, ffp)[..., :ff].transpose(2, 1, 0, 3).reshape(w_gate_up.shape)
    g_dn = g_dn[..., :ff].transpose(0, 2, 1).reshape(w_down.shape)
    gain_sums = jnp.stack(
        [
            jnp.sum(g_qkv * w_qkv.astype(F32), axis=(0, 2)),
            jnp.sum(g_gu * w_gate_up.astype(F32), axis=(0, 2)),
        ]
    )
    gain_sums = gain_sums + lax.ppermute(gain_sums, "tp", [(0, 1), (1, 0)])
    return (
        out.reshape(tokens.shape),
        in_grad.reshape(tokens.shape),
        g_qkv * gain[0][None, :, None],
        g_out,
        g_gu * gain[1][None, :, None],
        g_dn,
        gain_sums,
    )


def solution(mesh):
    in_specs = (
        P(None, ("fsdp", "tp"), None),
        P(None, "fsdp"),
        P(None, "fsdp", "tp"),
        P("tp", "fsdp"),
        P(None, "fsdp", "tp"),
        P("tp", "fsdp"),
        P(None, "fsdp"),
        P(None, ("fsdp", "tp"), None),
    )
    out_specs = (
        P(None, ("fsdp", "tp"), None),
        P(None, ("fsdp", "tp"), None),
        P(None, "fsdp", "tp"),
        P("tp", "fsdp"),
        P(None, "fsdp", "tp"),
        P("tp", "fsdp"),
        P(None, "fsdp"),
    )
    ring = mesh.shape["fsdp"] // SUB
    return jax.shard_map(
        functools.partial(body, ring), mesh=mesh, in_specs=in_specs, out_specs=out_specs, check_vma=False
    )
```

time: 1700 us -> 475 us (0.28)
  waiting for transfers between devices: 1200 us -> 0.01 us
  Pallas kernels: 0 us -> 429 us
  matrix products: 194 us -> 0 us
  local copies, waits for them, and re-layouts: 144 us -> 25.9 us
  blocking collectives: 91 us -> 0 us
  starting transfers between devices: 23.7 us -> 1.54 us
    unnamed x20 -> x0, waiting for transfers between devices: 683 us -> none
    pallas_call x0 -> x1, Pallas kernels: none -> 429 us  [fused(): pl.pallas_call(kernel, out_shape=[jax.ShapeDtypeStruct(shape, kind) for _...]
    reduce_scatter x10 -> x0, waiting for transfers between devices: 309 us -> none  [the longest x1 189 us: owner_sums(): lax.psum_scatter(grad_down, 'fsdp', scatter_dimension=1, tiled=True)]
    all_gather x4 -> x0, waiting for transfers between devices: 208 us -> none  [the longest x1 75 us: fetch_weights(): lax.all_gather(weights[2], 'fsdp', axis=1, tiled=True)]
    dot_general x36 -> x0, matrix products: 194 us -> none  [the longest x2 36.1 us: body(): jnp.einsum('td,stf->sdf', mixed_all, d_gate_up, preferred_element_type=jn...]
    all_gather x9 -> x0, blocking collectives: 85.5 us -> none  [the longest x1 20.3 us: fetch_weights(): lax.all_gather(weights[4], 'fsdp', axis=1, tiled=True)]
    unnamed x205 -> x24, local copies, waits for them, and re-layouts: 65.9 us -> 1.75 us
    add x1 -> x0, local copies, waits for them, and re-layouts: 53.2 us -> none  [body(): totals = shares if totals is None else jax.tree.map(jnp.add, totals, shares)]
  transfers between devices with their start and end apart: 27 -> 1, of which waited for: 12 -> 0; matrix products, arithmetic and copies ran while one was open for 18% -> 1% of each run, Pallas kernels for 0% -> 0%
where the time goes in v1:
time: 475 us; the launch traced here: 467 us
  Pallas kernels  429 us (90%)
  local copies, waits for them, and re-layouts  25.9 us (5%)
  other arithmetic  9.16 us (2%)
    pallas_call x1, Pallas kernels, fused(): pl.pallas_call(kernel, out_shape=[jax.ShapeDtypeStruct(shape, kind) for _...  429 us
  transfers between devices with their start and end apart: 1, of which 0 were waited for; matrix products, arithmetic and copies ran while one was open for 1% of the time, Pallas kernels for 0%

profile of v1, /device:TPU:0, one launch (start us, length us, event | category | flops | bytes accessed | tf_op | source)
XLA Modules:
  0.0 466.7 jit_solution(6887222247531256652)
XLA Ops:
  0.6 0.7 convert_element_type.35
  1.3 1.5 fusion
  2.8 1.3 reshape.89
  4.1 1.2 copy.23
  5.3 1.0 pad_bitcast_fusion
  6.3 0.0 copy-start.1
  6.3 1.6 reshape.90.refs_2_
  7.9 0.0 copy-done.1
  7.9 0.2 fusion.2
  8.1 0.8 reshape.85
  8.9 0.0 copy-start.6
  8.9 0.7 pad_bitcast_fusion.1
  9.6 1.2 reshape.86.refs_0_
  10.8 0.0 copy-done.6
  10.8 0.6 reshape.91
  11.4 0.0 copy-start.9
  11.4 0.1 copy.24
  11.5 0.0 copy-start.10
  11.5 0.9 pad_bitcast_fusion.2.refs_3_
  12.4 0.0 copy-done.9
  12.4 0.3 reshape.87
  12.7 0.2 pad_bitcast_fusion.3
  12.9 0.8 reshape.88.refs_1_
  13.8 0.0 copy-done.10
  13.8 0.6 pad.24.refs_4_
  14.4 428.7 %shard_map.135 = (bf16[128,1792]{1,0:T(8,128)(2,1)}, f32[128,1792]{1,0:T(8,128)}, bf16[4,112,768]{2,1,0:T(8,128)(2,1)}, bf16[4,112,256]{2,1,0:T(8,128)(2,1)}, bf...) custom-call(bf16[4,112,768]{2,1,0:T(8,128)(2,1)} %reshape.86.refs_0_, bf16[4,112,256]{2,1,0:T(8,128)(2,1)} %reshape.88.refs_1_, ...), custom_call_target="tpu_custom_call" | custom-call | tf_op jit(solution)/shard_map/pallas_call | solution.py:656
  443.1 2.7 reshape.102
  445.8 0.8 convert_bitcast_fusion
  446.6 1.5 copy.27
  448.1 0.0 copy-start
  448.1 2.4 reshape.112
  450.6 0.0 copy-done
  450.6 0.0 copy-start.4
  450.6 3.4 fusion.1
  454.0 0.0 copy-done.4
  454.0 0.2 reshape.96
  454.2 0.5 convert_bitcast_fusion.1
  454.7 0.5 copy.25
  455.2 0.0 copy-start.2
  455.2 2.0 reshape.108
  457.2 0.0 copy-done.2
  457.2 0.0 copy-start.5
  457.2 1.3 fusion.3
  458.6 0.0 copy-start.8
  458.6 1.5 collective-permute-start
  460.1 0.0 copy-done.5
  460.1 0.1 convert_bitcast_fusion.2
  460.2 0.0 copy-done.8
  460.2 0.1 reshape.99
  460.3 0.2 convert_bitcast_fusion.3
  460.4 0.4 copy.28
  460.9 1.6 reshape.114
  462.5 0.0 copy-start.7
  462.5 0.0 copy-start.3
  462.5 0.2 copy.26
  462.6 1.3 reshape.110
  464.0 0.0 collective-permute-done
  464.0 0.6 fusion.4
  464.5 0.0 copy-done.7
  464.5 0.8 copy.35
  465.3 0.0 copy-done.3
  465.3 0.9 copy.36
  (3 shorter events, 0.0 us)
Async XLA Ops:
  6.3 1.6 copy-start.1
  8.9 1.9 copy-start.6
  11.4 1.0 copy-start.9
  11.5 2.3 copy-start.10
  448.1 2.5 copy-start
  450.6 3.4 copy-start.4
  455.2 2.1 copy-start.2
  457.2 2.9 copy-start.5
  458.6 1.6 copy-start.8
  458.6 5.4 %collective-permute-start = (f32[2,112]{1,0:T(2,128)S(1)}, f32[2,112]{1,0:T(2,128)S(1)}, u32[]{:S(2)}, u32[]{:S(2)}) collective-permute-start(f32[2,112]{1,0:T(2,128)S(1)} %pad_maximum_fusion), channel_id=1, source_target_pairs={{0,1},{1,0},{2,3},{3,2},{4,5},{5,4},{6,7},{7,6},{8,9},{9,8},{10,11... | collective-permute-start | bytes 2696 | tf_op jit(solution)/shard_map/ppermute | solution.py:730
  462.5 2.1 copy-start.7
  462.5 2.8 copy-start.3

commit v2 on v1

v2 whole, which is shorter than its diff:
```python
import functools

import jax
import jax.numpy as jnp
from jax import lax
from jax.experimental import pallas as pl
from jax.experimental.pallas import tpu as pltpu
from jax.sharding import PartitionSpec as P

DH = 112
HP = 128
WINDOW = 64
EPSILON = 1e-06
SUB = 4
BF = jnp.bfloat16
F32 = jnp.float32
NN = (((1,), (0,)), ((), ()))
NT = (((1,), (1,)), ((), ()))
TN = (((0,), (0,)), ((), ()))


def dot(a, b, dims):
    return lax.dot_general(a, b, dims, preferred_element_type=F32)


def flat(value):
    return value.reshape(-1, value.shape[-1])


class Kernel:
    def __init__(self, cfg, refs):
        self.cfg = cfg
        self.__dict__.update(refs)
        self.f = lax.axis_index("fsdp")
        self.y = lax.axis_index("tp")
        core = self.f % 2
        self.x = (self.f // 2) % 2
        self.hi = self.f // 8
        self.s = (self.f // 4) % 2 * 2 + core
        self.sib = self.s + 1 - 2 * core
        self.zn = (self.s + 2) % SUB
        self.diag = (self.sib + 2) % SUB
        self.yn = 1 - self.y
        self.next_hi = (self.hi + 1) % cfg["NH"]
        self.last_hi = (self.hi + cfg["NH"] - 1) % cfg["NH"]
        self.count = 0
        self.local_count = 0
        self.sends = []
        self.gathered = []

    def index(self, hi, s, x):
        return hi * 8 + s // 2 * 4 + x * 2 + s % 2

    def mate(self, s):
        return {"fsdp": self.index(self.hi, s, self.x), "tp": self.y}

    def peer(self, hi, x):
        return {"fsdp": self.index(hi, self.s, x), "tp": self.y}

    def barrier(self):
        sem = pltpu.get_barrier_semaphore()
        partners = [self.mate(s) for s in (self.sib, self.zn, self.diag)]
        partners += [{"fsdp": self.f, "tp": self.yn}, self.peer(self.hi, 1 - self.x)]
        partners += [self.peer(self.next_hi, self.x), self.peer(self.next_hi, 1 - self.x)]
        if self.cfg["NH"] > 2:
            partners += [self.peer(self.last_hi, self.x), self.peer(self.last_hi, 1 - self.x)]
        for partner in partners:
            pl.semaphore_signal(sem, inc=1, device_id=partner, device_id_type=pl.DeviceIdType.MESH)
        pl.semaphore_wait(sem, len(partners))

    def remote(self, src, dst, device):
        k = self.count
        self.count += 1
        copy = pltpu.make_async_remote_copy(
            src_ref=src,
            dst_ref=dst,
            send_sem=self.send_sems.at[k],
            recv_sem=self.recv_sems.at[k],
            device_id=device,
            device_id_type=pl.DeviceIdType.MESH,
        )
        copy.start()
        self.sends.append(copy)
        return copy

    def to_sib(self, src, dst):
        return self.remote(src, dst, self.mate(self.sib))

    def to_z(self, src, dst):
        return self.remote(src, dst, self.mate(self.zn))

    def to_y(self, src, dst):
        return self.remote(src, dst, {"fsdp": self.f, "tp": self.yn})

    def to_x(self, src, dst):
        return self.remote(src, dst, self.peer(self.hi, 1 - self.x))

    def to_half(self, src, dst):
        return self.remote(src, dst, self.peer(self.next_hi, self.x))

    def local(self, src, dst):
        k = self.local_count
        self.local_count += 1
        copy = pltpu.make_async_copy(src, dst, self.local_sems.at[k])
        copy.start()
        return copy


    def rows(self, hi, z, x):
        size = 2 * self.cfg["DB"]
        return pl.ds(pl.multiple_of(((hi * 2 + z) * 2 + x) * size, 16), size)

    def share(self, ref, s):
        db = self.cfg["DB"]
        return ref.at[pl.ds(pl.multiple_of(self.index(self.hi, s, self.x) * db, 16), db), :]

    def columns_out(self, shares, full):
        if self.cfg["whole"]:
            return self.local(shares, full).wait
        mine = self.share(full, self.s)
        copies = [self.remote(shares.at[s], mine, self.mate(s)) for s in (self.zn, self.diag, self.sib)]
        own = self.local(shares.at[self.s], mine)

        def wait():
            for c in copies:
                c.wait_recv()
            own.wait()

        return wait

    def columns_back(self, full, result):
        if self.cfg["whole"]:
            return self.local(full, result).wait
        copies = [
            self.remote(self.share(full, s), result.at[self.s], self.mate(s)) for s in (self.zn, self.diag, self.sib)
        ]
        own = self.local(self.share(full, self.s), result.at[self.s])

        def wait():
            for c in copies:
                c.wait_recv()
            own.wait()

        return wait

    def spread(self, full):
        if self.cfg["whole"]:
            return None
        parts = [full.at[self.rows(self.hi, z, self.x), :] for z in range(2)]
        far = [self.to_half(part, part) for part in parts]
        near = [self.to_x(part, part) for part in parts]
        self.gathered += far + near
        return {"full": full, "far": far, "near": near}

    def spread_on(self, g):
        if g is None:
            return
        for z, c in enumerate(g["far"]):
            c.wait_recv()
            part = g["full"].at[self.rows(self.next_hi, z, self.x), :]
            onward = self.to_x(part, part)
            g["near"].append(onward)
            self.gathered.append(onward)

    def spread_done(self, g):
        if g is not None:
            for c in g["near"]:
                c.wait_recv()

    def add_rows(self, grad, rows, parts):
        size, tile = 2 * self.cfg["DB"], 2 * self.cfg["DB"]
        tile = next(t for t in (112, 32, 16) if size % t == 0)
        for i in range(size // tile):
            place = pl.ds(pl.multiple_of(rows.start + i * tile, 16), tile)
            total = grad[place, :].astype(F32)
            for part in parts:
                total = total + part[i * tile : (i + 1) * tile, :].astype(F32)
            grad[place, :] = total.astype(BF)

    def collect(self, grad, slots):
        if self.cfg["whole"]:
            return None
        near = []
        for k, hi in enumerate((self.next_hi, self.hi)):
            for z in range(2):
                near.append(self.to_x(grad.at[self.rows(hi, z, 1 - self.x), :], slots.at[2 * k + z]))
        return {"grad": grad, "slots": slots, "near": near}

    def collect_on(self, g):
        if g is None:
            return
        g["far"] = []
        for z in range(2):
            g["near"][z].wait_recv()
            rows = self.rows(self.next_hi, z, self.x)
            self.add_rows(g["grad"], rows, [g["slots"].at[z]])
            g["far"].append(self.to_half(g["grad"].at[rows, :], g["slots"].at[4 + z]))

    def collect_done(self, g):
        if g is None:
            return
        for z in range(2):
            g["near"][2 + z].wait_recv()
            g["far"][z].wait_recv()
            rows = self.rows(self.hi, z, self.x)
            self.add_rows(g["grad"], rows, [g["slots"].at[2 + z], g["slots"].at[4 + z]])


    def rim_out(self, ends, slots):
        after = self.peer((self.hi + self.x) % self.cfg["NH"], 1 - self.x)
        return [self.to_x(ends[0], slots(self.x)), self.remote(ends[1], slots(1 - self.x), after)]

    def rim_home(self, slots, ends):
        before = self.peer((self.hi + self.cfg["NH"] - 1 + self.x) % self.cfg["NH"], 1 - self.x)
        return [self.to_x(slots(1 - self.x), ends[0]), self.remote(slots(self.x), ends[1], before)]


    def gather_start(self, buf):
        own = buf.at[self.s, self.y]
        return {"x": self.to_z(own, own), "y": self.to_y(own, own), "own": self.to_sib(own, own), "buf": buf}

    def gather_relay(self, g):
        buf, cut = g["buf"], self.cfg["cut"]
        g["x"].wait_recv()
        part = buf.at[self.zn, self.y, :, slice(0, cut)]
        g["d0"] = self.to_y(part, part)
        whole = buf.at[self.zn, self.y]
        g["fx"] = self.to_sib(whole, whole)
        g["y"].wait_recv()
        part = buf.at[self.s, self.yn, :, slice(cut, self.cfg["D"])]
        g["d1"] = self.to_z(part, part)
        whole = buf.at[self.s, self.yn]
        g["fy"] = self.to_sib(whole, whole)

    def gather_finish(self, g):
        buf, cut = g["buf"], self.cfg["cut"]
        g["d0"].wait_recv()
        part = buf.at[self.zn, self.yn, :, slice(0, cut)]
        f0 = self.to_sib(part, part)
        g["d1"].wait_recv()
        part = buf.at[self.zn, self.yn, :, slice(cut, self.cfg["D"])]
        f1 = self.to_sib(part, part)
        for c in (g["own"], g["fx"], g["fy"], f0, f1):
            c.wait_recv()
        g["copies"] = [g[n] for n in ("own", "x", "y", "d0", "d1", "fx", "fy")] + [f0, f1]

    def scatter_pair(self, st, partial):
        sc, rc = st["sc"], st["rc"]
        copies = []
        for k, pair in enumerate(((self.sib + 2) % SUB, self.sib)):
            sc[k] = partial(pair).astype(BF).reshape(sc.shape[1:])
            copies.append(self.to_sib(sc.at[k], rc.at[k]))
        return {"pair": copies, "st": st}

    def scatter_send(self, g, partial):
        st, cut, d = g["st"], self.cfg["cut"], self.cfg["D"]
        so, rc = st["so"], st["rc"]
        lo, hi = slice(0, cut), slice(cut, d)
        value = partial(self.zn)
        g["pair"][0].wait_recv()
        so[0] = (value + flat(rc[0].astype(F32))).astype(BF).reshape(so.shape[1:])
        g["d0"] = self.to_z(so.at[0, self.yn, :, lo], st["rd0"])
        g["d1"] = self.to_y(so.at[0, self.yn, :, hi], st["rd1"])
        g["x0"] = self.to_z(so.at[0, self.y, :, lo], st["rx"].at[:, lo])
        value = partial(self.s)
        g["pair"][1].wait_recv()
        so[1] = (value + flat(rc[1].astype(F32))).astype(BF).reshape(so.shape[1:])
        g["y1"] = self.to_y(so.at[1, self.yn, :, hi], st["ry"].at[:, hi])

    def scatter_relay(self, g):
        st, cut, d = g["st"], self.cfg["cut"], self.cfg["D"]
        so = st["so"]
        lo, hi = slice(0, cut), slice(cut, d)
        g["d1"].wait_recv()
        so[0, self.y, :, hi] = (so[0, self.y, :, hi].astype(F32) + st["rd1"][...].astype(F32)).astype(BF)
        g["x1"] = self.to_z(so.at[0, self.y, :, hi], st["rx"].at[:, hi])
        g["d0"].wait_recv()
        so[1, self.yn, :, lo] = (so[1, self.yn, :, lo].astype(F32) + st["rd0"][...].astype(F32)).astype(BF)
        g["y0"] = self.to_y(so.at[1, self.yn, :, lo], st["ry"].at[:, lo])

    def scatter_finish(self, g):
        st = g["st"]
        for name in ("x0", "x1", "y0", "y1"):
            g[name].wait_recv()
        total = st["so"][1, self.y].astype(F32) + st["rx"][...].astype(F32) + st["ry"][...].astype(F32)
        self.settle(g["pair"] + [g[n] for n in ("d0", "d1", "x0", "x1", "y0", "y1")])
        return total


    def place(self, s):
        return 1 + 2 * s + s // 2

    def project(self, w):
        def step(i, _):
            rows = flat(self.u1[i])
            out = dot(rows, w[...], NN).astype(BF)
            self.qkv[pl.ds(self.place(i), 2)] = out.reshape(2, 2 * WINDOW, out.shape[1])
            return 0

        lax.fori_loop(0, SUB, step, 0)

    def masks(self, s):
        at = 1 + s + s // 2
        before, own = self.starts[at - 1], self.starts[at]
        lane = lax.broadcasted_iota(jnp.int32, before.shape, 1)
        even = jnp.where(lane < WINDOW, pltpu.roll(before, WINDOW, 1), pltpu.roll(own, WINDOW, 1))
        shape = (WINDOW, 2 * WINDOW)
        i = lax.broadcasted_iota(jnp.int32, shape, 0)
        j = lax.broadcasted_iota(jnp.int32, shape, 1)
        square = (2 * WINDOW, 2 * WINDOW)
        later = lax.broadcasted_iota(jnp.int32, square, 0) > lax.broadcasted_iota(jnp.int32, square, 1)
        later = later.astype(F32).astype(BF)
        band = (j <= i + WINDOW) & (j > i)
        result = []
        for rows in (even, own):
            per_batch = []
            for batch in range(2):
                line = jnp.broadcast_to(rows[batch : batch + 1, :], shape)
                line = jnp.where(j <= i + WINDOW, line, 0.0).astype(BF)
                between = dot(line, later, NN)
                per_batch.append(band & (between < 0.5))
            result.append(per_batch)
        return result

    def tile(self, index, batch, part, head):
        cols = slice(part * 2 * HP + head * HP, part * 2 * HP + (head + 1) * HP)
        return self.qkv[index, batch * WINDOW : (batch + 1) * WINDOW, cols]

    def attend(self):
        def step(n, _):
            s = SUB - 1 - n
            allowed = self.masks(s)
            for half in range(2):
                p = self.place(s) + half
                for batch in range(2):
                    for head in range(2):
                        q = self.tile(p, batch, 0, head)
                        k = jnp.concatenate([self.tile(p - 1, batch, 1, head), self.tile(p, batch, 1, head)], axis=0)
                        v = jnp.concatenate([self.tile(p - 1, batch, 2, head), self.tile(p, batch, 2, head)], axis=0)
                        scores = dot(q, k, NT) * DH ** (-0.5)
                        scores = jnp.where(allowed[half][batch], scores, -1e30)
                        top = jnp.max(scores, axis=-1, keepdims=True)
                        weights = jnp.exp(scores - top)
                        probs = weights / jnp.sum(weights, axis=-1, keepdims=True)
                        self.probs[2 * s + half, 2 * batch + head] = probs
                        out = dot(probs.astype(BF), v, NN).astype(BF)
                        self.heads[s, half, batch * WINDOW : (batch + 1) * WINDOW, head * HP : (head + 1) * HP] = out
            return 0

        lax.fori_loop(0, SUB, step, 0)

    def attend_back(self, s):
        run = s // 2
        for half in range(2):
            p = self.place(s) + half
            for batch in range(2):
                rows = slice(batch * WINDOW, (batch + 1) * WINDOW)
                for head in range(2):
                    cols = slice(head * HP, (head + 1) * HP)
                    q = self.tile(p, batch, 0, head)
                    k = jnp.concatenate([self.tile(p - 1, batch, 1, head), self.tile(p, batch, 1, head)], axis=0)
                    v = jnp.concatenate([self.tile(p - 1, batch, 2, head), self.tile(p, batch, 2, head)], axis=0)
                    probs = self.probs[2 * s + half, 2 * batch + head]
                    d_out = self.d_heads[s, half, rows, cols]
                    d_probs = dot(d_out, v, NT)
                    inner = jnp.sum(probs * d_probs, axis=-1, keepdims=True)
                    d_scores = (probs * (d_probs - inner)).astype(BF)
                    d_q = dot(d_scores, k, NN) * DH ** (-0.5)
                    d_k = dot(d_scores, q, TN) * DH ** (-0.5)
                    d_v = dot(probs.astype(BF), d_out, TN)
                    self.qkv[p, rows, head * HP : (head + 1) * HP] = d_q.astype(BF)
                    for part, grad in ((1, d_k), (2, d_v)):
                        slot = slice((part - 1) * 2 * HP + head * HP, (part - 1) * 2 * HP + (head + 1) * HP)
                        place = slice(part * 2 * HP + head * HP, part * 2 * HP + (head + 1) * HP)
                        done = self.carry[run, rows, slot] + grad[:WINDOW]
                        self.qkv[p - 1, rows, place] = done.astype(BF)
                        self.carry[run, rows, slot] = grad[WINDOW:]

    def grad_into(self, target, left, right):
        width = 256

        def step(m, _):
            cols = pl.ds(pl.multiple_of(m * width, width), width)
            parts = right()
            each = SUB // len(parts)
            total = 0.0
            for k, part in enumerate(parts):
                total = total + dot(flat(left[k * each : (k + 1) * each, :, :, cols]), part, TN)
            target[cols, :] = total.astype(BF)
            return 0

        lax.fori_loop(0, self.cfg["D"] // width, step, 0)

    def feed_forward(self):
        ff = self.w_dn.shape[1]

        def step(i, _):
            rows = flat(self.u2[i])
            gate = dot(rows, self.w_ga[...], NN)
            upward = dot(rows, self.w_up[...], NN)
            d_hidden = dot(flat(self.g[i]), self.w_dn[...], NN)
            sig = jax.nn.sigmoid(gate)
            silu = gate * sig
            shape = (2, 2 * WINDOW, ff)
            self.hidden[i] = (silu * upward).astype(BF).reshape(shape)
            d_gate = d_hidden * upward * sig * (1.0 + gate * (1.0 - sig))
            self.d_ga[i] = d_gate.astype(BF).reshape(shape)
            self.d_up[i] = (d_hidden * silu).astype(BF).reshape(shape)
            return 0

        lax.fori_loop(0, SUB, step, 0)

    def run(self):
        cfg = self.cfg
        me = (self.s, self.y)
        norm = lambda v: lax.rsqrt(jnp.mean(v * v, axis=-1, keepdims=True) + EPSILON)
        whole = lambda ref: [flat(ref[...])]

        self.barrier()
        qkv_here = self.columns_out(self.sh_qkv, self.w_qkv)
        line = 1 + self.s + self.s // 2
        start_copies = [
            self.remote(self.starts_in, self.starts.at[line], self.mate(s)) for s in (self.sib, self.zn, self.diag)
        ]
        self.starts[line] = self.starts_in[...]

        x = self.x_in[...].astype(F32)
        self.u1[me] = (x * norm(x)).astype(BF)
        gather_one = self.gather_start(self.u1)
        out_here = self.columns_out(self.sh_out, self.w_out)
        qkv_here()
        go_qkv = self.spread(self.w_qkv)
        ga_here = self.columns_out(self.sh_ga, self.w_ga)
        for c in start_copies:
            c.wait_recv()
        rim_starts = self.rim_out([self.starts.at[2], self.starts.at[5]], lambda run: self.starts.at[3 * run])
        self.gather_relay(gather_one)
        out_here()
        go_out = self.spread(self.w_out)
        self.g[me] = self.g_in[...]
        self.gather_finish(gather_one)
        self.spread_on(go_qkv)
        up_here = self.columns_out(self.sh_up, self.w_up)
        gather_g = self.gather_start(self.g)
        dn_here = self.columns_out(self.sh_dn, self.w_dn)
        self.spread_done(go_qkv)

        self.project(self.w_qkv)
        rims = self.rim_out(
            [self.qkv.at[4, :, slice(2 * HP, 6 * HP)], self.qkv.at[9, :, slice(2 * HP, 6 * HP)]],
            lambda run: self.qkv.at[5 * run, :, slice(2 * HP, 6 * HP)],
        )
        self.spread_on(go_out)
        ga_here()
        go_ga = self.spread(self.w_ga)
        self.gather_relay(gather_g)
        for c in rim_starts + rims:
            c.wait_recv()
        self.attend()
        self.gather_finish(gather_g)
        self.spread_done(go_out)

        partial = lambda pair: dot(flat(self.heads[pair]), self.w_out[...], NT)
        stage = {n: getattr(self, n) for n in ("sc", "rc", "so", "rd0", "rd1", "rx", "ry")}
        scatter = self.scatter_pair(stage, partial)
        self.scatter_send(scatter, partial)
        self.scatter_relay(scatter)
        up_here()
        go_up = self.spread(self.w_up)
        self.spread_on(go_ga)
        self.resid[...] = self.x_in[...].astype(F32) + self.scatter_finish(scatter)
        resid = self.resid[...]
        self.u2[me] = (resid * norm(resid)).astype(BF)
        gather_two = self.gather_start(self.u2)
        dn_here()
        go_dn = self.spread(self.w_dn)
        self.gather_relay(gather_two)
        self.spread_on(go_up)
        self.gather_finish(gather_two)
        self.spread_on(go_dn)
        for go in (go_ga, go_up, go_dn):
            self.spread_done(go)

        self.feed_forward()
        partial = lambda pair: dot(flat(self.d_ga[pair]), self.w_ga[...], NT) + dot(
            flat(self.d_up[pair]), self.w_up[...], NT
        )
        scatter = self.scatter_pair(stage, partial)
        self.scatter_send(scatter, partial)
        self.grad_into(self.g_dn, self.g, lambda: whole(self.hidden))
        sum_dn = self.collect(self.g_dn, self.slots_dn)
        self.scatter_relay(scatter)
        self.settle(self.gathered)
        self.grad_into(self.w_ga, self.u2, lambda: whole(self.d_ga))
        sum_ga = self.collect(self.w_ga, self.slots_ga)
        self.grad_into(self.w_up, self.u2, lambda: whole(self.d_up))
        sum_up = self.collect(self.w_up, self.slots_up)
        d_unit = self.scatter_finish(scatter)
        resid = self.resid[...]
        scale = norm(resid)
        unit = resid * scale
        inner = jnp.mean(d_unit * unit, axis=-1, keepdims=True)
        self.d_resid[...] = self.g_in[...].astype(F32) + scale * (d_unit - unit * inner)
        self.d_r[me] = self.d_resid[...].astype(BF)
        self.settle(gather_g["copies"] + gather_two["copies"] + rims)
        gather_d = self.gather_start(self.d_r)
        self.collect_on(sum_dn)
        self.gather_relay(gather_d)
        self.gather_finish(gather_d)

        def heads_back(i, _):
            value = dot(flat(self.d_r[i]), self.w_out[...], NN).astype(BF)
            self.d_heads[i] = value.reshape(2, 2 * WINDOW, 2 * HP)
            return 0

        lax.fori_loop(0, SUB, heads_back, 0)

        view = {
            "sc": self.u2.at[0:2],
            "so": self.u2.at[2:4],
            "rc": self.g.at[0:2],
            "rd0": self.g.at[2, 0, :, slice(0, cfg["cut"])],
            "rd1": self.g.at[2, 0, :, slice(cfg["cut"], cfg["D"])],
            "rx": self.g.at[2, 1],
            "ry": self.g.at[3, 0],
        }
        partial = lambda pair: dot(flat(self.hidden[pair]), self.w_dn[...], NT)
        mlp = self.scatter_pair(view, partial)
        self.scatter_send(mlp, partial)
        self.collect_on(sum_ga)

        self.carry[...] = jnp.zeros_like(self.carry)

        def first(run, _):
            self.attend_back(2 * run)
            return 0

        def second(run, _):
            self.attend_back(2 * run + 1)
            return 0

        lax.fori_loop(0, 2, first, 0)
        rim_back = self.rim_home(
            lambda run: self.qkv.at[5 * run, :, slice(2 * HP, 6 * HP)], [self.rim.at[0], self.rim.at[1]]
        )
        self.scatter_relay(mlp)
        lax.fori_loop(0, 2, second, 0)
        self.collect_on(sum_up)
        for c in rim_back:
            c.wait_recv()
        for run in range(2):
            done = self.carry[run] + self.rim[run].astype(F32)
            self.qkv[5 * run + 4, :, 2 * HP :] = done.astype(BF)

        self.grad_into(self.g_qkv, self.u1, lambda: [flat(self.qkv[1:5]), flat(self.qkv[6:10])])
        sum_qkv = self.collect(self.g_qkv, self.slots_qkv)
        partial = lambda pair: dot(flat(self.qkv[pl.ds(self.place(pair), 2)]), self.w_qkv[...], NT)
        scatter = self.scatter_pair(stage, partial)
        self.scatter_send(scatter, partial)
        self.grad_into(self.w_out, self.d_r, lambda: whole(self.heads))
        sum_out = self.collect(self.w_out, self.slots_out)
        self.scatter_relay(scatter)
        self.out[...] = (self.resid[...] + self.scatter_finish(mlp)).astype(BF)
        self.collect_done(sum_dn)
        dn_back = self.columns_back(self.g_dn, self.o_dn)
        self.collect_done(sum_ga)
        ga_back = self.columns_back(self.w_ga, self.o_ga)
        d_unit = self.scatter_finish(scatter)
        x = self.x_in[...].astype(F32)
        scale = norm(x)
        unit = x * scale
        inner = jnp.mean(d_unit * unit, axis=-1, keepdims=True)
        self.in_grad[...] = self.d_resid[...] + scale * (d_unit - unit * inner)
        self.collect_on(sum_qkv)
        self.collect_on(sum_out)
        self.collect_done(sum_up)
        up_back = self.columns_back(self.w_up, self.o_up)
        self.collect_done(sum_qkv)
        qkv_back = self.columns_back(self.g_qkv, self.o_qkv)
        self.collect_done(sum_out)
        out_back = self.columns_back(self.w_out, self.o_out)
        for wait in (dn_back, ga_back, up_back, qkv_back, out_back):
            wait()
        self.settle()

    def settle(self, copies=None):
        for c in self.sends:
            if copies is None or any(c is other for other in copies):
                c.wait_send()
        if copies is None:
            self.sends = []
        else:
            self.sends = [c for c in self.sends if not any(c is other for other in copies)]


def fused(cfg, shares, starts, x, g):
    d, db = cfg["D"], cfg["DB"]
    rows = 2 * WINDOW
    cut = cfg["cut"]
    anywhere = pl.BlockSpec(memory_space=pl.ANY)
    vmem = pl.BlockSpec(memory_space=pltpu.VMEM)
    keys = ("qkv", "out", "ga", "up", "dn")
    width = {key: share.shape[-1] for key, share in zip(keys, shares, strict=True)}
    result = (d,) if cfg["whole"] else (SUB, db)
    outs = [("out", (rows, d), BF, vmem), ("in_grad", (rows, d), F32, vmem)]
    outs += [("o_" + key, result + (width[key],), BF, anywhere) for key in keys]
    ins = [("sh_" + key, anywhere) for key in keys] + [("starts_in", vmem), ("x_in", vmem), ("g_in", vmem)]
    plane = (SUB, 2, rows)
    scratch = [("w_" + key, (d, width[key]), BF) for key in keys]
    scratch += [("g_" + key, (d, width[key]), BF) for key in ("qkv", "dn")]
    slot = 16 if cfg["whole"] else 2 * db
    scratch += [("slots_" + key, (6, slot, width[key]), BF) for key in keys]
    scratch += [(name, plane + (d,), BF) for name in ("u1", "u2", "g", "d_r")]
    scratch += [(name, plane + (width["out"],), BF) for name in ("heads", "d_heads")]
    scratch += [(name, plane + (width["dn"],), BF) for name in ("hidden", "d_ga", "d_up")]
    scratch += [(name, (2, 2, rows, d), BF) for name in ("sc", "rc", "so")]
    scratch += [
        ("starts", (SUB + 2, 8, rows), F32),
        ("qkv", (2 * SUB + 2, rows, width["qkv"]), BF),
        ("probs", (2 * SUB, 4, WINDOW, 2 * WINDOW), F32),
        ("carry", (2, rows, 4 * HP), F32),
        ("rim", (2, rows, 4 * HP), BF),
        ("resid", (rows, d), F32),
        ("d_resid", (rows, d), F32),
        ("rd0", (rows, cut), BF),
        ("rd1", (rows, d - cut), BF),
        ("rx", (rows, d), BF),
        ("ry", (rows, d), BF),
    ]
    number = 190
    names = [n for n, _ in ins] + [n for n, *_ in outs] + [n for n, *_ in scratch]
    names += ["send_sems", "recv_sems", "local_sems"]

    def kernel(*refs):
        Kernel(cfg, dict(zip(names, refs, strict=True))).run()

    return pl.pallas_call(
        kernel,
        out_shape=[jax.ShapeDtypeStruct(shape, kind) for _, shape, kind, _ in outs],
        in_specs=[spec for _, spec in ins],
        out_specs=[spec for *_, spec in outs],
        scratch_shapes=[pltpu.VMEM(shape, kind) for _, shape, kind in scratch]
        + [
            pltpu.SemaphoreType.DMA((number,)),
            pltpu.SemaphoreType.DMA((number,)),
            pltpu.SemaphoreType.DMA((10,)),
        ],
        compiler_params=pltpu.CompilerParams(
            collective_id=0, has_side_effects=True, vmem_limit_bytes=63 * 2**20
        ),
    )(*shares, starts, x, g)


def padded(value, size):
    pads = [(0, 0)] * (value.ndim - 1) + [(0, size - value.shape[-1])]
    return jnp.pad(value, pads)


def body(size, tokens, doc_starts, w_qkv, w_out, w_gate_up, w_down, gains, cotangent):
    batches, rows, d = tokens.shape
    db = w_qkv.shape[1]
    ff = w_gate_up.shape[2] // SUB
    ffp = -(-ff // HP) * HP
    heads = w_qkv.shape[2] // (SUB * DH)
    gain = gains.astype(F32)
    whole = size != 16 or db % 16 != 0
    cfg = {"D": d, "NH": size // 8, "DB": db, "cut": d // 256 * 128, "whole": whole}

    sh_qkv = (w_qkv.astype(F32) * gain[0][None, :, None]).astype(BF).reshape(3, db, SUB, heads, DH)
    sh_qkv = padded(sh_qkv, HP).transpose(2, 1, 0, 3, 4).reshape(SUB, db, 3 * heads * HP)
    sh_out = w_out.T.reshape(db, SUB, heads, DH)
    sh_out = padded(sh_out, HP).transpose(1, 0, 2, 3).reshape(SUB, db, heads * HP)
    scaled = (w_gate_up.astype(F32) * gain[1][None, :, None]).astype(BF).reshape(2, db, SUB, ff)
    sh_ga, sh_up = [padded(scaled[k], ffp).transpose(1, 0, 2) for k in range(2)]
    sh_dn = padded(w_down.T.reshape(db, SUB, ff), ffp).transpose(1, 0, 2)
    shares = [sh_qkv, sh_out, sh_ga, sh_up, sh_dn]

    if whole:
        f = lax.axis_index("fsdp")
        s = (f // 4) % 2 * 2 + f % 2
        everyone = [lax.all_gather(v, "fsdp", axis=1, tiled=True) for v in shares]
        shares = [lax.dynamic_index_in_dim(v, s, 0, keepdims=False) for v in everyone]
    starts = jnp.pad(doc_starts.astype(F32), ((0, 8 - batches), (0, 0)))
    out, in_grad, *grads = fused(
        cfg, shares, starts, tokens.reshape(batches * rows, d), cotangent.reshape(batches * rows, d)
    )
    if whole:
        mine = (jnp.arange(SUB) == s)[:, None, None]
        grads = [
            lax.psum_scatter(jnp.where(mine, v[None], 0).astype(BF), "fsdp", scatter_dimension=1, tiled=True)
            for v in grads
        ]
    g_qkv, g_out, g_ga, g_up, g_dn = [v.astype(F32) for v in grads]
    g_qkv = g_qkv.reshape(SUB, db, 3, heads, HP)[..., :DH].transpose(2, 1, 0, 3, 4).reshape(w_qkv.shape)
    g_out = g_out.reshape(SUB, db, heads, HP)[..., :DH].transpose(0, 2, 3, 1).reshape(w_out.shape)
    g_gu = jnp.stack([v[..., :ff].transpose(1, 0, 2).reshape(w_gate_up.shape[1:]) for v in (g_ga, g_up)])
    g_dn = g_dn[..., :ff].transpose(0, 2, 1).reshape(w_down.shape)
    gain_sums = jnp.stack(
        [
            jnp.sum(g_qkv * w_qkv.astype(F32), axis=(0, 2)),
            jnp.sum(g_gu * w_gate_up.astype(F32), axis=(0, 2)),
        ]
    )
    gain_sums = gain_sums + lax.ppermute(gain_sums, "tp", [(0, 1), (1, 0)])
    return (
        out.reshape(tokens.shape),
        in_grad.reshape(tokens.shape),
        g_qkv * gain[0][None, :, None],
        g_out,
        g_gu * gain[1][None, :, None],
        g_dn,
        gain_sums,
    )


def solution(mesh):
    in_specs = (
        P(None, ("fsdp", "tp"), None),
        P(None, "fsdp"),
        P(None, "fsdp", "tp"),
        P("tp", "fsdp"),
        P(None, "fsdp", "tp"),
        P("tp", "fsdp"),
        P(None, "fsdp"),
        P(None, ("fsdp", "tp"), None),
    )
    out_specs = (
        P(None, ("fsdp", "tp"), None),
        P(None, ("fsdp", "tp"), None),
        P(None, "fsdp", "tp"),
        P("tp", "fsdp"),
        P(None, "fsdp", "tp"),
        P("tp", "fsdp"),
        P(None, "fsdp"),
    )
    return jax.shard_map(
        functools.partial(body, mesh.shape["fsdp"]), mesh=mesh, in_specs=in_specs, out_specs=out_specs, check_vma=False
    )
```

time: 475 us -> 408 us (0.86)
  Pallas kernels: 429 us -> 370 us
    pallas_call x1, Pallas kernels: 429 us -> 370 us  [fused(): pl.pallas_call(kernel, out_shape=[jax.ShapeDtypeStruct(shape, kind) for _...]
    reshape x6 -> x0, local copies, waits for them, and re-layouts: 10.7 us -> none  [the longest x3 6.64 us: body(): g_gu.reshape(SUB, db, 2, ffp)[..., :ff].transpose(2, 1, 0, 3)]
where the time goes in v2:
time: 408 us; the launch traced here: 402 us
  Pallas kernels  370 us (91%)
  local copies, waits for them, and re-layouts  22.6 us (6%)
  other arithmetic  7.43 us (2%)
    pallas_call x1, Pallas kernels, fused(): pl.pallas_call(kernel, out_shape=[jax.ShapeDtypeStruct(shape, kind) for _...  370 us
  transfers between devices with their start and end apart: 1, of which 0 were waited for; matrix products, arithmetic and copies ran while one was open for 1% of the time, Pallas kernels for 0%

profile of v2, /device:TPU:0, one launch (start us, length us, event | category | flops | bytes accessed | tf_op | source)
XLA Modules:
  0.0 402.4 jit_solution(1513173551343502806)
XLA Ops:
  0.6 0.0 copy-start.8
  0.6 0.7 convert_element_type.40
  1.4 0.7 convert_element_type.36
  2.0 1.2 reshape.76
  3.3 0.2 pad_bitcast_fusion.4
  3.5 0.8 reshape.77.refs_1_
  4.3 0.0 copy-done.8
  4.3 0.6 reshape.78
  5.0 0.0 copy-start.2
  5.0 0.1 copy.23
  5.1 0.9 pad_bitcast_fusion.1.refs_4_
  5.9 0.2 copy-done.2
  6.1 0.2 fusion.2
  6.3 0.8 reshape.74
  7.1 0.0 copy-start
  7.1 0.7 pad_bitcast_fusion
  7.8 1.2 reshape.75.refs_0_
  9.0 0.0 copy-done
  9.0 0.3 fusion
  9.3 0.1 fusion.5
  9.3 0.6 squeeze.7
  10.0 0.1 copy.22
  10.1 0.9 pad_bitcast_fusion.2.refs_3_
  10.9 0.6 squeeze.6
  11.5 0.1 copy.21
  11.6 0.9 pad_bitcast_fusion.3.refs_2_
  12.5 0.6 pad.27.refs_5_
  13.1 370.0 %shard_map.135 = (bf16[128,1792]{1,0:T(8,128)(2,1)}, f32[128,1792]{1,0:T(8,128)}, bf16[4,112,768]{2,1,0:T(8,128)(2,1)}, bf16[4,112,256]{2,1,0:T(8,128)(2,1)}, bf...) custom-call(bf16[4,112,768]{2,1,0:T(8,128)(2,1)} %reshape.75.refs_0_, ...), custom_call_target="tpu_custom_call" | custom-call | tf_op jit(solution)/shard_map/pallas_call | solution.py:637
  383.1 1.1 slice_bitcast_fusion.1
  384.2 0.0 copy-start.5
  384.2 0.2 copy.26
  384.4 1.2 stack_reshape.8
  385.6 0.0 copy-done.5
  385.6 0.2 reshape.83
  385.8 0.5 convert_bitcast_fusion
  386.3 0.5 copy.24
  386.8 2.0 reshape.92
  388.8 1.3 fusion.3
  390.2 0.0 copy-done.6
  390.2 0.2 copy-done.7
  390.3 0.1 convert_bitcast_fusion.1
  390.5 0.0 copy-start.1
  390.5 0.0 copy-start.3
  390.5 0.2 copy.27
  390.7 1.2 stack_reshape.9
  391.9 0.0 copy-done.1
  391.9 0.0 copy-done.3
  391.9 2.9 fusion.1
  394.9 1.1 collective-permute-start
  396.0 0.0 copy-done.10
  396.0 0.1 reshape.86
  396.0 0.2 convert_bitcast_fusion.2
  396.2 0.2 copy.25
  396.4 1.3 reshape.94
  397.7 0.4 copy.28
  398.1 0.0 copy-start.9
  398.1 0.0 copy-start.4
  398.1 1.6 reshape.96
  399.7 0.0 collective-permute-done
  399.7 0.6 fusion.4
  400.3 0.0 copy-done.9
  400.3 0.8 copy.35
  401.1 0.0 copy-done.4
  401.1 0.9 copy.36
  (5 shorter events, 0.0 us)
Async XLA Ops:
  0.6 3.7 copy-start.8
  5.0 1.1 copy-start.2
  7.1 1.9 copy-start
  384.2 1.5 copy-start.5
  388.8 1.3 copy-start.6
  388.8 1.5 copy-start.7
  390.5 1.5 copy-start.1
  390.5 1.5 copy-start.3
  391.9 4.0 %copy-start.10 = (bf16[4,112,256]{2,1,0:T(8,128)(2,1)S(1)}, bf16[4,112,256]{2,1,0:T(8,128)(2,1)}, u32[]{:S(2)}) copy-start(bf16[4,112,256]{2,1,0:T(8,128)(2,1)} %get-tuple-element.17) | copy-start | bytes 688132
  394.9 4.8 %collective-permute-start = (f32[2,112]{1,0:T(2,128)S(1)}, f32[2,112]{1,0:T(2,128)S(1)}, u32[]{:S(2)}, u32[]{:S(2)}) collective-permute-start(f32[2,112]{1,0:T(2,128)S(1)} %pad_maximum_fusion.1), channel_id=1, source_target_pairs={{0,1},{1,0},{2,3},{3,2},{4,5},{5,4},{6,7},{7,6},{8,9},{9,8},{10,11... | collective-permute-start | bytes 2696 | tf_op jit(solution)/shard_map/ppermute | solution.py:704
  398.1 2.2 copy-start.9
  398.1 2.9 copy-start.4

commit v3 on v2

--- a/solution.py
+++ b/solution.py
@@ -27,6 +27,29 @@
     return value.reshape(-1, value.shape[-1])
 
 
+def eye(size):
+    shape = (size, size)
+    return lax.broadcasted_iota(jnp.int32, shape, 0) == lax.broadcasted_iota(jnp.int32, shape, 1)
+
+
+def padded(value, size):
+    extra = size - value.shape[-1]
+    if not extra:
+        return value
+    return jnp.concatenate([value, jnp.zeros(value.shape[:-1] + (extra,), value.dtype)], axis=-1)
+
+
+class Conditional:
+    def __init__(self, copy, sent, received):
+        self.copy, self.sent, self.received = copy, sent, received
+
+    def wait_send(self):
+        pl.when(self.sent)(self.copy.wait_send)
+
+    def wait_recv(self):
+        pl.when(self.received)(self.copy.wait_recv)
+
+
 class Kernel:
     def __init__(self, cfg, refs):
         self.cfg = cfg
@@ -36,6 +59,9 @@
         core = self.f % 2
         self.x = (self.f // 2) % 2
         self.hi = self.f // 8
+        self.z = (self.f // 4) % 2
+        self.is_middle = self.hi + self.z == 1
+        self.is_end = self.hi + self.z != 1
         self.s = (self.f // 4) % 2 * 2 + core
         self.sib = self.s + 1 - 2 * core
         self.zn = (self.s + 2) % SUB
@@ -47,12 +73,18 @@
         self.local_count = 0
         self.sends = []
         self.gathered = []
+        self.given = []
+        middle = cfg["D"] // 256 * 128
+        self.halves = (slice(0, middle), slice(middle, cfg["D"]))
 
     def index(self, hi, s, x):
         return hi * 8 + s // 2 * 4 + x * 2 + s % 2
 
     def mate(self, s):
         return {"fsdp": self.index(self.hi, s, self.x), "tp": self.y}
+
+    def other(self, s):
+        return {"fsdp": self.index(self.next_hi, s, self.x), "tp": self.y}
 
     def peer(self, hi, x):
         return {"fsdp": self.index(hi, self.s, x), "tp": self.y}
@@ -61,14 +93,16 @@
         sem = pltpu.get_barrier_semaphore()
         partners = [self.mate(s) for s in (self.sib, self.zn, self.diag)]
         partners += [{"fsdp": self.f, "tp": self.yn}, self.peer(self.hi, 1 - self.x)]
-        partners += [self.peer(self.next_hi, self.x), self.peer(self.next_hi, 1 - self.x)]
-        if self.cfg["NH"] > 2:
-            partners += [self.peer(self.last_hi, self.x), self.peer(self.last_hi, 1 - self.x)]
+        partners += [self.peer(self.next_hi, 1 - self.x)]
+        if self.cfg["whole"]:
+            partners += [self.peer(self.last_hi, 1 - self.x)]
+        else:
+            partners += [self.other(s) for s in (self.s, self.sib, self.zn, self.diag)]
         for partner in partners:
             pl.semaphore_signal(sem, inc=1, device_id=partner, device_id_type=pl.DeviceIdType.MESH)
         pl.semaphore_wait(sem, len(partners))
 
-    def remote(self, src, dst, device):
+    def remote(self, src, dst, device, sent=None, received=None):
         k = self.count
         self.count += 1
         copy = pltpu.make_async_remote_copy(
@@ -79,7 +113,11 @@
             device_id=device,
             device_id_type=pl.DeviceIdType.MESH,
         )
-        copy.start()
+        if sent is None:
+            copy.start()
+        else:
+            pl.when(sent)(copy.start)
+            copy = Conditional(copy, sent, received)
         self.sends.append(copy)
         return copy
 
@@ -114,19 +152,92 @@
         db = self.cfg["DB"]
         return ref.at[pl.ds(pl.multiple_of(self.index(self.hi, s, self.x) * db, 16), db), :]
 
-    def columns_out(self, shares, full):
+    def columns_out(self, key):
+        full = getattr(self, "w_" + key)
         if self.cfg["whole"]:
-            return self.local(shares, full).wait
+            return {"full": full, "own": self.local(getattr(self, "sh_" + key), full), "here": []}
+        self.prepare(key)
+        shares = functools.partial(self.prepared, key)
         mine = self.share(full, self.s)
-        copies = [self.remote(shares.at[s], mine, self.mate(s)) for s in (self.zn, self.diag, self.sib)]
-        own = self.local(shares.at[self.s], mine)
-
-        def wait():
-            for c in copies:
+        here = [self.remote(shares(s), mine, self.mate(s)) for s in (self.zn, self.diag, self.sib)]
+        self.given += here
+        return {"full": full, "shares": shares, "own": self.local(shares(self.s), mine), "here": here}
+
+    def prepared(self, key, s):
+        db = self.cfg["DB"]
+        rows = pl.ds(pl.multiple_of(s % 2 * db, 16), db)
+        return getattr(self, "slots_" + key).at[s // 2, rows, :]
+
+    def gain_column(self, k):
+        db = self.cfg["DB"]
+        line = jnp.broadcast_to(self.gains[...].astype(F32)[k : k + 1, :], (db, db))
+        return jnp.sum(jnp.where(eye(db), line, 0.0), axis=1, keepdims=True)
+
+    def prepare(self, key):
+        db, ff = self.cfg["DB"], self.cfg["FF"]
+        slots = getattr(self, "slots_" + key)
+        if key in ("qkv", "ga", "up"):
+            gain = self.gain_column(0 if key == "qkv" else 1)
+        for s in range(SUB):
+            if key == "qkv":
+                blocks = [(k, 2 * s + h) for k in range(3) for h in range(2)]
+                parts = [self.raw_qkv[k, :, n * DH : (n + 1) * DH].astype(F32) * gain for k, n in blocks]
+            elif key == "out":
+                parts = [self.raw_out[:, n * DH : (n + 1) * DH].astype(F32) for n in (2 * s, 2 * s + 1)]
+            elif key == "dn":
+                parts = [self.raw_dn[:, s * ff : (s + 1) * ff].astype(F32)]
+            else:
+                parts = [self.raw_gu[int(key == "up"), :, s * ff : (s + 1) * ff].astype(F32) * gain]
+            value = jnp.concatenate([padded(part, -(-part.shape[1] // HP) * HP) for part in parts], axis=1)
+            slots[s // 2, s % 2 * db : (s % 2 + 1) * db, :] = value.astype(BF)
+
+    def columns_far(self, g):
+        if self.cfg["whole"]:
+            return
+        mine = self.share(g["full"], self.s)
+        g["far"], g["middle"] = [], []
+        for s in (self.s, self.sib):
+            g["far"].append(self.remote(g["shares"](s), mine, self.other(s)))
+        for s in (self.zn, self.diag):
+            g["middle"].append(self.remote(g["shares"](s), mine, self.other(s), self.is_middle, self.is_middle))
+        self.given += g["far"] + g["middle"]
+
+    def spread(self, g):
+        for c in g["here"]:
+            c.wait_recv()
+        g["own"].wait()
+        if self.cfg["whole"]:
+            return
+        part = g["full"].at[self.rows(self.hi, 1 - self.z, self.x), :]
+        g["passed"] = self.remote(part, part, self.other(self.s), self.is_middle, self.is_end)
+        parts = [g["full"].at[self.rows(self.hi, z, self.x), :] for z in range(2)]
+        g["near"] = [self.to_x(part, part) for part in parts]
+        self.gathered += [g["passed"]] + g["near"]
+
+    def onward(self, g, z):
+        part = g["full"].at[self.rows(self.next_hi, z, self.x), :]
+        copy = self.to_x(part, part)
+        g["near"].append(copy)
+        self.gathered.append(copy)
+
+    def spread_same(self, g):
+        if self.cfg["whole"]:
+            return
+        for c in g["far"]:
+            c.wait_recv()
+        self.onward(g, self.z)
+
+    def spread_rest(self, g):
+        if self.cfg["whole"]:
+            return
+        for c in g["middle"] + [g["passed"]]:
+            c.wait_recv()
+        self.onward(g, 1 - self.z)
+
+    def spread_done(self, g):
+        if not self.cfg["whole"]:
+            for c in g["near"]:
                 c.wait_recv()
-            own.wait()
-
-        return wait
 
     def columns_back(self, full, result):
         if self.cfg["whole"]:
@@ -142,30 +253,6 @@
             own.wait()
 
         return wait
-
-    def spread(self, full):
-        if self.cfg["whole"]:
-            return None
-        parts = [full.at[self.rows(self.hi, z, self.x), :] for z in range(2)]
-        far = [self.to_half(part, part) for part in parts]
-        near = [self.to_x(part, part) for part in parts]
-        self.gathered += far + near
-        return {"full": full, "far": far, "near": near}
-
-    def spread_on(self, g):
-        if g is None:
-            return
-        for z, c in enumerate(g["far"]):
-            c.wait_recv()
-            part = g["full"].at[self.rows(self.next_hi, z, self.x), :]
-            onward = self.to_x(part, part)
-            g["near"].append(onward)
-            self.gathered.append(onward)
-
-    def spread_done(self, g):
-        if g is not None:
-            for c in g["near"]:
-                c.wait_recv()
 
     def add_rows(self, grad, rows, parts):
         size, tile = 2 * self.cfg["DB"], 2 * self.cfg["DB"]
@@ -217,73 +304,61 @@
 
     def gather_start(self, buf):
         own = buf.at[self.s, self.y]
-        return {"x": self.to_z(own, own), "y": self.to_y(own, own), "own": self.to_sib(own, own), "buf": buf}
+        return {"z": self.to_z(own, own), "y": self.to_y(own, own), "own": self.to_sib(own, own), "buf": buf}
 
     def gather_relay(self, g):
-        buf, cut = g["buf"], self.cfg["cut"]
-        g["x"].wait_recv()
-        part = buf.at[self.zn, self.y, :, slice(0, cut)]
-        g["d0"] = self.to_y(part, part)
-        whole = buf.at[self.zn, self.y]
-        g["fx"] = self.to_sib(whole, whole)
+        buf = g["buf"]
+        g["z"].wait_recv()
+        part = buf.at[self.zn, self.y]
+        g["d"] = self.to_y(part, part)
+        g["fz"] = self.to_sib(part, part)
         g["y"].wait_recv()
-        part = buf.at[self.s, self.yn, :, slice(cut, self.cfg["D"])]
-        g["d1"] = self.to_z(part, part)
-        whole = buf.at[self.s, self.yn]
-        g["fy"] = self.to_sib(whole, whole)
+        part = buf.at[self.s, self.yn]
+        g["fy"] = self.to_sib(part, part)
 
     def gather_finish(self, g):
-        buf, cut = g["buf"], self.cfg["cut"]
-        g["d0"].wait_recv()
-        part = buf.at[self.zn, self.yn, :, slice(0, cut)]
-        f0 = self.to_sib(part, part)
-        g["d1"].wait_recv()
-        part = buf.at[self.zn, self.yn, :, slice(cut, self.cfg["D"])]
-        f1 = self.to_sib(part, part)
-        for c in (g["own"], g["fx"], g["fy"], f0, f1):
-            c.wait_recv()
-        g["copies"] = [g[n] for n in ("own", "x", "y", "d0", "d1", "fx", "fy")] + [f0, f1]
+        g["d"].wait_recv()
+        part = g["buf"].at[self.zn, self.yn]
+        g["fd"] = self.to_sib(part, part)
+        for name in ("own", "fz", "fy", "fd"):
+            g[name].wait_recv()
+        g["copies"] = [g[n] for n in ("own", "z", "y", "d", "fz", "fy", "fd")]
 
     def scatter_pair(self, st, partial):
         sc, rc = st["sc"], st["rc"]
         copies = []
-        for k, pair in enumerate(((self.sib + 2) % SUB, self.sib)):
+        for k, pair in enumerate((self.diag, self.sib)):
             sc[k] = partial(pair).astype(BF).reshape(sc.shape[1:])
             copies.append(self.to_sib(sc.at[k], rc.at[k]))
         return {"pair": copies, "st": st}
 
     def scatter_send(self, g, partial):
-        st, cut, d = g["st"], self.cfg["cut"], self.cfg["D"]
+        st = g["st"]
         so, rc = st["so"], st["rc"]
-        lo, hi = slice(0, cut), slice(cut, d)
         value = partial(self.zn)
         g["pair"][0].wait_recv()
         so[0] = (value + flat(rc[0].astype(F32))).astype(BF).reshape(so.shape[1:])
-        g["d0"] = self.to_z(so.at[0, self.yn, :, lo], st["rd0"])
-        g["d1"] = self.to_y(so.at[0, self.yn, :, hi], st["rd1"])
-        g["x0"] = self.to_z(so.at[0, self.y, :, lo], st["rx"].at[:, lo])
+        g["d"] = [self.to_y(so.at[0, self.yn, :, h], st["rd"].at[:, h]) for h in self.halves]
         value = partial(self.s)
         g["pair"][1].wait_recv()
         so[1] = (value + flat(rc[1].astype(F32))).astype(BF).reshape(so.shape[1:])
-        g["y1"] = self.to_y(so.at[1, self.yn, :, hi], st["ry"].at[:, hi])
+        g["y"] = self.to_y(so.at[1, self.yn], st["ry"])
 
     def scatter_relay(self, g):
-        st, cut, d = g["st"], self.cfg["cut"], self.cfg["D"]
+        st = g["st"]
         so = st["so"]
-        lo, hi = slice(0, cut), slice(cut, d)
-        g["d1"].wait_recv()
-        so[0, self.y, :, hi] = (so[0, self.y, :, hi].astype(F32) + st["rd1"][...].astype(F32)).astype(BF)
-        g["x1"] = self.to_z(so.at[0, self.y, :, hi], st["rx"].at[:, hi])
-        g["d0"].wait_recv()
-        so[1, self.yn, :, lo] = (so[1, self.yn, :, lo].astype(F32) + st["rd0"][...].astype(F32)).astype(BF)
-        g["y0"] = self.to_y(so.at[1, self.yn, :, lo], st["ry"].at[:, lo])
+        g["z"] = []
+        for c, h in zip(g["d"], self.halves, strict=True):
+            c.wait_recv()
+            so[0, self.y, :, h] = (so[0, self.y, :, h].astype(F32) + st["rd"][:, h].astype(F32)).astype(BF)
+            g["z"].append(self.to_z(so.at[0, self.y, :, h], st["rz"].at[:, h]))
 
     def scatter_finish(self, g):
         st = g["st"]
-        for name in ("x0", "x1", "y0", "y1"):
-            g[name].wait_recv()
-        total = st["so"][1, self.y].astype(F32) + st["rx"][...].astype(F32) + st["ry"][...].astype(F32)
-        self.settle(g["pair"] + [g[n] for n in ("d0", "d1", "x0", "x1", "y0", "y1")])
+        for c in g["z"] + [g["y"]]:
+            c.wait_recv()
+        total = st["so"][1, self.y].astype(F32) + st["rz"][...].astype(F32) + st["ry"][...].astype(F32)
+        self.settle(g["pair"] + g["d"] + g["z"] + [g["y"]])
         return total
 
 
@@ -417,82 +492,89 @@
         whole = lambda ref: [flat(ref[...])]
 
         self.barrier()
-        qkv_here = self.columns_out(self.sh_qkv, self.w_qkv)
         line = 1 + self.s + self.s // 2
-        start_copies = [
-            self.remote(self.starts_in, self.starts.at[line], self.mate(s)) for s in (self.sib, self.zn, self.diag)
-        ]
-        self.starts[line] = self.starts_in[...]
-
+        own_starts = self.doc_starts[...].astype(F32)
+        fill = jnp.zeros((self.starts.shape[1] - own_starts.shape[0], own_starts.shape[1]), F32)
+        self.starts[line] = jnp.concatenate([own_starts, fill], axis=0)
+        own_line = self.starts.at[line]
+        start_copies = [self.remote(own_line, own_line, self.mate(s)) for s in (self.sib, self.zn, self.diag)]
+        qkv = self.columns_out("qkv")
         x = self.x_in[...].astype(F32)
         self.u1[me] = (x * norm(x)).astype(BF)
         gather_one = self.gather_start(self.u1)
-        out_here = self.columns_out(self.sh_out, self.w_out)
-        qkv_here()
-        go_qkv = self.spread(self.w_qkv)
-        ga_here = self.columns_out(self.sh_ga, self.w_ga)
+        self.columns_far(qkv)
+        out = self.columns_out("out")
+        self.columns_far(out)
+        self.spread(qkv)
         for c in start_copies:
             c.wait_recv()
         rim_starts = self.rim_out([self.starts.at[2], self.starts.at[5]], lambda run: self.starts.at[3 * run])
         self.gather_relay(gather_one)
-        out_here()
-        go_out = self.spread(self.w_out)
+        self.spread(out)
+        ga = self.columns_out("ga")
         self.g[me] = self.g_in[...]
+        self.spread_same(qkv)
         self.gather_finish(gather_one)
-        self.spread_on(go_qkv)
-        up_here = self.columns_out(self.sh_up, self.w_up)
-        gather_g = self.gather_start(self.g)
-        dn_here = self.columns_out(self.sh_dn, self.w_dn)
-        self.spread_done(go_qkv)
+        self.spread_rest(qkv)
+        self.spread_done(qkv)
 
         self.project(self.w_qkv)
         rims = self.rim_out(
             [self.qkv.at[4, :, slice(2 * HP, 6 * HP)], self.qkv.at[9, :, slice(2 * HP, 6 * HP)]],
             lambda run: self.qkv.at[5 * run, :, slice(2 * HP, 6 * HP)],
         )
-        self.spread_on(go_out)
-        ga_here()
-        go_ga = self.spread(self.w_ga)
-        self.gather_relay(gather_g)
+        self.columns_far(ga)
+        self.spread(ga)
+        up = self.columns_out("up")
+        self.columns_far(up)
+        self.spread_same(out)
+        self.spread_rest(out)
         for c in rim_starts + rims:
             c.wait_recv()
         self.attend()
-        self.gather_finish(gather_g)
-        self.spread_done(go_out)
+        self.spread(up)
+        dn = self.columns_out("dn")
+        self.spread_done(out)
 
         partial = lambda pair: dot(flat(self.heads[pair]), self.w_out[...], NT)
-        stage = {n: getattr(self, n) for n in ("sc", "rc", "so", "rd0", "rd1", "rx", "ry")}
+        stage = {n: getattr(self, n) for n in ("sc", "rc", "so", "rd", "rz", "ry")}
         scatter = self.scatter_pair(stage, partial)
         self.scatter_send(scatter, partial)
+        self.spread_same(ga)
         self.scatter_relay(scatter)
-        up_here()
-        go_up = self.spread(self.w_up)
-        self.spread_on(go_ga)
+        gather_g = self.gather_start(self.g)
+        self.columns_far(dn)
+        self.spread(dn)
+        self.spread_rest(ga)
         self.resid[...] = self.x_in[...].astype(F32) + self.scatter_finish(scatter)
         resid = self.resid[...]
         self.u2[me] = (resid * norm(resid)).astype(BF)
         gather_two = self.gather_start(self.u2)
-        dn_here()
-        go_dn = self.spread(self.w_dn)
+        self.gather_relay(gather_g)
+        self.spread_same(up)
+        self.spread_rest(up)
         self.gather_relay(gather_two)
-        self.spread_on(go_up)
+        self.gather_finish(gather_g)
+        self.spread_same(dn)
         self.gather_finish(gather_two)
-        self.spread_on(go_dn)
-        for go in (go_ga, go_up, go_dn):
-            self.spread_done(go)
+        self.settle(self.given)
+        self.spread_rest(dn)
+        for g in (ga, up, dn):
+            self.spread_done(g)
 
         self.feed_forward()
+        self.grad_into(self.g_dn, self.g, lambda: whole(self.hidden))
+        sum_dn = self.collect(self.g_dn, self.slots_dn)
         partial = lambda pair: dot(flat(self.d_ga[pair]), self.w_ga[...], NT) + dot(
             flat(self.d_up[pair]), self.w_up[...], NT
         )
         scatter = self.scatter_pair(stage, partial)
         self.scatter_send(scatter, partial)
-        self.grad_into(self.g_dn, self.g, lambda: whole(self.hidden))
-        sum_dn = self.collect(self.g_dn, self.slots_dn)
-        self.scatter_relay(scatter)
         self.settle(self.gathered)
         self.grad_into(self.w_ga, self.u2, lambda: whole(self.d_ga))
         sum_ga = self.collect(self.w_ga, self.slots_ga)
+        self.scatter_relay(scatter)
+        self.collect_on(sum_dn)
         self.grad_into(self.w_up, self.u2, lambda: whole(self.d_up))
         sum_up = self.collect(self.w_up, self.slots_up)
         d_unit = self.scatter_finish(scatter)
@@ -500,12 +582,12 @@
         scale = norm(resid)
         unit = resid * scale
         inner = jnp.mean(d_unit * unit, axis=-1, keepdims=True)
-        self.d_resid[...] = self.g_in[...].astype(F32) + scale * (d_unit - unit * inner)
-        self.d_r[me] = self.d_resid[...].astype(BF)
+        self.in_grad[...] = self.g_in[...].astype(F32) + scale * (d_unit - unit * inner)
+        self.d_r[me] = self.in_grad[...].astype(BF)
         self.settle(gather_g["copies"] + gather_two["copies"] + rims)
         gather_d = self.gather_start(self.d_r)
-        self.collect_on(sum_dn)
         self.gather_relay(gather_d)
+        self.collect_on(sum_ga)
         self.gather_finish(gather_d)
 
         def heads_back(i, _):
@@ -515,71 +597,77 @@
 
         lax.fori_loop(0, SUB, heads_back, 0)
 
+        self.carry[...] = jnp.zeros_like(self.carry)
+
+        def first(run, _):
+            self.attend_back(2 * run)
+            return 0
+
+        def second(run, _):
+            self.attend_back(2 * run + 1)
+            return 0
+
+        lax.fori_loop(0, 2, first, 0)
+        rim_back = self.rim_home(
+            lambda run: self.qkv.at[5 * run, :, slice(2 * HP, 6 * HP)], [self.rim.at[0], self.rim.at[1]]
+        )
+        self.grad_into(self.w_out, self.d_r, lambda: whole(self.heads))
+        sum_out = self.collect(self.w_out, self.slots_out)
+        self.collect_done(sum_dn)
+        backs = [self.columns_back(self.g_dn, self.o_dn)]
+        self.collect_on(sum_up)
+        lax.fori_loop(0, 2, second, 0)
+        of_q, of_kv = slice(0, 2 * HP), slice(2 * HP, 6 * HP)
+        g_q, g_kv = self.g_qkv.at[:, of_q], self.g_qkv.at[:, of_kv]
+        self.grad_into(g_q, self.u1, lambda: [flat(self.qkv[1:5, :, of_q]), flat(self.qkv[6:10, :, of_q])])
+        sum_q = self.collect(g_q, self.slots_qkv.at[:, :, of_q])
+        for c in rim_back:
+            c.wait_recv()
+        for run in range(2):
+            done = self.carry[run] + self.rim[run].astype(F32)
+            self.qkv[5 * run + 4, :, 2 * HP :] = done.astype(BF)
+
+        self.grad_into(g_kv, self.u1, lambda: [flat(self.qkv[1:5, :, of_kv]), flat(self.qkv[6:10, :, of_kv])])
+        sum_kv = self.collect(g_kv, self.slots_qkv.at[:, :, of_kv])
+        self.collect_done(sum_ga)
+        backs.append(self.columns_back(self.w_ga, self.o_ga))
+        partial = lambda pair: dot(flat(self.qkv[pl.ds(self.place(pair), 2)]), self.w_qkv[...], NT)
+        scatter = self.scatter_pair(stage, partial)
+        self.scatter_send(scatter, partial)
+        self.collect_on(sum_out)
+        self.scatter_relay(scatter)
+        self.collect_on(sum_q)
+
         view = {
             "sc": self.u2.at[0:2],
             "so": self.u2.at[2:4],
             "rc": self.g.at[0:2],
-            "rd0": self.g.at[2, 0, :, slice(0, cfg["cut"])],
-            "rd1": self.g.at[2, 0, :, slice(cfg["cut"], cfg["D"])],
-            "rx": self.g.at[2, 1],
+            "rd": self.g.at[2, 0],
+            "rz": self.g.at[2, 1],
             "ry": self.g.at[3, 0],
         }
         partial = lambda pair: dot(flat(self.hidden[pair]), self.w_dn[...], NT)
         mlp = self.scatter_pair(view, partial)
         self.scatter_send(mlp, partial)
-        self.collect_on(sum_ga)
-
-        self.carry[...] = jnp.zeros_like(self.carry)
-
-        def first(run, _):
-            self.attend_back(2 * run)
-            return 0
-
-        def second(run, _):
-            self.attend_back(2 * run + 1)
-            return 0
-
-        lax.fori_loop(0, 2, first, 0)
-        rim_back = self.rim_home(
-            lambda run: self.qkv.at[5 * run, :, slice(2 * HP, 6 * HP)], [self.rim.at[0], self.rim.at[1]]
-        )
+        self.collect_done(sum_up)
+        backs.append(self.columns_back(self.w_up, self.o_up))
+        self.collect_on(sum_kv)
+        self.collect_done(sum_out)
+        backs.append(self.columns_back(self.w_out, self.o_out))
         self.scatter_relay(mlp)
-        lax.fori_loop(0, 2, second, 0)
-        self.collect_on(sum_up)
-        for c in rim_back:
-            c.wait_recv()
-        for run in range(2):
-            done = self.carry[run] + self.rim[run].astype(F32)
-            self.qkv[5 * run + 4, :, 2 * HP :] = done.astype(BF)
-
-        self.grad_into(self.g_qkv, self.u1, lambda: [flat(self.qkv[1:5]), flat(self.qkv[6:10])])
-        sum_qkv = self.collect(self.g_qkv, self.slots_qkv)
-        partial = lambda pair: dot(flat(self.qkv[pl.ds(self.place(pair), 2)]), self.w_qkv[...], NT)
-        scatter = self.scatter_pair(stage, partial)
-        self.scatter_send(scatter, partial)
-        self.grad_into(self.w_out, self.d_r, lambda: whole(self.heads))
-        sum_out = self.collect(self.w_out, self.slots_out)
-        self.scatter_relay(scatter)
-        self.out[...] = (self.resid[...] + self.scatter_finish(mlp)).astype(BF)
-        self.collect_done(sum_dn)
-        dn_back = self.columns_back(self.g_dn, self.o_dn)
-        self.collect_done(sum_ga)
-        ga_back = self.columns_back(self.w_ga, self.o_ga)
         d_unit = self.scatter_finish(scatter)
         x = self.x_in[...].astype(F32)
         scale = norm(x)
         unit = x * scale
         inner = jnp.mean(d_unit * unit, axis=-1, keepdims=True)
-        self.in_grad[...] = self.d_resid[...] + scale * (d_unit - unit * inner)
-        self.collect_on(sum_qkv)
-        self.collect_on(sum_out)
-        self.collect_done(sum_up)
-        up_back = self.columns_back(self.w_up, self.o_up)
-        self.collect_done(sum_qkv)
-        qkv_back = self.columns_back(self.g_qkv, self.o_qkv)
-        self.collect_done(sum_out)
-        out_back = self.columns_back(self.w_out, self.o_out)
-        for wait in (dn_back, ga_back, up_back, qkv_back, out_back):
+        self.in_grad[...] += scale * (d_unit - unit * inner)
+        self.collect_done(sum_q)
+        back_to = lambda span: self.o_qkv.at[:, span] if cfg["whole"] else self.o_qkv.at[:, :, span]
+        backs.append(self.columns_back(g_q, back_to(of_q)))
+        self.out[...] = (self.resid[...] + self.scatter_finish(mlp)).astype(BF)
+        self.collect_done(sum_kv)
+        backs.append(self.columns_back(g_kv, back_to(of_kv)))
+        for wait in backs:
             wait()
         self.settle()
 
@@ -593,18 +681,20 @@
             self.sends = [c for c in self.sends if not any(c is other for other in copies)]
 
 
-def fused(cfg, shares, starts, x, g):
+def fused(cfg, width, weights, starts, x, g):
     d, db = cfg["D"], cfg["DB"]
     rows = 2 * WINDOW
-    cut = cfg["cut"]
     anywhere = pl.BlockSpec(memory_space=pl.ANY)
     vmem = pl.BlockSpec(memory_space=pltpu.VMEM)
     keys = ("qkv", "out", "ga", "up", "dn")
-    width = {key: share.shape[-1] for key, share in zip(keys, shares, strict=True)}
     result = (d,) if cfg["whole"] else (SUB, db)
     outs = [("out", (rows, d), BF, vmem), ("in_grad", (rows, d), F32, vmem)]
     outs += [("o_" + key, result + (width[key],), BF, anywhere) for key in keys]
-    ins = [("sh_" + key, anywhere) for key in keys] + [("starts_in", vmem), ("x_in", vmem), ("g_in", vmem)]
+    if cfg["whole"]:
+        ins = [("sh_" + key, anywhere) for key in keys]
+    else:
+        ins = [(name, vmem) for name in ("raw_qkv", "raw_out", "raw_gu", "raw_dn", "gains")]
+    ins += [(name, vmem) for name in ("doc_starts", "x_in", "g_in")]
     plane = (SUB, 2, rows)
     scratch = [("w_" + key, (d, width[key]), BF) for key in keys]
     scratch += [("g_" + key, (d, width[key]), BF) for key in ("qkv", "dn")]
@@ -621,13 +711,11 @@
         ("carry", (2, rows, 4 * HP), F32),
         ("rim", (2, rows, 4 * HP), BF),
         ("resid", (rows, d), F32),
-        ("d_resid", (rows, d), F32),
-        ("rd0", (rows, cut), BF),
-        ("rd1", (rows, d - cut), BF),
-        ("rx", (rows, d), BF),
+        ("rd", (rows, d), BF),
+        ("rz", (rows, d), BF),
         ("ry", (rows, d), BF),
     ]
-    number = 190
+    number = 200
     names = [n for n, _ in ins] + [n for n, *_ in outs] + [n for n, *_ in scratch]
     names += ["send_sems", "recv_sems", "local_sems"]
 
@@ -643,17 +731,47 @@
         + [
             pltpu.SemaphoreType.DMA((number,)),
             pltpu.SemaphoreType.DMA((number,)),
-            pltpu.SemaphoreType.DMA((10,)),
+            pltpu.SemaphoreType.DMA((11,)),
         ],
         compiler_params=pltpu.CompilerParams(
             collective_id=0, has_side_effects=True, vmem_limit_bytes=63 * 2**20
         ),
-    )(*shares, starts, x, g)
-
-
-def padded(value, size):
-    pads = [(0, 0)] * (value.ndim - 1) + [(0, size - value.shape[-1])]
-    return jnp.pad(value, pads)
+    )(*weights, starts, x, g)
+
+
+def assemble(ff, o_qkv, o_out, o_ga, o_up, o_dn, w_qkv, w_gu, gains, g_qkv, g_out, g_gu, g_dn, g_gain):
+    db = w_qkv.shape[1]
+    lines = gains[...].astype(F32)
+    same = eye(db)
+
+    def column(k):
+        return jnp.sum(jnp.where(same, jnp.broadcast_to(lines[k : k + 1, :], (db, db)), 0.0), axis=1, keepdims=True)
+
+    sums = []
+    gain = column(0)
+    total = jnp.zeros((db, 1), F32)
+    for k in range(3):
+        parts = []
+        for s in range(SUB):
+            for h in range(2):
+                start = (2 * k + h) * HP
+                parts.append(o_qkv[s, :, start : start + DH].astype(F32))
+        value = jnp.concatenate(parts, axis=1)
+        total = total + jnp.sum(value * w_qkv[k].astype(F32), axis=1, keepdims=True)
+        g_qkv[k] = value * gain
+    sums.append(total)
+    gain = column(1)
+    total = jnp.zeros((db, 1), F32)
+    for k, ref in enumerate((o_ga, o_up)):
+        value = jnp.concatenate([ref[s, :, :ff].astype(F32) for s in range(SUB)], axis=1)
+        total = total + jnp.sum(value * w_gu[k].astype(F32), axis=1, keepdims=True)
+        g_gu[k] = value * gain
+    sums.append(total)
+    for k, total in enumerate(sums):
+        g_gain[k : k + 1, :] = jnp.sum(jnp.where(same, jnp.broadcast_to(total, (db, db)), 0.0), axis=0, keepdims=True)
+    parts = [o_out[s, :, h * HP : h * HP + DH].astype(F32) for s in range(SUB) for h in range(2)]
+    g_out[...] = jnp.concatenate(parts, axis=1)
+    g_dn[...] = jnp.concatenate([o_dn[s, :, :ff].astype(F32) for s in range(SUB)], axis=1)
 
 
 def body(size, tokens, doc_starts, w_qkv, w_out, w_gate_up, w_down, gains, cotangent):
@@ -662,10 +780,29 @@
     ff = w_gate_up.shape[2] // SUB
     ffp = -(-ff // HP) * HP
     heads = w_qkv.shape[2] // (SUB * DH)
+    whole = size != 16 or db % 16 != 0
+    cfg = {"D": d, "NH": size // 8, "DB": db, "FF": ff, "whole": whole}
+    width = {"qkv": 3 * heads * HP, "out": heads * HP, "ga": ffp, "up": ffp, "dn": ffp}
+    acts = [doc_starts, tokens.reshape(batches * rows, d), cotangent.reshape(batches * rows, d)]
+
+    def results(out, in_grad, g_qkv, g_out, g_gu, g_dn, gain_sums):
+        gain_sums = gain_sums + lax.ppermute(gain_sums, "tp", [(0, 1), (1, 0)])
+        return (out.reshape(tokens.shape), in_grad.reshape(tokens.shape), g_qkv, g_out, g_gu, g_dn, gain_sums)
+
+    if not whole:
+        out, in_grad, *grads = fused(cfg, width, [w_qkv, w_out.T, w_gate_up, w_down.T, gains], *acts)
+        vmem = pl.BlockSpec(memory_space=pltpu.VMEM)
+        grads = pl.pallas_call(
+            functools.partial(assemble, ff),
+            out_shape=[jax.ShapeDtypeStruct(v.shape, F32) for v in (w_qkv, w_out.T, w_gate_up, w_down.T, gains)],
+            in_specs=[vmem] * 8,
+            out_specs=[vmem] * 5,
+            compiler_params=pltpu.CompilerParams(vmem_limit_bytes=40 * 2**20),
+        )(*grads, w_qkv, w_gate_up, gains)
+        g_qkv, g_out, g_gu, g_dn, gain_sums = grads
+        return results(out, in_grad, g_qkv, g_out.T, g_gu, g_dn.T, gain_sums)
+
     gain = gains.astype(F32)
-    whole = size != 16 or db % 16 != 0
-    cfg = {"D": d, "NH": size // 8, "DB": db, "cut": d // 256 * 128, "whole": whole}
-
     sh_qkv = (w_qkv.astype(F32) * gain[0][None, :, None]).astype(BF).reshape(3, db, SUB, heads, DH)
     sh_qkv = padded(sh_qkv, HP).transpose(2, 1, 0, 3, 4).reshape(SUB, db, 3 * heads * HP)
     sh_out = w_out.T.reshape(db, SUB, heads, DH)
@@ -673,24 +810,16 @@
     scaled = (w_gate_up.astype(F32) * gain[1][None, :, None]).astype(BF).reshape(2, db, SUB, ff)
     sh_ga, sh_up = [padded(scaled[k], ffp).transpose(1, 0, 2) for k in range(2)]
     sh_dn = padded(w_down.T.reshape(db, SUB, ff), ffp).transpose(1, 0, 2)
-    shares = [sh_qkv, sh_out, sh_ga, sh_up, sh_dn]
-
-    if whole:
-        f = lax.axis_index("fsdp")
-        s = (f // 4) % 2 * 2 + f % 2
-        everyone = [lax.all_gather(v, "fsdp", axis=1, tiled=True) for v in shares]
-        shares = [lax.dynamic_index_in_dim(v, s, 0, keepdims=False) for v in everyone]
-    starts = jnp.pad(doc_starts.astype(F32), ((0, 8 - batches), (0, 0)))
-    out, in_grad, *grads = fused(
-        cfg, shares, starts, tokens.reshape(batches * rows, d), cotangent.reshape(batches * rows, d)
-    )
-    if whole:
-        mine = (jnp.arange(SUB) == s)[:, None, None]
-        grads = [
-            lax.psum_scatter(jnp.where(mine, v[None], 0).astype(BF), "fsdp", scatter_dimension=1, tiled=True)
-            for v in grads
-        ]
-    g_qkv, g_out, g_ga, g_up, g_dn = [v.astype(F32) for v in grads]
+    f = lax.axis_index("fsdp")
+    s = (f // 4) % 2 * 2 + f % 2
+    everyone = [lax.all_gather(v, "fsdp", axis=1, tiled=True) for v in (sh_qkv, sh_out, sh_ga, sh_up, sh_dn)]
+    shares = [lax.dynamic_index_in_dim(v, s, 0, keepdims=False) for v in everyone]
+    out, in_grad, *grads = fused(cfg, width, shares, *acts)
+    mine = (jnp.arange(SUB) == s)[:, None, None]
+    g_qkv, g_out, g_ga, g_up, g_dn = [
+        lax.psum_scatter(jnp.where(mine, v[None], 0).astype(BF), "fsdp", scatter_dimension=1, tiled=True).astype(F32)
+        for v in grads
+    ]
     g_qkv = g_qkv.reshape(SUB, db, 3, heads, HP)[..., :DH].transpose(2, 1, 0, 3, 4).reshape(w_qkv.shape)
     g_out = g_out.reshape(SUB, db, heads, HP)[..., :DH].transpose(0, 2, 3, 1).reshape(w_out.shape)
     g_gu = jnp.stack([v[..., :ff].transpose(1, 0, 2).reshape(w_gate_up.shape[1:]) for v in (g_ga, g_up)])
@@ -701,16 +830,8 @@
             jnp.sum(g_gu * w_gate_up.astype(F32), axis=(0, 2)),
         ]
     )
-    gain_sums = gain_sums + lax.ppermute(gain_sums, "tp", [(0, 1), (1, 0)])
-    return (
-        out.reshape(tokens.shape),
-        in_grad.reshape(tokens.shape),
-        g_qkv * gain[0][None, :, None],
-        g_out,
-        g_gu * gain[1][None, :, None],
-        g_dn,
-        gain_sums,
-    )
+    g_qkv, g_gu = g_qkv * gain[0][None, :, None], g_gu * gain[1][None, :, None]
+    return results(out, in_grad, g_qkv, g_out, g_gu, g_dn, gain_sums)
 
 
 def solution(mesh):

time: 408 us -> 373 us (0.914); the launches traced: 402 us -> 373 us
  local copies, waits for them, and re-layouts: 22.6 us -> 8.15 us
  Pallas kernels: 370 us -> 360 us
  other arithmetic: 7.43 us -> 0.56 us
    pallas_call x1, Pallas kernels: 370 us -> 357 us  [fused(): pl.pallas_call(kernel, out_shape=[jax.ShapeDtypeStruct(shape, kind) for _...]
    reshape x14 -> x0, local copies, waits for them, and re-layouts: 10.9 us -> none  [the longest x3 2.67 us: body(): g_qkv.reshape(SUB, db, 3, heads, HP)[..., :DH].transpose(2, 1, 0, 3, 4)]
    unnamed x24 -> x22, local copies, waits for them, and re-layouts: 2.1 us -> 8.15 us
    transpose x8 -> x0, local copies, waits for them, and re-layouts: 5.12 us -> none  [the longest x2 1.73 us: body(): sh_ga, sh_up = [padded(scaled[k], ffp).transpose(1, 0, 2) for k in range(2)]]
    reduce_sum x2 -> x0, other arithmetic: 4.27 us -> none  [the longest x1 2.94 us: body(): jnp.sum(g_gu * w_gate_up.astype(F32), axis=(0, 2))]
  transfers between devices with their start and end apart: 1 -> 1, of which waited for: 0 -> 1; matrix products, arithmetic and copies ran while one was open for 1% -> 0% of each run, Pallas kernels for 0% -> 0%
where the time goes in v3:
time: 373 us
  Pallas kernels  360 us (97%)
  local copies, waits for them, and re-layouts  8.15 us (2%)
    pallas_call x1, Pallas kernels, fused(): pl.pallas_call(kernel, out_shape=[jax.ShapeDtypeStruct(shape, kind) for _...  357 us
    unnamed x22, local copies, waits for them, and re-layouts  8.15 us
  transfers between devices with their start and end apart: 1, of which 1 were waited for; matrix products, arithmetic and copies ran while one was open for 0% of the time, Pallas kernels for 0%

profile of v3, /device:TPU:0, one launch (start us, length us, event | category | flops | bytes accessed | tf_op | source)
XLA Modules:
  0.0 372.9 jit_solution(5843727301645113063)
XLA Ops:
  0.6 0.0 copy-start.1
  0.6 0.0 copy-start.7
  0.7 356.5 %shard_map.135 = (bf16[128,1792]{1,0:T(8,128)(2,1)}, f32[128,1792]{1,0:T(8,128)}, bf16[4,112,768]{2,1,0:T(8,128)(2,1)}, bf16[4,112,256]{2,1,0:T(8,128)(2,1)}, bf...) custom-call(bf16[3,112,896]{2,1,0:T(8,128)(2,1)} %w_qkv.1, ...), custom_call_target="tpu_custom_call" | custom-call | tf_op jit(solution)/shard_map/pallas_call | solution.py:725
  357.2 0.0 copy-done.1
  357.2 0.0 copy-done.7
  357.2 0.0 copy-start
  357.2 1.2 copy-done
  358.5 0.0 copy-start.2
  358.5 1.1 copy-done.2
  359.6 0.0 copy-start.3
  359.6 1.1 copy-done.3
  360.6 0.0 copy-start.4
  360.6 1.1 copy-done.4
  361.7 0.0 copy-start.5
  361.7 1.1 copy-done.5
  362.7 0.0 copy-start.6
  362.7 0.9 copy-done.6
  363.7 0.0 copy-start.9
  363.7 3.3 shard_map.136
  367.0 0.0 copy-start.8
  367.0 1.5 collective-permute-start
  368.5 2.1 collective-permute-done
  370.6 0.6 add.3
  371.2 0.0 copy-done.9
  371.2 0.8 copy.17
  371.9 0.0 copy-done.8
  371.9 0.9 copy.18
Async XLA Ops:
  0.6 356.6 %copy-start.1 = (bf16[3,112,896]{2,1,0:T(8,128)(2,1)S(1)}, bf16[3,112,896]{2,1,0:T(8,128)(2,1)}, u32[]{:S(2)}) copy-start(bf16[3,112,896]{2,1,0:T(8,128)(2,1)} %w_qkv.1) | copy-start | bytes 1806340
  0.6 356.6 %copy-start.7 = (bf16[2,112]{1,0:T(2,128)(2,1)S(1)}, bf16[2,112]{1,0:T(2,128)(2,1)}, u32[]{:S(2)}) copy-start(bf16[2,112]{1,0:T(2,128)(2,1)} %gains.1) | copy-start | bytes 1348
  357.2 1.2 copy-start
  358.5 1.1 copy-start.2
  359.6 1.1 copy-start.3
  360.6 1.1 copy-start.4
  361.7 1.1 copy-start.5
  362.7 0.9 copy-start.6
  363.7 7.5 %copy-start.9 = (bf16[128,1792]{1,0:T(8,128)(2,1)S(1)}, bf16[128,1792]{1,0:T(8,128)(2,1)}, u32[]{:S(2)}) copy-start(bf16[128,1792]{1,0:T(8,128)(2,1)} %get-tuple-element.19) | copy-start | bytes 1376260
  367.0 4.9 %copy-start.8 = (f32[128,1792]{1,0:T(8,128)S(1)}, f32[128,1792]{1,0:T(8,128)}, u32[]{:S(2)}) copy-start(f32[128,1792]{1,0:T(8,128)} %get-tuple-element.20) | copy-start | bytes 2752516
  367.0 3.6 collective-permute-start

commit v4 on v3

--- a/solution.py
+++ b/solution.py
@@ -100,7 +100,7 @@
             partners += [self.other(s) for s in (self.s, self.sib, self.zn, self.diag)]
         for partner in partners:
             pl.semaphore_signal(sem, inc=1, device_id=partner, device_id_type=pl.DeviceIdType.MESH)
-        pl.semaphore_wait(sem, len(partners))
+        return lambda: pl.semaphore_wait(sem, len(partners))
 
     def remote(self, src, dst, device, sent=None, received=None):
         k = self.count
@@ -156,7 +156,8 @@
         full = getattr(self, "w_" + key)
         if self.cfg["whole"]:
             return {"full": full, "own": self.local(getattr(self, "sh_" + key), full), "here": []}
-        self.prepare(key)
+        if key != "qkv":
+            self.prepare(key)
         shares = functools.partial(self.prepared, key)
         mine = self.share(full, self.s)
         here = [self.remote(shares(s), mine, self.mate(s)) for s in (self.zn, self.diag, self.sib)]
@@ -271,13 +272,12 @@
         for k, hi in enumerate((self.next_hi, self.hi)):
             for z in range(2):
                 near.append(self.to_x(grad.at[self.rows(hi, z, 1 - self.x), :], slots.at[2 * k + z]))
-        return {"grad": grad, "slots": slots, "near": near}
-
-    def collect_on(self, g):
+        return {"grad": grad, "slots": slots, "near": near, "far": []}
+
+    def collect_on(self, g, planes=(0, 1)):
         if g is None:
             return
-        g["far"] = []
-        for z in range(2):
+        for z in planes:
             g["near"][z].wait_recv()
             rows = self.rows(self.next_hi, z, self.x)
             self.add_rows(g["grad"], rows, [g["slots"].at[z]])
@@ -304,25 +304,35 @@
 
     def gather_start(self, buf):
         own = buf.at[self.s, self.y]
-        return {"z": self.to_z(own, own), "y": self.to_y(own, own), "own": self.to_sib(own, own), "buf": buf}
+        halves = [own.at[:, h] for h in self.halves]
+        z = [self.to_z(half, half) for half in halves]
+        return {"z": z, "y": self.to_y(own, own), "own": self.to_sib(own, own), "buf": buf}
 
     def gather_relay(self, g):
         buf = g["buf"]
-        g["z"].wait_recv()
-        part = buf.at[self.zn, self.y]
-        g["d"] = self.to_y(part, part)
-        g["fz"] = self.to_sib(part, part)
+        g["d"], g["fz"] = [], []
+        for c, h in zip(g["z"], self.halves, strict=True):
+            c.wait_recv()
+            part = buf.at[self.zn, self.y, :, h]
+            g["d"].append(self.to_y(part, part))
+            g["fz"].append(self.to_sib(part, part))
         g["y"].wait_recv()
         part = buf.at[self.s, self.yn]
         g["fy"] = self.to_sib(part, part)
-
-    def gather_finish(self, g):
-        g["d"].wait_recv()
-        part = g["buf"].at[self.zn, self.yn]
-        g["fd"] = self.to_sib(part, part)
-        for name in ("own", "fz", "fy", "fd"):
-            g[name].wait_recv()
-        g["copies"] = [g[n] for n in ("own", "z", "y", "d", "fz", "fy", "fd")]
+        g["own"].wait_recv()
+
+    def gather_near(self, g):
+        g["fy"].wait_recv()
+
+    def gather_finish(self, g, near=False):
+        g["fd"] = []
+        for c, h in zip(g["d"], self.halves, strict=True):
+            c.wait_recv()
+            part = g["buf"].at[self.zn, self.yn, :, h]
+            g["fd"].append(self.to_sib(part, part))
+        for c in ([] if near else [g["fy"]]) + g["fz"] + g["fd"]:
+            c.wait_recv()
+        g["copies"] = [g["own"], g["y"], g["fy"]] + g["z"] + g["d"] + g["fz"] + g["fd"]
 
     def scatter_pair(self, st, partial):
         sc, rc = st["sc"], st["rc"]
@@ -466,10 +476,11 @@
 
         lax.fori_loop(0, self.cfg["D"] // width, step, 0)
 
-    def feed_forward(self):
+    def feed_forward(self, plane):
         ff = self.w_dn.shape[1]
 
-        def step(i, _):
+        def step(k, _):
+            i = 2 * plane + k
             rows = flat(self.u2[i])
             gate = dot(rows, self.w_ga[...], NN)
             upward = dot(rows, self.w_up[...], NN)
@@ -483,7 +494,7 @@
             self.d_up[i] = (d_hidden * silu).astype(BF).reshape(shape)
             return 0
 
-        lax.fori_loop(0, SUB, step, 0)
+        lax.fori_loop(0, 2, step, 0)
 
     def run(self):
         cfg = self.cfg
@@ -491,31 +502,33 @@
         norm = lambda v: lax.rsqrt(jnp.mean(v * v, axis=-1, keepdims=True) + EPSILON)
         whole = lambda ref: [flat(ref[...])]
 
-        self.barrier()
+        everyone_here = self.barrier()
         line = 1 + self.s + self.s // 2
         own_starts = self.doc_starts[...].astype(F32)
         fill = jnp.zeros((self.starts.shape[1] - own_starts.shape[0], own_starts.shape[1]), F32)
         self.starts[line] = jnp.concatenate([own_starts, fill], axis=0)
         own_line = self.starts.at[line]
+        x = self.x_in[...].astype(F32)
+        self.u1[me] = (x * norm(x)).astype(BF)
+        if not cfg["whole"]:
+            self.prepare("qkv")
+        everyone_here()
         start_copies = [self.remote(own_line, own_line, self.mate(s)) for s in (self.sib, self.zn, self.diag)]
         qkv = self.columns_out("qkv")
-        x = self.x_in[...].astype(F32)
-        self.u1[me] = (x * norm(x)).astype(BF)
         gather_one = self.gather_start(self.u1)
         self.columns_far(qkv)
+        self.spread(qkv)
         out = self.columns_out("out")
         self.columns_far(out)
-        self.spread(qkv)
         for c in start_copies:
             c.wait_recv()
         rim_starts = self.rim_out([self.starts.at[2], self.starts.at[5]], lambda run: self.starts.at[3 * run])
         self.gather_relay(gather_one)
+        self.spread_same(qkv)
         self.spread(out)
         ga = self.columns_out("ga")
-        self.g[me] = self.g_in[...]
-        self.spread_same(qkv)
+        self.spread_rest(qkv)
         self.gather_finish(gather_one)
-        self.spread_rest(qkv)
         self.spread_done(qkv)
 
         self.project(self.w_qkv)
@@ -534,35 +547,37 @@
         self.attend()
         self.spread(up)
         dn = self.columns_out("dn")
+        self.spread_same(ga)
         self.spread_done(out)
 
         partial = lambda pair: dot(flat(self.heads[pair]), self.w_out[...], NT)
         stage = {n: getattr(self, n) for n in ("sc", "rc", "so", "rd", "rz", "ry")}
         scatter = self.scatter_pair(stage, partial)
         self.scatter_send(scatter, partial)
-        self.spread_same(ga)
+        self.spread_rest(ga)
         self.scatter_relay(scatter)
+        self.g[me] = self.g_in[...]
         gather_g = self.gather_start(self.g)
         self.columns_far(dn)
         self.spread(dn)
-        self.spread_rest(ga)
+        self.spread_same(up)
+        self.spread_rest(up)
         self.resid[...] = self.x_in[...].astype(F32) + self.scatter_finish(scatter)
         resid = self.resid[...]
         self.u2[me] = (resid * norm(resid)).astype(BF)
         gather_two = self.gather_start(self.u2)
         self.gather_relay(gather_g)
-        self.spread_same(up)
-        self.spread_rest(up)
+        self.spread_same(dn)
+        self.settle(self.given)
+        self.spread_rest(dn)
         self.gather_relay(gather_two)
         self.gather_finish(gather_g)
-        self.spread_same(dn)
-        self.gather_finish(gather_two)
-        self.settle(self.given)
-        self.spread_rest(dn)
         for g in (ga, up, dn):
             self.spread_done(g)
-
-        self.feed_forward()
+        self.gather_near(gather_two)
+        self.feed_forward(self.s // 2)
+        self.gather_finish(gather_two, near=True)
+        self.feed_forward(1 - self.s // 2)
         self.grad_into(self.g_dn, self.g, lambda: whole(self.hidden))
         sum_dn = self.collect(self.g_dn, self.slots_dn)
         partial = lambda pair: dot(flat(self.d_ga[pair]), self.w_ga[...], NT) + dot(
@@ -574,7 +589,7 @@
         self.grad_into(self.w_ga, self.u2, lambda: whole(self.d_ga))
         sum_ga = self.collect(self.w_ga, self.slots_ga)
         self.scatter_relay(scatter)
-        self.collect_on(sum_dn)
+        self.collect_on(sum_dn, (0,))
         self.grad_into(self.w_up, self.u2, lambda: whole(self.d_up))
         sum_up = self.collect(self.w_up, self.slots_up)
         d_unit = self.scatter_finish(scatter)
@@ -586,57 +601,8 @@
         self.d_r[me] = self.in_grad[...].astype(BF)
         self.settle(gather_g["copies"] + gather_two["copies"] + rims)
         gather_d = self.gather_start(self.d_r)
+        self.collect_on(sum_dn, (1,))
         self.gather_relay(gather_d)
-        self.collect_on(sum_ga)
-        self.gather_finish(gather_d)
-
-        def heads_back(i, _):
-            value = dot(flat(self.d_r[i]), self.w_out[...], NN).astype(BF)
-            self.d_heads[i] = value.reshape(2, 2 * WINDOW, 2 * HP)
-            return 0
-
-        lax.fori_loop(0, SUB, heads_back, 0)
-
-        self.carry[...] = jnp.zeros_like(self.carry)
-
-        def first(run, _):
-            self.attend_back(2 * run)
-            return 0
-
-        def second(run, _):
-            self.attend_back(2 * run + 1)
-            return 0
-
-        lax.fori_loop(0, 2, first, 0)
-        rim_back = self.rim_home(
-            lambda run: self.qkv.at[5 * run, :, slice(2 * HP, 6 * HP)], [self.rim.at[0], self.rim.at[1]]
-        )
-        self.grad_into(self.w_out, self.d_r, lambda: whole(self.heads))
-        sum_out = self.collect(self.w_out, self.slots_out)
-        self.collect_done(sum_dn)
-        backs = [self.columns_back(self.g_dn, self.o_dn)]
-        self.collect_on(sum_up)
-        lax.fori_loop(0, 2, second, 0)
-        of_q, of_kv = slice(0, 2 * HP), slice(2 * HP, 6 * HP)
-        g_q, g_kv = self.g_qkv.at[:, of_q], self.g_qkv.at[:, of_kv]
-        self.grad_into(g_q, self.u1, lambda: [flat(self.qkv[1:5, :, of_q]), flat(self.qkv[6:10, :, of_q])])
-        sum_q = self.collect(g_q, self.slots_qkv.at[:, :, of_q])
-        for c in rim_back:
-            c.wait_recv()
-        for run in range(2):
-            done = self.carry[run] + self.rim[run].astype(F32)
-            self.qkv[5 * run + 4, :, 2 * HP :] = done.astype(BF)
-
-        self.grad_into(g_kv, self.u1, lambda: [flat(self.qkv[1:5, :, of_kv]), flat(self.qkv[6:10, :, of_kv])])
-        sum_kv = self.collect(g_kv, self.slots_qkv.at[:, :, of_kv])
-        self.collect_done(sum_ga)
-        backs.append(self.columns_back(self.w_ga, self.o_ga))
-        partial = lambda pair: dot(flat(self.qkv[pl.ds(self.place(pair), 2)]), self.w_qkv[...], NT)
-        scatter = self.scatter_pair(stage, partial)
-        self.scatter_send(scatter, partial)
-        self.collect_on(sum_out)
-        self.scatter_relay(scatter)
-        self.collect_on(sum_q)
 
         view = {
             "sc": self.u2.at[0:2],
@@ -649,24 +615,76 @@
         partial = lambda pair: dot(flat(self.hidden[pair]), self.w_dn[...], NT)
         mlp = self.scatter_pair(view, partial)
         self.scatter_send(mlp, partial)
+        self.collect_on(sum_ga)
+        self.gather_finish(gather_d)
+
+        d_heads = self.d_heads = self.d_ga.at[:, :, :, slice(0, 2 * HP)]
+
+        def heads_back(i, _):
+            value = dot(flat(self.d_r[i]), self.w_out[...], NN).astype(BF)
+            d_heads[i] = value.reshape(2, 2 * WINDOW, 2 * HP)
+            return 0
+
+        lax.fori_loop(0, SUB, heads_back, 0)
+        self.collect_done(sum_dn)
+        backs = [self.columns_back(self.g_dn, self.o_dn)]
+
+        self.carry[...] = jnp.zeros_like(self.carry)
+
+        def first(run, _):
+            self.attend_back(2 * run)
+            return 0
+
+        def second(run, _):
+            self.attend_back(2 * run + 1)
+            return 0
+
+        lax.fori_loop(0, 2, first, 0)
+        rim_back = self.rim_home(
+            lambda run: self.qkv.at[5 * run, :, slice(2 * HP, 6 * HP)], [self.rim.at[0], self.rim.at[1]]
+        )
+        self.scatter_relay(mlp)
+        lax.fori_loop(0, 2, second, 0)
+        of_q, of_kv = slice(0, 2 * HP), slice(2 * HP, 6 * HP)
+        g_q, g_kv = self.g_qkv.at[:, of_q], self.g_qkv.at[:, of_kv]
+        self.grad_into(g_q, self.u1, lambda: [flat(self.qkv[1:5, :, of_q]), flat(self.qkv[6:10, :, of_q])])
+        sum_q = self.collect(g_q, self.slots_qkv.at[:, :, of_q])
+        self.collect_on(sum_up)
+        self.collect_done(sum_ga)
+        backs.append(self.columns_back(self.w_ga, self.o_ga))
+        for c in rim_back:
+            c.wait_recv()
+        for run in range(2):
+            done = self.carry[run] + self.rim[run].astype(F32)
+            self.qkv[5 * run + 4, :, 2 * HP :] = done.astype(BF)
+
+        self.grad_into(g_kv, self.u1, lambda: [flat(self.qkv[1:5, :, of_kv]), flat(self.qkv[6:10, :, of_kv])])
+        sum_kv = self.collect(g_kv, self.slots_qkv.at[:, :, of_kv])
+        self.grad_into(self.w_out, self.d_r, lambda: whole(self.heads))
+        sum_out = self.collect(self.w_out, self.slots_out)
+        partial = lambda pair: dot(flat(self.qkv[pl.ds(self.place(pair), 2)]), self.w_qkv[...], NT)
+        scatter = self.scatter_pair(stage, partial)
+        self.scatter_send(scatter, partial)
+        self.collect_on(sum_q)
+        self.scatter_relay(scatter)
         self.collect_done(sum_up)
         backs.append(self.columns_back(self.w_up, self.o_up))
         self.collect_on(sum_kv)
-        self.collect_done(sum_out)
-        backs.append(self.columns_back(self.w_out, self.o_out))
-        self.scatter_relay(mlp)
+        self.out[...] = (self.resid[...] + self.scatter_finish(mlp)).astype(BF)
+        back_to = lambda span: self.o_qkv.at[:, span] if cfg["whole"] else self.o_qkv.at[:, :, span]
+        self.collect_done(sum_q)
+        backs.append(self.columns_back(g_q, back_to(of_q)))
         d_unit = self.scatter_finish(scatter)
         x = self.x_in[...].astype(F32)
         scale = norm(x)
         unit = x * scale
         inner = jnp.mean(d_unit * unit, axis=-1, keepdims=True)
         self.in_grad[...] += scale * (d_unit - unit * inner)
-        self.collect_done(sum_q)
-        back_to = lambda span: self.o_qkv.at[:, span] if cfg["whole"] else self.o_qkv.at[:, :, span]
-        backs.append(self.columns_back(g_q, back_to(of_q)))
-        self.out[...] = (self.resid[...] + self.scatter_finish(mlp)).astype(BF)
+        self.collect_on(sum_out)
         self.collect_done(sum_kv)
         backs.append(self.columns_back(g_kv, back_to(of_kv)))
+        self.collect_done(sum_out)
+        backs.append(self.columns_back(self.w_out, self.o_out))
         for wait in backs:
             wait()
         self.settle()
@@ -701,7 +719,7 @@
     slot = 16 if cfg["whole"] else 2 * db
     scratch += [("slots_" + key, (6, slot, width[key]), BF) for key in keys]
     scratch += [(name, plane + (d,), BF) for name in ("u1", "u2", "g", "d_r")]
-    scratch += [(name, plane + (width["out"],), BF) for name in ("heads", "d_heads")]
+    scratch += [(name, plane + (width["out"],), BF) for name in ("heads",)]
     scratch += [(name, plane + (width["dn"],), BF) for name in ("hidden", "d_ga", "d_up")]
     scratch += [(name, (2, 2, rows, d), BF) for name in ("sc", "rc", "so")]
     scratch += [
@@ -715,7 +733,7 @@
         ("rz", (rows, d), BF),
         ("ry", (rows, d), BF),
     ]
-    number = 200
+    number = 220
     names = [n for n, _ in ins] + [n for n, *_ in outs] + [n for n, *_ in scratch]
     names += ["send_sems", "recv_sems", "local_sems"]
 
@@ -734,7 +752,7 @@
             pltpu.SemaphoreType.DMA((11,)),
         ],
         compiler_params=pltpu.CompilerParams(
-            collective_id=0, has_side_effects=True, vmem_limit_bytes=63 * 2**20
+            collective_id=0, has_side_effects=True, vmem_limit_bytes=64 * 2**20
         ),
     )(*weights, starts, x, g)
 

time: 373 us -> 344 us (0.922)
  Pallas kernels: 360 us -> 329 us
    pallas_call x1, Pallas kernels: 357 us -> 325 us  [fused(): pl.pallas_call(kernel, out_shape=[jax.ShapeDtypeStruct(shape, kind) for _...]
where the time goes in v4:
time: 344 us; the launch traced here: 343 us
  Pallas kernels  329 us (96%)
  local copies, waits for them, and re-layouts  9.87 us (3%)
    pallas_call x1, Pallas kernels, fused(): pl.pallas_call(kernel, out_shape=[jax.ShapeDtypeStruct(shape, kind) for _...  325 us
    unnamed x22, local copies, waits for them, and re-layouts  9.87 us
  transfers between devices with their start and end apart: 1, of which 1 were waited for; matrix products, arithmetic and copies ran while one was open for 0% of the time, Pallas kernels for 0%

profile of v4, /device:TPU:0, one launch (start us, length us, event | category | flops | bytes accessed | tf_op | source)
XLA Modules:
  0.0 343.3 jit_solution(497907340740827883)
XLA Ops:
  0.6 325.3 %shard_map.135 = (bf16[128,1792]{1,0:T(8,128)(2,1)}, f32[128,1792]{1,0:T(8,128)}, bf16[4,112,768]{2,1,0:T(8,128)(2,1)}, bf16[4,112,256]{2,1,0:T(8,128)(2,1)}, bf...) custom-call(bf16[3,112,896]{2,1,0:T(8,128)(2,1)} %w_qkv.1, ...), custom_call_target="tpu_custom_call" | custom-call | tf_op jit(solution)/shard_map/pallas_call | solution.py:743
  325.9 0.0 copy-start
  326.0 1.2 copy-done
  327.2 0.0 copy-start.1
  327.2 1.1 copy-done.1
  328.3 0.0 copy-start.2
  328.3 1.1 copy-done.2
  329.4 0.0 copy-start.3
  329.4 1.1 copy-done.3
  330.4 0.0 copy-start.4
  330.4 1.1 copy-done.4
  331.5 0.0 copy-start.5
  331.5 1.1 copy-done.5
  332.5 0.0 copy-start.6
  332.5 0.9 copy-done.6
  333.5 0.0 copy-start.7
  333.5 0.7 copy-done.7
  334.1 0.0 copy-start.9
  334.1 3.3 shard_map.136
  337.5 0.0 copy-start.8
  337.5 0.5 collective-permute-start
  337.9 3.1 collective-permute-done
  341.0 0.6 add.3
  341.6 0.0 copy-done.9
  341.6 0.8 copy.17
  342.4 0.0 copy-done.8
  342.4 0.9 copy.18
Async XLA Ops:
  325.9 1.2 copy-start
  327.2 1.1 copy-start.1
  328.3 1.1 copy-start.2
  329.4 1.1 copy-start.3
  330.4 1.1 copy-start.4
  331.5 1.1 copy-start.5
  332.5 0.9 copy-start.6
  333.5 0.7 copy-start.7
  334.1 7.5 %copy-start.9 = (bf16[128,1792]{1,0:T(8,128)(2,1)S(1)}, bf16[128,1792]{1,0:T(8,128)(2,1)}, u32[]{:S(2)}) copy-start(bf16[128,1792]{1,0:T(8,128)(2,1)} %get-tuple-element.19) | copy-start | bytes 1376260
  337.5 4.9 %copy-start.8 = (f32[128,1792]{1,0:T(8,128)S(1)}, f32[128,1792]{1,0:T(8,128)}, u32[]{:S(2)}) copy-start(f32[128,1792]{1,0:T(8,128)} %get-tuple-element.20) | copy-start | bytes 2752516
  337.5 3.6 %collective-permute-start = (f32[2,112]{1,0:T(2,128)S(1)}, f32[2,112]{1,0:T(2,128)S(1)}, u32[]{:S(2)}, u32[]{:S(2)}) collective-permute-start(f32[2,112]{1,0:T(2,128)S(1)} %get-tuple-element.30), channel_id=1, source_target_pairs={{0,1},{1,0},{2,3},{3,2},{4,5},{5,4},{6,7},{7,6},{8,9},{9,8},{10,11... | collective-permute-start | bytes 2696 | tf_op jit(solution)/shard_map/ppermute | solution.py:807

commit v5 on v4

--- a/solution.py
+++ b/solution.py
@@ -411,9 +411,9 @@
         cols = slice(part * 2 * HP + head * HP, part * 2 * HP + (head + 1) * HP)
         return self.qkv[index, batch * WINDOW : (batch + 1) * WINDOW, cols]
 
-    def attend(self):
-        def step(n, _):
-            s = SUB - 1 - n
+    def attend(self, first):
+        def step(run, _):
+            s = 2 * run + first
             allowed = self.masks(s)
             for half in range(2):
                 p = self.place(s) + half
@@ -432,7 +432,7 @@
                         self.heads[s, half, batch * WINDOW : (batch + 1) * WINDOW, head * HP : (head + 1) * HP] = out
             return 0
 
-        lax.fori_loop(0, SUB, step, 0)
+        lax.fori_loop(0, 2, step, 0)
 
     def attend_back(self, s):
         run = s // 2
@@ -518,16 +518,15 @@
         gather_one = self.gather_start(self.u1)
         self.columns_far(qkv)
         self.spread(qkv)
+        for c in start_copies:
+            c.wait_recv()
+        rim_starts = self.rim_out([self.starts.at[2], self.starts.at[5]], lambda run: self.starts.at[3 * run])
+        self.spread_same(qkv)
+        self.gather_relay(gather_one)
+        self.spread_rest(qkv)
         out = self.columns_out("out")
         self.columns_far(out)
-        for c in start_copies:
-            c.wait_recv()
-        rim_starts = self.rim_out([self.starts.at[2], self.starts.at[5]], lambda run: self.starts.at[3 * run])
-        self.gather_relay(gather_one)
-        self.spread_same(qkv)
-        self.spread(out)
         ga = self.columns_out("ga")
-        self.spread_rest(qkv)
         self.gather_finish(gather_one)
         self.spread_done(qkv)
 
@@ -536,15 +535,17 @@
             [self.qkv.at[4, :, slice(2 * HP, 6 * HP)], self.qkv.at[9, :, slice(2 * HP, 6 * HP)]],
             lambda run: self.qkv.at[5 * run, :, slice(2 * HP, 6 * HP)],
         )
+        self.spread(out)
         self.columns_far(ga)
-        self.spread(ga)
         up = self.columns_out("up")
-        self.columns_far(up)
+        self.attend(1)
         self.spread_same(out)
         self.spread_rest(out)
         for c in rim_starts + rims:
             c.wait_recv()
-        self.attend()
+        self.spread(ga)
+        self.columns_far(up)
+        self.attend(0)
         self.spread(up)
         dn = self.columns_out("dn")
         self.spread_same(ga)
@@ -554,20 +555,20 @@
         stage = {n: getattr(self, n) for n in ("sc", "rc", "so", "rd", "rz", "ry")}
         scatter = self.scatter_pair(stage, partial)
         self.scatter_send(scatter, partial)
+        self.scatter_relay(scatter)
         self.spread_rest(ga)
-        self.scatter_relay(scatter)
         self.g[me] = self.g_in[...]
         gather_g = self.gather_start(self.g)
         self.columns_far(dn)
         self.spread(dn)
         self.spread_same(up)
-        self.spread_rest(up)
         self.resid[...] = self.x_in[...].astype(F32) + self.scatter_finish(scatter)
         resid = self.resid[...]
         self.u2[me] = (resid * norm(resid)).astype(BF)
         gather_two = self.gather_start(self.u2)
+        self.spread_rest(up)
+        self.spread_same(dn)
         self.gather_relay(gather_g)
-        self.spread_same(dn)
         self.settle(self.given)
         self.spread_rest(dn)
         self.gather_relay(gather_two)
@@ -757,7 +758,16 @@
     )(*weights, starts, x, g)
 
 
-def assemble(ff, o_qkv, o_out, o_ga, o_up, o_dn, w_qkv, w_gu, gains, g_qkv, g_out, g_gu, g_dn, g_gain):
+def assemble(ff, *refs):
+    gains, sources, results, g_gain = refs[0], refs[1:10], refs[10:16], refs[16]
+    held, made, sems = refs[17:26], refs[26:30], refs[30]
+    copies = [pltpu.make_async_copy(a, b, sems.at[k]) for k, (a, b) in enumerate(zip(sources, held, strict=True))]
+    for c in copies:
+        c.start()
+    ready = made + held[7:]
+    back = [pltpu.make_async_copy(a, b, sems.at[9 + k]) for k, (a, b) in enumerate(zip(ready, results, strict=True))]
+    o_ga, o_up, w_gu, o_dn, o_qkv, w_qkv, o_out = held[:7]
+    g_gu, g_dn, g_qkv, g_out = made
     db = w_qkv.shape[1]
     lines = gains[...].astype(F32)
     same = eye(db)
@@ -765,9 +775,26 @@
     def column(k):
         return jnp.sum(jnp.where(same, jnp.broadcast_to(lines[k : k + 1, :], (db, db)), 0.0), axis=1, keepdims=True)
 
-    sums = []
+    def put(k, total):
+        g_gain[k : k + 1, :] = jnp.sum(jnp.where(same, jnp.broadcast_to(total, (db, db)), 0.0), axis=0, keepdims=True)
+
+    gain = column(1)
+    total = jnp.zeros((db, 1), F32)
+    copies[2].wait()
+    for k, ref in enumerate((o_ga, o_up)):
+        copies[k].wait()
+        value = jnp.concatenate([ref[s, :, :ff].astype(F32) for s in range(SUB)], axis=1)
+        total = total + jnp.sum(value * w_gu[k].astype(F32), axis=1, keepdims=True)
+        g_gu[k] = value * gain
+    back[0].start()
+    put(1, total)
+    copies[3].wait()
+    g_dn[...] = jnp.concatenate([o_dn[s, :, :ff].astype(F32) for s in range(SUB)], axis=1)
+    back[1].start()
     gain = column(0)
     total = jnp.zeros((db, 1), F32)
+    copies[4].wait()
+    copies[5].wait()
     for k in range(3):
         parts = []
         for s in range(SUB):
@@ -777,19 +804,17 @@
         value = jnp.concatenate(parts, axis=1)
         total = total + jnp.sum(value * w_qkv[k].astype(F32), axis=1, keepdims=True)
         g_qkv[k] = value * gain
-    sums.append(total)
-    gain = column(1)
-    total = jnp.zeros((db, 1), F32)
-    for k, ref in enumerate((o_ga, o_up)):
-        value = jnp.concatenate([ref[s, :, :ff].astype(F32) for s in range(SUB)], axis=1)
-        total = total + jnp.sum(value * w_gu[k].astype(F32), axis=1, keepdims=True)
-        g_gu[k] = value * gain
-    sums.append(total)
-    for k, total in enumerate(sums):
-        g_gain[k : k + 1, :] = jnp.sum(jnp.where(same, jnp.broadcast_to(total, (db, db)), 0.0), axis=0, keepdims=True)
+    back[2].start()
+    put(0, total)
+    copies[6].wait()
     parts = [o_out[s, :, h * HP : h * HP + DH].astype(F32) for s in range(SUB) for h in range(2)]
     g_out[...] = jnp.concatenate(parts, axis=1)
-    g_dn[...] = jnp.concatenate([o_dn[s, :, :ff].astype(F32) for s in range(SUB)], axis=1)
+    back[3].start()
+    for k in range(2):
+        copies[7 + k].wait()
+        back[4 + k].start()
+    for c in back:
+        c.wait()
 
 
 def body(size, tokens, doc_starts, w_qkv, w_out, w_gate_up, w_down, gains, cotangent):
@@ -809,15 +834,20 @@
 
     if not whole:
         out, in_grad, *grads = fused(cfg, width, [w_qkv, w_out.T, w_gate_up, w_down.T, gains], *acts)
-        vmem = pl.BlockSpec(memory_space=pltpu.VMEM)
-        grads = pl.pallas_call(
+        o_qkv, o_out, o_ga, o_up, o_dn = grads
+        sources = [o_ga, o_up, w_gate_up, o_dn, o_qkv, w_qkv, o_out, out, in_grad]
+        made = [jax.ShapeDtypeStruct(v.shape, F32) for v in (w_gate_up, w_down.T, w_qkv, w_out.T)]
+        shapes = made + [jax.ShapeDtypeStruct(v.shape, v.dtype) for v in (out, in_grad)]
+        shapes.append(jax.ShapeDtypeStruct(gains.shape, F32))
+        anywhere, vmem = pl.BlockSpec(memory_space=pl.ANY), pl.BlockSpec(memory_space=pltpu.VMEM)
+        g_gu, g_dn, g_qkv, g_out, out, in_grad, gain_sums = pl.pallas_call(
             functools.partial(assemble, ff),
-            out_shape=[jax.ShapeDtypeStruct(v.shape, F32) for v in (w_qkv, w_out.T, w_gate_up, w_down.T, gains)],
-            in_specs=[vmem] * 8,
-            out_specs=[vmem] * 5,
-            compiler_params=pltpu.CompilerParams(vmem_limit_bytes=40 * 2**20),
-        )(*grads, w_qkv, w_gate_up, gains)
-        g_qkv, g_out, g_gu, g_dn, gain_sums = grads
+            out_shape=shapes,
+            in_specs=[vmem] + [anywhere] * 9,
+            out_specs=[anywhere] * 6 + [vmem],
+            scratch_shapes=[pltpu.VMEM(v.shape, v.dtype) for v in sources + made] + [pltpu.SemaphoreType.DMA((15,))],
+            compiler_params=pltpu.CompilerParams(vmem_limit_bytes=63 * 2**20),
+        )(gains, *sources)
         return results(out, in_grad, g_qkv, g_out.T, g_gu, g_dn.T, gain_sums)
 
     gain = gains.astype(F32)

time: 344 us -> 329 us (0.956)
  local copies, waits for them, and re-layouts: 9.87 us -> 0 us
  Pallas kernels: 329 us -> 322 us
    unnamed x22 -> x0, local copies, waits for them, and re-layouts: 9.87 us -> none
    pallas_call x1, Pallas kernels: 325 us -> 316 us  [fused(): pl.pallas_call(kernel, out_shape=[jax.ShapeDtypeStruct(shape, kind) for _...]
where the time goes in v5:
time: 329 us
  Pallas kernels  322 us (98%)
    pallas_call x1, Pallas kernels, fused(): pl.pallas_call(kernel, out_shape=[jax.ShapeDtypeStruct(shape, kind) for _...  316 us
  transfers between devices with their start and end apart: 1, of which 1 were waited for; matrix products, arithmetic and copies ran while one was open for 0% of the time, Pallas kernels for 0%

profile of v5, /device:TPU:0, one launch (start us, length us, event | category | flops | bytes accessed | tf_op | source)
XLA Modules:
  0.0 328.5 jit_solution(16458633711271677468)
XLA Ops:
  0.6 316.0 %shard_map.135 = (bf16[128,1792]{1,0:T(8,128)(2,1)}, f32[128,1792]{1,0:T(8,128)}, bf16[4,112,768]{2,1,0:T(8,128)(2,1)}, bf16[4,112,256]{2,1,0:T(8,128)(2,1)}, bf...) custom-call(bf16[3,112,896]{2,1,0:T(8,128)(2,1)} %refs_6_.1, ...), custom_call_target="tpu_custom_call" | custom-call | tf_op jit(solution)/shard_map/pallas_call | solution.py:744
  316.6 6.2 %shard_map.136 = (f32[2,112,2432]{2,1,0:T(8,128)}, f32[112,2432]{1,0:T(8,128)}, f32[3,112,896]{2,1,0:T(8,128)}, f32[112,896]{1,0:T(8,128)}, bf16[128,1792]{1,0:T...) custom-call(bf16[2,112]{1,0:T(2,128)(2,1)} %refs_0_.3, bf16[4,112,640]{2,1,0:T(8,128)(2,1)} %get-tuple-element.21.refs_1_, ...), custom_call_target="tpu_custom_call" | custom-call | tf_op jit(solution)/shard_map/pallas_call | solution.py:843
  322.8 2.7 collective-permute-start
  325.5 1.8 collective-permute-done
  327.3 1.2 add.3
Async XLA Ops:
  322.8 4.5 %collective-permute-start = (f32[2,112]{1,0:T(2,128)}, f32[2,112]{1,0:T(2,128)S(1)}, u32[]{:S(2)}, u32[]{:S(2)}) collective-permute-start(f32[2,112]{1,0:T(2,128)} %get-tuple-element.34), channel_id=1, source_target_pairs={{0,1},{1,0},{2,3},{3,2},{4,5},{5,4},{6,7},{7,6},{8,9},{9,8},{10,11... | collective-permute-start | bytes 2696 | tf_op jit(solution)/shard_map/ppermute | solution.py:832

commit v6 on v5

--- a/solution.py
+++ b/solution.py
@@ -12,6 +12,7 @@
 WINDOW = 64
 EPSILON = 1e-06
 SUB = 4
+NARROW = 1
 BF = jnp.bfloat16
 F32 = jnp.float32
 NN = (((1,), (0,)), ((), ()))
@@ -40,14 +41,28 @@
 
 
 class Conditional:
-    def __init__(self, copy, sent, received):
-        self.copy, self.sent, self.received = copy, sent, received
+    def __init__(self, copy, sent, received, part=None, narrow=None):
+        self.copy, self.sent, self.received, self.part, self.narrow = copy, sent, received, part, narrow
+
+    def under(self, condition, k, name):
+        if self.part is None:
+            pl.when(condition)(getattr(self.copy, name))
+            return
+        thin = self.narrow[k]
+        wide = jnp.logical_not(thin)
+        if condition is not None:
+            thin, wide = jnp.logical_and(condition, thin), jnp.logical_and(condition, wide)
+        pl.when(thin)(getattr(self.part, name))
+        pl.when(wide)(getattr(self.copy, name))
+
+    def start(self):
+        self.under(self.sent, 0, "start")
 
     def wait_send(self):
-        pl.when(self.sent)(self.copy.wait_send)
+        self.under(self.sent, 0, "wait_send")
 
     def wait_recv(self):
-        pl.when(self.received)(self.copy.wait_recv)
+        self.under(self.received, 1, "wait_recv")
 
 
 class Kernel:
@@ -63,6 +78,8 @@
         self.is_middle = self.hi + self.z == 1
         self.is_end = self.hi + self.z != 1
         self.s = (self.f // 4) % 2 * 2 + core
+        self.col = self.column_of(self.s)
+        self.is_narrow = self.col == NARROW
         self.sib = self.s + 1 - 2 * core
         self.zn = (self.s + 2) % SUB
         self.diag = (self.sib + 2) % SUB
@@ -77,6 +94,11 @@
         middle = cfg["D"] // 256 * 128
         self.halves = (slice(0, middle), slice(middle, cfg["D"]))
 
+    def column_of(self, s):
+        if self.cfg["whole"]:
+            return s
+        return (s // 2 + self.hi) % 2 * 2 + s % 2
+
     def index(self, hi, s, x):
         return hi * 8 + s // 2 * 4 + x * 2 + s % 2
 
@@ -87,7 +109,8 @@
         return {"fsdp": self.index(self.next_hi, s, self.x), "tp": self.y}
 
     def peer(self, hi, x):
-        return {"fsdp": self.index(hi, self.s, x), "tp": self.y}
+        s = self.s if self.cfg["whole"] else jnp.where(hi == self.hi, self.s, self.zn)
+        return {"fsdp": self.index(hi, s, x), "tp": self.y}
 
     def barrier(self):
         sem = pltpu.get_barrier_semaphore()
@@ -102,25 +125,33 @@
             pl.semaphore_signal(sem, inc=1, device_id=partner, device_id_type=pl.DeviceIdType.MESH)
         return lambda: pl.semaphore_wait(sem, len(partners))
 
-    def remote(self, src, dst, device, sent=None, received=None):
+    def remote(self, src, dst, device, sent=None, received=None, narrow=None):
         k = self.count
         self.count += 1
-        copy = pltpu.make_async_remote_copy(
-            src_ref=src,
-            dst_ref=dst,
-            send_sem=self.send_sems.at[k],
-            recv_sem=self.recv_sems.at[k],
-            device_id=device,
-            device_id_type=pl.DeviceIdType.MESH,
-        )
-        if sent is None:
-            copy.start()
-        else:
-            pl.when(sent)(copy.start)
+
+        def describe(src, dst):
+            return pltpu.make_async_remote_copy(
+                src_ref=src,
+                dst_ref=dst,
+                send_sem=self.send_sems.at[k],
+                recv_sem=self.recv_sems.at[k],
+                device_id=device,
+                device_id_type=pl.DeviceIdType.MESH,
+            )
+
+        copy = describe(src, dst)
+        if narrow is not None:
+            part = slice(0, src.shape[1] - HP)
+            copy = Conditional(copy, sent, received, describe(src.at[:, part], dst.at[:, part]), narrow)
+        elif sent is not None:
             copy = Conditional(copy, sent, received)
+        copy.start()
         self.sends.append(copy)
         return copy
 
+    def narrow(self, key, sent, received):
+        return (sent, received) if key in ("ga", "up", "dn") and self.cfg["uneven"] else None
+
     def to_sib(self, src, dst):
         return self.remote(src, dst, self.mate(self.sib))
 
@@ -130,11 +161,11 @@
     def to_y(self, src, dst):
         return self.remote(src, dst, {"fsdp": self.f, "tp": self.yn})
 
-    def to_x(self, src, dst):
-        return self.remote(src, dst, self.peer(self.hi, 1 - self.x))
-
-    def to_half(self, src, dst):
-        return self.remote(src, dst, self.peer(self.next_hi, self.x))
+    def to_x(self, src, dst, narrow=None):
+        return self.remote(src, dst, self.peer(self.hi, 1 - self.x), narrow=narrow)
+
+    def to_half(self, src, dst, narrow=None):
+        return self.remote(src, dst, self.peer(self.next_hi, self.x), narrow=narrow)
 
     def local(self, src, dst):
         k = self.local_count
@@ -160,9 +191,15 @@
             self.prepare(key)
         shares = functools.partial(self.prepared, key)
         mine = self.share(full, self.s)
-        here = [self.remote(shares(s), mine, self.mate(s)) for s in (self.zn, self.diag, self.sib)]
+        here = []
+        for s in (self.zn, self.diag, self.sib):
+            col = self.column_of(s)
+            narrow = self.narrow(key, col == NARROW, self.is_narrow)
+            here.append(self.remote(shares(col), mine, self.mate(s), narrow=narrow))
         self.given += here
-        return {"full": full, "shares": shares, "own": self.local(shares(self.s), mine), "here": here}
+        same = self.narrow(key, self.is_narrow, self.is_narrow)
+        own = self.local(shares(self.col), mine)
+        return {"key": key, "full": full, "shares": shares, "own": own, "here": here, "narrow": same}
 
     def prepared(self, key, s):
         db = self.cfg["DB"]
@@ -175,7 +212,7 @@
         return jnp.sum(jnp.where(eye(db), line, 0.0), axis=1, keepdims=True)
 
     def prepare(self, key):
-        db, ff = self.cfg["DB"], self.cfg["FF"]
+        db = self.cfg["DB"]
         slots = getattr(self, "slots_" + key)
         if key in ("qkv", "ga", "up"):
             gain = self.gain_column(0 if key == "qkv" else 1)
@@ -186,10 +223,10 @@
             elif key == "out":
                 parts = [self.raw_out[:, n * DH : (n + 1) * DH].astype(F32) for n in (2 * s, 2 * s + 1)]
             elif key == "dn":
-                parts = [self.raw_dn[:, s * ff : (s + 1) * ff].astype(F32)]
+                parts = [self.raw_dn[:, self.cfg["spans"][s]].astype(F32)]
             else:
-                parts = [self.raw_gu[int(key == "up"), :, s * ff : (s + 1) * ff].astype(F32) * gain]
-            value = jnp.concatenate([padded(part, -(-part.shape[1] // HP) * HP) for part in parts], axis=1)
+                parts = [self.raw_gu[int(key == "up"), :, self.cfg["spans"][s]].astype(F32) * gain]
+            value = jnp.concatenate([padded(part, slots.shape[2] // len(parts)) for part in parts], axis=1)
             slots[s // 2, s % 2 * db : (s % 2 + 1) * db, :] = value.astype(BF)
 
     def columns_far(self, g):
@@ -197,10 +234,15 @@
             return
         mine = self.share(g["full"], self.s)
         g["far"], g["middle"] = [], []
-        for s in (self.s, self.sib):
-            g["far"].append(self.remote(g["shares"](s), mine, self.other(s)))
-        for s in (self.zn, self.diag):
-            g["middle"].append(self.remote(g["shares"](s), mine, self.other(s), self.is_middle, self.is_middle))
+        for s, col in ((self.zn, self.col), (self.diag, self.column_of(self.sib))):
+            narrow = self.narrow(g["key"], col == NARROW, self.is_narrow)
+            g["far"].append(self.remote(g["shares"](col), mine, self.other(s), narrow=narrow))
+        for s, col in ((self.s, self.column_of(self.zn)), (self.sib, self.column_of(self.diag))):
+            narrow = self.narrow(g["key"], col == NARROW, self.is_narrow)
+            device = self.other(s)
+            g["middle"].append(
+                self.remote(g["shares"](col), mine, device, self.is_middle, self.is_end, narrow=narrow)
+            )
         self.given += g["far"] + g["middle"]
 
     def spread(self, g):
@@ -210,14 +252,15 @@
         if self.cfg["whole"]:
             return
         part = g["full"].at[self.rows(self.hi, 1 - self.z, self.x), :]
-        g["passed"] = self.remote(part, part, self.other(self.s), self.is_middle, self.is_end)
+        device = self.other(self.zn)
+        g["passed"] = self.remote(part, part, device, self.is_middle, self.is_middle, narrow=g["narrow"])
         parts = [g["full"].at[self.rows(self.hi, z, self.x), :] for z in range(2)]
-        g["near"] = [self.to_x(part, part) for part in parts]
+        g["near"] = [self.to_x(part, part, g["narrow"]) for part in parts]
         self.gathered += [g["passed"]] + g["near"]
 
     def onward(self, g, z):
         part = g["full"].at[self.rows(self.next_hi, z, self.x), :]
-        copy = self.to_x(part, part)
+        copy = self.to_x(part, part, g["narrow"])
         g["near"].append(copy)
         self.gathered.append(copy)
 
@@ -226,27 +269,28 @@
             return
         for c in g["far"]:
             c.wait_recv()
-        self.onward(g, self.z)
+        self.onward(g, 1 - self.z)
 
     def spread_rest(self, g):
         if self.cfg["whole"]:
             return
         for c in g["middle"] + [g["passed"]]:
             c.wait_recv()
-        self.onward(g, 1 - self.z)
+        self.onward(g, self.z)
 
     def spread_done(self, g):
         if not self.cfg["whole"]:
             for c in g["near"]:
                 c.wait_recv()
 
-    def columns_back(self, full, result):
+    def columns_back(self, full, result, key=""):
         if self.cfg["whole"]:
             return self.local(full, result).wait
-        copies = [
-            self.remote(self.share(full, s), result.at[self.s], self.mate(s)) for s in (self.zn, self.diag, self.sib)
-        ]
-        own = self.local(self.share(full, self.s), result.at[self.s])
+        copies = []
+        for s in (self.zn, self.diag, self.sib):
+            narrow = self.narrow(key, self.is_narrow, self.column_of(s) == NARROW)
+            copies.append(self.remote(self.share(full, s), result.at[self.col], self.mate(s), narrow=narrow))
+        own = self.local(self.share(full, self.s), result.at[self.col])
 
         def wait():
             for c in copies:
@@ -265,14 +309,15 @@
                 total = total + part[i * tile : (i + 1) * tile, :].astype(F32)
             grad[place, :] = total.astype(BF)
 
-    def collect(self, grad, slots):
+    def collect(self, grad, slots, key=""):
         if self.cfg["whole"]:
             return None
         near = []
+        narrow = self.narrow(key, self.is_narrow, self.is_narrow)
         for k, hi in enumerate((self.next_hi, self.hi)):
             for z in range(2):
-                near.append(self.to_x(grad.at[self.rows(hi, z, 1 - self.x), :], slots.at[2 * k + z]))
-        return {"grad": grad, "slots": slots, "near": near, "far": []}
+                near.append(self.to_x(grad.at[self.rows(hi, z, 1 - self.x), :], slots.at[2 * k + z], narrow))
+        return {"grad": grad, "slots": slots, "near": near, "far": [], "narrow": narrow}
 
     def collect_on(self, g, planes=(0, 1)):
         if g is None:
@@ -281,7 +326,7 @@
             g["near"][z].wait_recv()
             rows = self.rows(self.next_hi, z, self.x)
             self.add_rows(g["grad"], rows, [g["slots"].at[z]])
-            g["far"].append(self.to_half(g["grad"].at[rows, :], g["slots"].at[4 + z]))
+            g["far"].append(self.to_half(g["grad"].at[rows, :], g["slots"].at[4 + z], g["narrow"]))
 
     def collect_done(self, g):
         if g is None:
@@ -503,6 +548,13 @@
         whole = lambda ref: [flat(ref[...])]
 
         everyone_here = self.barrier()
+        if cfg["uneven"]:
+
+            @pl.when(self.is_narrow)
+            def _():
+                for w in (self.w_ga, self.w_up, self.w_dn):
+                    w[:, w.shape[1] - HP :] = jnp.zeros((w.shape[0], HP), BF)
+
         line = 1 + self.s + self.s // 2
         own_starts = self.doc_starts[...].astype(F32)
         fill = jnp.zeros((self.starts.shape[1] - own_starts.shape[0], own_starts.shape[1]), F32)
@@ -580,19 +632,20 @@
         self.gather_finish(gather_two, near=True)
         self.feed_forward(1 - self.s // 2)
         self.grad_into(self.g_dn, self.g, lambda: whole(self.hidden))
-        sum_dn = self.collect(self.g_dn, self.slots_dn)
+        sum_dn = self.collect(self.g_dn, self.slots_dn, "dn")
         partial = lambda pair: dot(flat(self.d_ga[pair]), self.w_ga[...], NT) + dot(
             flat(self.d_up[pair]), self.w_up[...], NT
         )
         scatter = self.scatter_pair(stage, partial)
         self.scatter_send(scatter, partial)
+        self.collect_on(sum_dn, (0,))
         self.settle(self.gathered)
         self.grad_into(self.w_ga, self.u2, lambda: whole(self.d_ga))
-        sum_ga = self.collect(self.w_ga, self.slots_ga)
+        sum_ga = self.collect(self.w_ga, self.slots_ga, "ga")
         self.scatter_relay(scatter)
-        self.collect_on(sum_dn, (0,))
+        self.collect_on(sum_dn, (1,))
         self.grad_into(self.w_up, self.u2, lambda: whole(self.d_up))
-        sum_up = self.collect(self.w_up, self.slots_up)
+        sum_up = self.collect(self.w_up, self.slots_up, "up")
         d_unit = self.scatter_finish(scatter)
         resid = self.resid[...]
         scale = norm(resid)
@@ -602,8 +655,9 @@
         self.d_r[me] = self.in_grad[...].astype(BF)
         self.settle(gather_g["copies"] + gather_two["copies"] + rims)
         gather_d = self.gather_start(self.d_r)
-        self.collect_on(sum_dn, (1,))
+        self.collect_on(sum_ga, (0,))
         self.gather_relay(gather_d)
+        self.collect_on(sum_ga, (1,))
 
         view = {
             "sc": self.u2.at[0:2],
@@ -616,7 +670,6 @@
         partial = lambda pair: dot(flat(self.hidden[pair]), self.w_dn[...], NT)
         mlp = self.scatter_pair(view, partial)
         self.scatter_send(mlp, partial)
-        self.collect_on(sum_ga)
         self.gather_finish(gather_d)
 
         d_heads = self.d_heads = self.d_ga.at[:, :, :, slice(0, 2 * HP)]
@@ -628,7 +681,7 @@
 
         lax.fori_loop(0, SUB, heads_back, 0)
         self.collect_done(sum_dn)
-        backs = [self.columns_back(self.g_dn, self.o_dn)]
+        backs = [self.columns_back(self.g_dn, self.o_dn, "dn")]
 
         self.carry[...] = jnp.zeros_like(self.carry)
 
@@ -645,14 +698,15 @@
             lambda run: self.qkv.at[5 * run, :, slice(2 * HP, 6 * HP)], [self.rim.at[0], self.rim.at[1]]
         )
         self.scatter_relay(mlp)
+        self.collect_on(sum_up, (0,))
         lax.fori_loop(0, 2, second, 0)
         of_q, of_kv = slice(0, 2 * HP), slice(2 * HP, 6 * HP)
         g_q, g_kv = self.g_qkv.at[:, of_q], self.g_qkv.at[:, of_kv]
         self.grad_into(g_q, self.u1, lambda: [flat(self.qkv[1:5, :, of_q]), flat(self.qkv[6:10, :, of_q])])
         sum_q = self.collect(g_q, self.slots_qkv.at[:, :, of_q])
-        self.collect_on(sum_up)
+        self.collect_on(sum_up, (1,))
         self.collect_done(sum_ga)
-        backs.append(self.columns_back(self.w_ga, self.o_ga))
+        backs.append(self.columns_back(self.w_ga, self.o_ga, "ga"))
         for c in rim_back:
             c.wait_recv()
         for run in range(2):
@@ -663,29 +717,30 @@
         sum_kv = self.collect(g_kv, self.slots_qkv.at[:, :, of_kv])
         self.grad_into(self.w_out, self.d_r, lambda: whole(self.heads))
         sum_out = self.collect(self.w_out, self.slots_out)
+        self.collect_on(sum_q)
         partial = lambda pair: dot(flat(self.qkv[pl.ds(self.place(pair), 2)]), self.w_qkv[...], NT)
         scatter = self.scatter_pair(stage, partial)
         self.scatter_send(scatter, partial)
-        self.collect_on(sum_q)
+        self.collect_on(sum_kv, (0,))
         self.scatter_relay(scatter)
+        self.collect_on(sum_kv, (1,))
         self.collect_done(sum_up)
-        backs.append(self.columns_back(self.w_up, self.o_up))
-        self.collect_on(sum_kv)
+        backs.append(self.columns_back(self.w_up, self.o_up, "up"))
         self.out[...] = (self.resid[...] + self.scatter_finish(mlp)).astype(BF)
         back_to = lambda span: self.o_qkv.at[:, span] if cfg["whole"] else self.o_qkv.at[:, :, span]
         self.collect_done(sum_q)
         backs.append(self.columns_back(g_q, back_to(of_q)))
+        self.collect_on(sum_out)
+        self.collect_done(sum_kv)
+        backs.append(self.columns_back(g_kv, back_to(of_kv)))
+        self.collect_done(sum_out)
+        backs.append(self.columns_back(self.w_out, self.o_out))
         d_unit = self.scatter_finish(scatter)
         x = self.x_in[...].astype(F32)
         scale = norm(x)
         unit = x * scale
         inner = jnp.mean(d_unit * unit, axis=-1, keepdims=True)
         self.in_grad[...] += scale * (d_unit - unit * inner)
-        self.collect_on(sum_out)
-        self.collect_done(sum_kv)
-        backs.append(self.columns_back(g_kv, back_to(of_kv)))
-        self.collect_done(sum_out)
-        backs.append(self.columns_back(self.w_out, self.o_out))
         for wait in backs:
             wait()
         self.settle()
@@ -758,7 +813,7 @@
     )(*weights, starts, x, g)
 
 
-def assemble(ff, *refs):
+def assemble(spans, *refs):
     gains, sources, results, g_gain = refs[0], refs[1:10], refs[10:16], refs[16]
     held, made, sems = refs[17:26], refs[26:30], refs[30]
     copies = [pltpu.make_async_copy(a, b, sems.at[k]) for k, (a, b) in enumerate(zip(sources, held, strict=True))]
@@ -783,13 +838,13 @@
     copies[2].wait()
     for k, ref in enumerate((o_ga, o_up)):
         copies[k].wait()
-        value = jnp.concatenate([ref[s, :, :ff].astype(F32) for s in range(SUB)], axis=1)
+        value = jnp.concatenate([ref[s, :, : p.stop - p.start].astype(F32) for s, p in enumerate(spans)], axis=1)
         total = total + jnp.sum(value * w_gu[k].astype(F32), axis=1, keepdims=True)
         g_gu[k] = value * gain
     back[0].start()
     put(1, total)
     copies[3].wait()
-    g_dn[...] = jnp.concatenate([o_dn[s, :, :ff].astype(F32) for s in range(SUB)], axis=1)
+    g_dn[...] = jnp.concatenate([o_dn[s, :, : p.stop - p.start].astype(F32) for s, p in enumerate(spans)], axis=1)
     back[1].start()
     gain = column(0)
     total = jnp.zeros((db, 1), F32)
@@ -824,7 +879,10 @@
     ffp = -(-ff // HP) * HP
     heads = w_qkv.shape[2] // (SUB * DH)
     whole = size != 16 or db % 16 != 0
-    cfg = {"D": d, "NH": size // 8, "DB": db, "FF": ff, "whole": whole}
+    uneven = not whole and w_gate_up.shape[2] == SUB * ffp - HP
+    sizes = [ffp - HP * (uneven and s == NARROW) if uneven else ff for s in range(SUB)]
+    spans = [slice(sum(sizes[:s]), sum(sizes[: s + 1])) for s in range(SUB)]
+    cfg = {"D": d, "NH": size // 8, "DB": db, "spans": spans, "uneven": uneven, "whole": whole}
     width = {"qkv": 3 * heads * HP, "out": heads * HP, "ga": ffp, "up": ffp, "dn": ffp}
     acts = [doc_starts, tokens.reshape(batches * rows, d), cotangent.reshape(batches * rows, d)]
 
@@ -841,7 +899,7 @@
         shapes.append(jax.ShapeDtypeStruct(gains.shape, F32))
         anywhere, vmem = pl.BlockSpec(memory_space=pl.ANY), pl.BlockSpec(memory_space=pltpu.VMEM)
         g_gu, g_dn, g_qkv, g_out, out, in_grad, gain_sums = pl.pallas_call(
-            functools.partial(assemble, ff),
+            functools.partial(assemble, spans),
             out_shape=shapes,
             in_specs=[vmem] + [anywhere] * 9,
             out_specs=[anywhere] * 6 + [vmem],

time: 329 us -> 316 us (0.960)
  Pallas kernels: 322 us -> 310 us
    pallas_call x1, Pallas kernels: 316 us -> 304 us  [fused(): pl.pallas_call(kernel, out_shape=[jax.ShapeDtypeStruct(shape, kind) for _...]
where the time goes in v6:
time: 316 us
  Pallas kernels  310 us (98%)
    pallas_call x1, Pallas kernels, fused(): pl.pallas_call(kernel, out_shape=[jax.ShapeDtypeStruct(shape, kind) for _...  304 us
  transfers between devices with their start and end apart: 1, of which 1 were waited for; matrix products, arithmetic and copies ran while one was open for 0% of the time, Pallas kernels for 0%

profile of v6, /device:TPU:0, one launch (start us, length us, event | category | flops | bytes accessed | tf_op | source)
XLA Modules:
  0.0 316.0 jit_solution(2939228771816477944)
XLA Ops:
  0.6 304.3 %shard_map.135 = (bf16[128,1792]{1,0:T(8,128)(2,1)}, f32[128,1792]{1,0:T(8,128)}, bf16[4,112,768]{2,1,0:T(8,128)(2,1)}, bf16[4,112,256]{2,1,0:T(8,128)(2,1)}, bf...) custom-call(bf16[3,112,896]{2,1,0:T(8,128)(2,1)} %refs_6_.1, ...), custom_call_target="tpu_custom_call" | custom-call | tf_op jit(solution)/shard_map/pallas_call | solution.py:799
  304.9 6.0 %shard_map.136 = (f32[2,112,2432]{2,1,0:T(8,128)}, f32[112,2432]{1,0:T(8,128)}, f32[3,112,896]{2,1,0:T(8,128)}, f32[112,896]{1,0:T(8,128)}, bf16[128,1792]{1,0:T...) custom-call(bf16[2,112]{1,0:T(2,128)(2,1)} %refs_0_.3, bf16[4,112,640]{2,1,0:T(8,128)(2,1)} %get-tuple-element.21.refs_1_, ...), custom_call_target="tpu_custom_call" | custom-call | tf_op jit(solution)/shard_map/pallas_call | solution.py:901
  310.9 1.5 collective-permute-start
  312.4 2.4 collective-permute-done
  314.8 1.2 add.3
Async XLA Ops:
  310.9 3.8 %collective-permute-start = (f32[2,112]{1,0:T(2,128)}, f32[2,112]{1,0:T(2,128)S(1)}, u32[]{:S(2)}, u32[]{:S(2)}) collective-permute-start(f32[2,112]{1,0:T(2,128)} %get-tuple-element.34), channel_id=1, source_target_pairs={{0,1},{1,0},{2,3},{3,2},{4,5},{5,4},{6,7},{7,6},{8,9},{9,8},{10,11... | collective-permute-start | bytes 2696 | tf_op jit(solution)/shard_map/ppermute | solution.py:890

commit v7 on v6

--- a/solution.py
+++ b/solution.py
@@ -521,14 +521,28 @@
 
         lax.fori_loop(0, self.cfg["D"] // width, step, 0)
 
-    def feed_forward(self, plane):
-        ff = self.w_dn.shape[1]
-
+    def gate_and_up(self, plane):
         def step(k, _):
             i = 2 * plane + k
             rows = flat(self.u2[i])
-            gate = dot(rows, self.w_ga[...], NN)
-            upward = dot(rows, self.w_up[...], NN)
+            self.d_ga[i] = dot(rows, self.w_ga[...], NN).astype(BF).reshape(self.d_ga.shape[1:])
+            self.d_up[i] = dot(rows, self.w_up[...], NN).astype(BF).reshape(self.d_up.shape[1:])
+            return 0
+
+        lax.fori_loop(0, 2, step, 0)
+
+    def feed_forward(self, plane, ahead):
+        ff = self.w_dn.shape[1]
+
+        def step(k, _):
+            i = 2 * plane + k
+            if ahead:
+                gate = flat(self.d_ga[i]).astype(F32)
+                upward = flat(self.d_up[i]).astype(F32)
+            else:
+                rows = flat(self.u2[i])
+                gate = dot(rows, self.w_ga[...], NN)
+                upward = dot(rows, self.w_up[...], NN)
             d_hidden = dot(flat(self.g[i]), self.w_dn[...], NN)
             sig = jax.nn.sigmoid(gate)
             silu = gate * sig
@@ -624,13 +638,15 @@
         self.settle(self.given)
         self.spread_rest(dn)
         self.gather_relay(gather_two)
-        self.gather_finish(gather_g)
-        for g in (ga, up, dn):
+        for g in (ga, up):
             self.spread_done(g)
         self.gather_near(gather_two)
-        self.feed_forward(self.s // 2)
+        self.gate_and_up(self.s // 2)
+        self.gather_finish(gather_g)
+        self.spread_done(dn)
+        self.feed_forward(self.s // 2, True)
         self.gather_finish(gather_two, near=True)
-        self.feed_forward(1 - self.s // 2)
+        self.feed_forward(1 - self.s // 2, False)
         self.grad_into(self.g_dn, self.g, lambda: whole(self.hidden))
         sum_dn = self.collect(self.g_dn, self.slots_dn, "dn")
         partial = lambda pair: dot(flat(self.d_ga[pair]), self.w_ga[...], NT) + dot(
@@ -642,8 +658,8 @@
         self.settle(self.gathered)
         self.grad_into(self.w_ga, self.u2, lambda: whole(self.d_ga))
         sum_ga = self.collect(self.w_ga, self.slots_ga, "ga")
+        self.collect_on(sum_dn, (1,))
         self.scatter_relay(scatter)
-        self.collect_on(sum_dn, (1,))
         self.grad_into(self.w_up, self.u2, lambda: whole(self.d_up))
         sum_up = self.collect(self.w_up, self.slots_up, "up")
         d_unit = self.scatter_finish(scatter)

time: 316 us -> 312 us (0.987)
  Pallas kernels: 310 us -> 306 us
    pallas_call x1, Pallas kernels: 304 us -> 300 us  [fused(): pl.pallas_call(kernel, out_shape=[jax.ShapeDtypeStruct(shape, kind) for _...]
where the time goes in v7:
time: 312 us
  Pallas kernels  306 us (98%)
    pallas_call x1, Pallas kernels, fused(): pl.pallas_call(kernel, out_shape=[jax.ShapeDtypeStruct(shape, kind) for _...  300 us
  transfers between devices with their start and end apart: 1, of which 1 were waited for; matrix products, arithmetic and copies ran while one was open for 0% of the time, Pallas kernels for 0%

profile of v7, /device:TPU:0, one launch (start us, length us, event | category | flops | bytes accessed | tf_op | source)
XLA Modules:
  0.0 312.0 jit_solution(9057188013145219760)
XLA Ops:
  0.6 300.2 %shard_map.135 = (bf16[128,1792]{1,0:T(8,128)(2,1)}, f32[128,1792]{1,0:T(8,128)}, bf16[4,112,768]{2,1,0:T(8,128)(2,1)}, bf16[4,112,256]{2,1,0:T(8,128)(2,1)}, bf...) custom-call(bf16[3,112,896]{2,1,0:T(8,128)(2,1)} %refs_6_.1, ...), custom_call_target="tpu_custom_call" | custom-call | tf_op jit(solution)/shard_map/pallas_call | solution.py:815
  300.8 6.0 %shard_map.136 = (f32[2,112,2432]{2,1,0:T(8,128)}, f32[112,2432]{1,0:T(8,128)}, f32[3,112,896]{2,1,0:T(8,128)}, f32[112,896]{1,0:T(8,128)}, bf16[128,1792]{1,0:T...) custom-call(bf16[2,112]{1,0:T(2,128)(2,1)} %refs_0_.3, bf16[4,112,640]{2,1,0:T(8,128)(2,1)} %get-tuple-element.21.refs_1_, ...), custom_call_target="tpu_custom_call" | custom-call | tf_op jit(solution)/shard_map/pallas_call | solution.py:917
  306.9 1.7 collective-permute-start
  308.6 2.2 collective-permute-done
  310.7 1.2 add.3
Async XLA Ops:
  306.9 3.8 %collective-permute-start = (f32[2,112]{1,0:T(2,128)}, f32[2,112]{1,0:T(2,128)S(1)}, u32[]{:S(2)}, u32[]{:S(2)}) collective-permute-start(f32[2,112]{1,0:T(2,128)} %get-tuple-element.34), channel_id=1, source_target_pairs={{0,1},{1,0},{2,3},{3,2},{4,5},{5,4},{6,7},{7,6},{8,9},{9,8},{10,11... | collective-permute-start | bytes 2696 | tf_op jit(solution)/shard_map/ppermute | solution.py:906

commit v8 on v7

--- a/solution.py
+++ b/solution.py
@@ -381,6 +381,7 @@
 
     def scatter_pair(self, st, partial):
         sc, rc = st["sc"], st["rc"]
+        self.settle(st.get("left", []))
         copies = []
         for k, pair in enumerate((self.diag, self.sib)):
             sc[k] = partial(pair).astype(BF).reshape(sc.shape[1:])
@@ -413,7 +414,7 @@
         for c in g["z"] + [g["y"]]:
             c.wait_recv()
         total = st["so"][1, self.y].astype(F32) + st["rz"][...].astype(F32) + st["ry"][...].astype(F32)
-        self.settle(g["pair"] + g["d"] + g["z"] + [g["y"]])
+        st["left"] = g["pair"] + g["d"] + g["z"] + [g["y"]]
         return total
 
 

time: 312 us -> 312 us (level)
  no operation moved by 1% of the time
where the time goes in v8:
time: 312 us
  Pallas kernels  306 us (98%)
    pallas_call x1, Pallas kernels, fused(): pl.pallas_call(kernel, out_shape=[jax.ShapeDtypeStruct(shape, kind) for _...  300 us
  transfers between devices with their start and end apart: 1, of which 1 were waited for; matrix products, arithmetic and copies ran while one was open for 0% of the time, Pallas kernels for 0%

profile of v8, /device:TPU:0, one launch (start us, length us, event | category | flops | bytes accessed | tf_op | source)
XLA Modules:
  0.0 311.9 jit_solution(18369158560540972509)
XLA Ops:
  0.6 300.2 %shard_map.135 = (bf16[128,1792]{1,0:T(8,128)(2,1)}, f32[128,1792]{1,0:T(8,128)}, bf16[4,112,768]{2,1,0:T(8,128)(2,1)}, bf16[4,112,256]{2,1,0:T(8,128)(2,1)}, bf...) custom-call(bf16[3,112,896]{2,1,0:T(8,128)(2,1)} %refs_6_.1, ...), custom_call_target="tpu_custom_call" | custom-call | tf_op jit(solution)/shard_map/pallas_call | solution.py:816
  300.8 6.0 %shard_map.136 = (f32[2,112,2432]{2,1,0:T(8,128)}, f32[112,2432]{1,0:T(8,128)}, f32[3,112,896]{2,1,0:T(8,128)}, f32[112,896]{1,0:T(8,128)}, bf16[128,1792]{1,0:T...) custom-call(bf16[2,112]{1,0:T(2,128)(2,1)} %refs_0_.3, bf16[4,112,640]{2,1,0:T(8,128)(2,1)} %get-tuple-element.21.refs_1_, ...), custom_call_target="tpu_custom_call" | custom-call | tf_op jit(solution)/shard_map/pallas_call | solution.py:918
  306.8 1.7 collective-permute-start
  308.5 2.1 collective-permute-done
  310.7 1.2 add.3
Async XLA Ops:
  306.8 3.8 %collective-permute-start = (f32[2,112]{1,0:T(2,128)}, f32[2,112]{1,0:T(2,128)S(1)}, u32[]{:S(2)}, u32[]{:S(2)}) collective-permute-start(f32[2,112]{1,0:T(2,128)} %get-tuple-element.34), channel_id=1, source_target_pairs={{0,1},{1,0},{2,3},{3,2},{4,5},{5,4},{6,7},{7,6},{8,9},{9,8},{10,11... | collective-permute-start | bytes 2696 | tf_op jit(solution)/shard_map/ppermute | solution.py:907
